TPU v7x, 32 devices: a whole 2x2x4 slice. The times are simulated.
32 devices in a mesh: date: 8 (over y, x, core), lat: 4 (over z).
Axes of the slice: x: 2, y: 2, z: 4, core: 2. Of those that a mesh axis runs over, the one named last changes fastest.
Arguments:
- inputs: bfloat16 [8, 2, 8, 720, 641], P('date', None, 'lat'), may hold values from -6 to 6
- noise: bfloat16 [8, 2, 8, 720, 8], P('date', None, 'lat'), may hold values from -6 to 6
- cotangent: bfloat16 [8, 2, 8, 720, 641], P('date', None, 'lat'), may hold values from -6 to 6
- params: bfloat16 [3313664], P(('date', 'lat')), as said below
- psi: float32 [8, 12], replicated, may hold values from 0.2 to 1
- step_counts: int32 [8], P('date'), may hold values from 1 to 2, as said below
- pixel_mask: int32 [8, 720], P('lat'), may hold values 0 or 1
- support_offsets: int32 [12, 2], replicated, may hold values from -2 to 2, as said below
- support_basis: int32 [12], replicated, may hold values from 0 to 3, as said below
Outputs:
- output: bfloat16 [8, 2, 8, 720, 641], P('date', None, 'lat')
- input_grad: bfloat16 [8, 2, 8, 720, 641], P('date', None, 'lat')
- param_grad: float32 [3313664], P(('date', 'lat'))
Inputs may be any that keep to these rules, and one draw needn't show every extreme that they name: `support_offsets`: each row is a distinct latitude and longitude offset of the window of 3 latitudes and 5 longitudes; latitude offsets -1 and +1 both occur. `support_basis`: each basis function names 3 support points. `step_counts`: some sample has 2 given steps. `params`: the unused entries are zero.
All inputs are finite; a program needn't handle non-finite values. No bound on the sum of `pixel_mask` on one device may be relied on, other than what follows from the above.
Results may differ from a plain program's by a relative error of at most 0.0059.
Values may be sent and summed in bfloat16 or wider, within the bound.
A program may use at most 320 MiB of HBM per device.

v0:
```python
import math

import jax
import jax.numpy as jnp
from jax import lax
from jax.sharding import PartitionSpec as P

C = 641
HID = 1282
BASIS = 4
SUPPORT = 12
REACH = 2
CIN = 649


def extended_2(cells, sides, width):
    for axis, dim in sides:
        count = lax.axis_size(axis)
        ends = count - 1
        head = lax.slice_in_dim(cells, 0, width, axis=dim)
        tail = lax.slice_in_dim(cells, cells.shape[dim] - width, cells.shape[dim], axis=dim)
        cells = jnp.concatenate(
            [
                lax.ppermute(tail, axis, [(i, (i + 1) % count) for i in range(ends)]),
                cells,
                lax.ppermute(head, axis, [((i + 1) % count, i) for i in range(ends)]),
            ],
            axis=dim,
        )
    return cells


def unpack(flat_params):
    layout = [(BASIS * CIN, C), (C,), (CIN,), (CIN,), (C,), (C,), (C, HID), (HID,), (HID, C), (C,)]
    pieces = []
    offset = 0
    for extent in layout:
        amount = math.prod(extent)
        pieces.append(flat_params[offset : offset + amount].reshape(extent))
        offset = offset + amount
    return pieces


def layer_norm(values, norm_gain, norm_shift):
    average = jnp.mean(values, axis=-1, keepdims=True)
    centered = values - average
    variance = jnp.mean(centered * centered, axis=-1, keepdims=True)
    return centered * lax.rsqrt(variance + 1e-05) * norm_gain + norm_shift


def wrap_columns(values):
    return jnp.concatenate([values[:, :, :, -REACH:], values, values[:, :, :, :REACH]], axis=3)


def contract_rows(left, right):
    return lax.dot_general(
        left, right, (((0,), (0,)), ((), ())), preferred_element_type=jnp.float32
    )


def contract_cols(left, right):
    return lax.dot_general(
        left, right, (((1,), (1,)), ((), ())), preferred_element_type=jnp.float32
    )


def forward_pass(inputs, noise, params, psi_rows, support_offsets, onehot):
    samples_dev, steps_dev, rows_dev, columns, channels = inputs.shape
    gathered = lax.all_gather(params, ("date", "lat"), axis=0, tiled=True)
    weights = unpack(gathered)
    (
        disco_weight,
        conv_bias,
        first_gain,
        first_shift,
        second_gain,
        second_shift,
        up_weight,
        up_bias,
        down_weight,
        down_bias,
    ) = weights
    stacked = jnp.concatenate([inputs.astype(jnp.float32), noise.astype(jnp.float32)], axis=-1)
    normed = layer_norm(stacked, first_gain.astype(jnp.float32), first_shift.astype(jnp.float32))
    extended = extended_2(normed.astype(jnp.bfloat16), (("lat", 2),), 1)
    extended = wrap_columns(extended)
    zero_index = jnp.zeros((), jnp.int32)
    terms = jnp.zeros((samples_dev, steps_dev, rows_dev, columns, BASIS, CIN), jnp.float32)
    for point in range(SUPPORT):
        lat_start = 1 + support_offsets[point, 0]
        lon_start = REACH + support_offsets[point, 1]
        window_part = lax.dynamic_slice(
            extended,
            (zero_index, zero_index, lat_start, lon_start, zero_index),
            (samples_dev, steps_dev, rows_dev, columns, CIN),
        )
        weighting = psi_rows[:, point][:, None] * onehot[point][None, :]
        terms = terms + weighting[None, None, :, None, :, None] * window_part[:, :, :, :, None, :]
    basis_low = terms.reshape(-1, BASIS * CIN).astype(jnp.bfloat16)
    conv = jnp.dot(basis_low, disco_weight, preferred_element_type=jnp.float32) + conv_bias.astype(
        jnp.float32
    )
    residual = inputs.astype(jnp.float32).reshape(-1, C) + conv
    second_low = layer_norm(
        residual, second_gain.astype(jnp.float32), second_shift.astype(jnp.float32)
    ).astype(jnp.bfloat16)
    pre_act = jnp.dot(second_low, up_weight, preferred_element_type=jnp.float32) + up_bias.astype(
        jnp.float32
    )
    activated = jax.nn.gelu(pre_act).astype(jnp.bfloat16)
    output_rows = (
        residual
        + jnp.dot(activated, down_weight, preferred_element_type=jnp.float32)
        + down_bias.astype(jnp.float32)
    )
    return (weights, stacked, basis_low, residual, second_low, pre_act, activated, output_rows)


def local(
    inputs, noise, cotangent, params, psi, step_counts, pixel_mask, support_offsets, support_basis
):
    samples_dev, steps_dev, rows_dev, columns, channels = inputs.shape
    first_row = lax.axis_index("lat") * rows_dev
    psi_padded = jnp.pad(psi, ((1, 1), (0, 0)))
    psi_ext = lax.dynamic_slice_in_dim(psi_padded, first_row, rows_dev + 2, 0)
    psi_rows = psi_ext[1:-1]
    onehot = (support_basis[:, None] == jnp.arange(BASIS, dtype=jnp.int32)[None, :]).astype(
        jnp.float32
    )
    saved = forward_pass(inputs, noise, params, psi_rows, support_offsets, onehot)
    output_rows = saved[7]
    saved = forward_pass(inputs, noise, params, psi_rows, support_offsets, onehot)
    weights, stacked, basis_low, residual, second_low, pre_act, activated = saved[:7]
    (
        disco_weight,
        conv_bias,
        first_gain,
        first_shift,
        second_gain,
        second_shift,
        up_weight,
        up_bias,
        down_weight,
        down_bias,
    ) = weights
    active = (jnp.arange(steps_dev, dtype=jnp.int32)[None, :] < step_counts[:, None]).astype(
        jnp.float32
    )
    valid = pixel_mask.astype(jnp.float32)
    seed_grad = (
        cotangent.astype(jnp.float32)
        * active[:, :, None, None, None]
        * valid[None, None, :, :, None]
    )
    seed_grad = seed_grad.reshape(-1, C)
    grad_branch = seed_grad.astype(jnp.bfloat16)
    grad_down_bias = jnp.sum(grad_branch.astype(jnp.float32), axis=0)
    grad_down = contract_rows(activated, grad_branch)
    grad_act = contract_cols(grad_branch, down_weight)
    gelu_value, gelu_back = jax.vjp(jax.nn.gelu, pre_act)
    grad_pre = gelu_back(grad_act)[0].astype(jnp.bfloat16)
    grad_up_bias = jnp.sum(grad_pre.astype(jnp.float32), axis=0)
    grad_up = contract_rows(second_low, grad_pre)
    grad_second = contract_cols(grad_pre, up_weight)
    norm_value, second_back = jax.vjp(
        layer_norm, residual, second_gain.astype(jnp.float32), second_shift.astype(jnp.float32)
    )
    grad_res_part, grad_second_gain, grad_second_shift = second_back(grad_second)
    grad_residual = seed_grad + grad_res_part
    grad_conv = grad_residual.astype(jnp.bfloat16)
    grad_conv_bias = jnp.sum(grad_conv.astype(jnp.float32), axis=0)
    grad_disco = contract_rows(basis_low, grad_conv)
    grad_basis = contract_cols(grad_conv, disco_weight).astype(jnp.bfloat16)
    grad_basis = grad_basis.reshape(samples_dev, steps_dev, rows_dev, columns, BASIS, CIN)
    grad_ext = extended_2(grad_basis, (("lat", 2),), 1)
    grad_ext = wrap_columns(grad_ext)
    zero_index = jnp.zeros((), jnp.int32)
    grad_normed = jnp.zeros((samples_dev, steps_dev, rows_dev, columns, CIN), jnp.float32)
    for point in range(SUPPORT):
        lat_start = 1 - support_offsets[point, 0]
        lon_start = REACH - support_offsets[point, 1]
        block_part = lax.dynamic_slice(
            grad_ext,
            (zero_index, zero_index, lat_start, lon_start, support_basis[point], zero_index),
            (samples_dev, steps_dev, rows_dev, columns, 1, CIN),
        )
        weighting = lax.dynamic_slice_in_dim(psi_ext[:, point], lat_start, rows_dev, 0)
        grad_normed = (
            grad_normed + weighting[None, None, :, None, None] * block_part[:, :, :, :, 0, :]
        )
    first_value, first_back = jax.vjp(
        layer_norm, stacked, first_gain.astype(jnp.float32), first_shift.astype(jnp.float32)
    )
    grad_stacked, grad_first_gain, grad_first_shift = first_back(grad_normed)
    input_rows = grad_stacked[..., :C] + grad_residual.reshape(
        samples_dev, steps_dev, rows_dev, columns, C
    )
    input_grad = input_rows.astype(jnp.bfloat16)
    flat_grad = jnp.concatenate(
        [
            grad_disco.reshape(-1),
            grad_conv_bias,
            grad_first_gain,
            grad_first_shift,
            grad_second_gain,
            grad_second_shift,
            grad_up.reshape(-1),
            grad_up_bias,
            grad_down.reshape(-1),
            grad_down_bias,
        ]
    )
    full_length = params.shape[0] * lax.axis_size(("date", "lat"))
    flat_grad = jnp.pad(flat_grad, (0, full_length - flat_grad.shape[0]))
    param_grad = lax.psum_scatter(flat_grad, ("date", "lat"), scatter_dimension=0, tiled=True)
    output = output_rows.reshape(samples_dev, steps_dev, rows_dev, columns, C).astype(jnp.bfloat16)
    return (output, input_grad, param_grad)


def solution(mesh):
    placed = (
        P("date", None, "lat", None, None),
        P("date", None, "lat", None, None),
        P("date", None, "lat", None, None),
        P(("date", "lat")),
        P(),
        P("date"),
        P("lat", None),
        P(),
        P(),
    )
    return jax.shard_map(
        local,
        mesh=mesh,
        in_specs=placed,
        out_specs=(
            P("date", None, "lat", None, None),
            P("date", None, "lat", None, None),
            P(("date", "lat")),
        ),
        check_vma=False,
    )
```

profile of v0, /device:TPU:4, one launch (start us, length us, event | category | flops | bytes accessed | tf_op | source)
XLA Modules:
  0.0 1990.7 jit_solution(12400274356718154673)
XLA Ops:
  88.2 8.3 copy_convert_fusion
  96.5 12.9 copy.56
  109.4 11.6 reshape.1716
  121.7 24.1 %convert_reduce_fusion.1 = (f32[641]{0:T(1024)}, bf16[1,2,2,720,641]{3,2,4,1,0:T(2,128)(2,1)S(1)}, f32[1,2,2,720,641]{3,2,4,1,0:T(2,128)}) fusion(f32[2,720]{1,0:T(2,128)S(1)} %convert_element_type.688, f32[2]{0:T(128)S(1)} %compare_convert_fusion, bf16[1,2,2,720,641]{3,2,4,1,0:T(2,128)(2,1)} %param.11), kind=kLoop, calls=%fused_computation.56 | loop fusion | flops 11075839 | bytes 14776972 | tf_op jit(solution)/shard_map/reduce_sum | solution.py:157
  150.4 10.4 convert_element_type.690
  160.8 7.9 copy.70
  168.6 12.0 reshape.1720
  199.7 20.0 %multiply_reduce_fusion.2 = f32[2,2,720]{2,0,1:T(2,128)S(1)} fusion(f32[2,2,720]{2,0,1:T(2,128)S(1)} %add_multiply_fusion, f32[1,2,2,720,8]{3,1,4,2,0:T(2,128)S(1)} %copy_convert_fusion.1, f32[1,2,2,720,641]{3,1,4,2,0:T(2,128)} %copy_convert_fusion), kind=kLoop, calls=%fused_computation.52 | loop fusion | flops 7473600 | bytes 7499520 | tf_op jit(solution)/shard_map/reduce_sum | solution.py:47
  220.4 122.3 %reduce.11 = bf16[32,103552]{1,0:T(8,128)(2,1)} reduce(bf16[32,1,103552]{2,1,0:T(2,128)(2,1)} %all-gather.3.cloned.1.call-done, bf16[]{:T(256)} %constant.220), dimensions={1}, to_apply=%all-gather.reduce_sub_computation | reduce | bytes 13254658 | tf_op jit(solution)/shard_map/all_gather | solution.py:69
  342.6 12.6 reshape.1759
  356.1 13.2 add_convert_fusion.1
  385.3 11.7 reshape.1717
  396.9 6.1 reshape.1718
  403.1 6.5 reshape.1719
  412.4 9.4 collective-permute-done
  427.2 41.2 %fusion.7 = bf16[1,2,4,724,649]{3,1,4,2,0:T(2,128)(2,1)S(1)} fusion(bf16[1,2,1,720,649]{3,1,4,2,0:T(2,128)(2,1)} %collective-permute-done.1, bf16[1,2,2,720,649]{3,1,4,2,0:T(2,128)(2,1)} %copy-done.1, bf16[1,2,1,720,649]{3,1,4,2,0:T(2,128)(2,1)} %collective-permute-done), kind=kLoop, calls=%fused_computation.18 | loop fusion | flops 67662144 | bytes 14994496 | tf_op jit(solution)/shard_map/concatenate | solution.py:52
  468.4 69.1 %bitcast_convert_fusion.11 = (f32[2,2,720,649]{2,0,3,1:T(2,128)}, f32[2,2,720,649]{2,0,3,1:T(2,128)}, f32[2,2,720,649]{2,0,3,1:T(2,128)}, f32[2,2,720,649]{2,0,3...) fusion(bf16[1,2,4,724,649]{3,1,4,2,0:T(2,128)(2,1)S(1)} %fusion, ...), kind=kLoop, calls=%fused_computation.77 | loop fusion | flops 16822080 | bytes 100932552 | tf_op jit(solution)/shard_map/convert_element_type | solution.py:98
  537.5 12.0 copy.58
  549.5 14.3 copy.62
  563.8 14.4 copy.63
  578.2 12.9 copy.64
  591.2 14.2 copy.65
  605.4 14.2 copy.66
  619.7 13.0 copy.67
  632.7 14.2 copy.68
  646.9 14.2 copy.69
  661.2 23.4 %bitcast_convert_fusion.10 = (f32[2,2,720,649]{2,0,3,1:T(2,128)}, f32[2,2,720,649]{2,0,3,1:T(2,128)S(1)}, f32[2,2,720,649]{2,0,3,1:T(2,128)S(1)}) fusion(bf16[1,2,4,724,649]{3,1,4,2,0:T(2,128)(2,1)S(1)} %fusion.7, s32[]{:T(128)S(6)} %select_n.222, s32[]{:T(128)S(6)} %select_n.223, s32[]{:T(128)S(6)} %select_n.226, s32[]{:T(128)S(6)} %select_n.227, ...), kind=kLoop, calls=%fused_computation.76 | loop fusion | flops 5607360 | bytes 33644184 | tf_op jit(solution)/shard_map/convert_element_type | solution.py:98
  684.6 12.8 copy.59
  697.4 14.2 copy.60
  711.6 14.1 copy.61
  725.7 113.0 %add_convert_fusion = bf16[2,2,720,4,649]{2,1,0,4,3:T(2,128)(2,1)} fusion(f32[2,2,720,649]{2,1,0,3:T(2,128)} %copy.69, f32[2,4]{0,1:T(4,128)S(1)} %get-tuple-element.132, f32[2,2,720,649]{2,1,0,3:T(2,128)} %copy.68, f32[2,4]{0,1:T(4,128)S(1)} %get-tuple-element.133, f32[2,2,720,649]{2,1,0,3:T(2,128)} %copy.67, f32[2,4]{0,1:T(4,128)S(1)} %get-tuple-element.134, ...), kind=kLoop, calls=%fused_computation.1 | loop fusion | flops 179435520 | bytes 104671104 | tf_op jit(solution)/shard_map/convert_element_type | solution.py:99
  838.7 37.1 %convert_element_type.676 = bf16[2880,2596]{0,1:T(8,128)(2,1)} reshape(bf16[2,2,720,4,649]{2,1,0,4,3:T(2,128)(2,1)} %add_convert_fusion) | data formatting | bytes 29905920 | tf_op jit(solution)/shard_map/convert_element_type | solution.py:99
  875.8 18.6 fusion.58
  895.4 15.4 multiply_convert_fusion
  910.8 20.1 %convert_reduce_fusion = (f32[1282]{0:T(1024)}, bf16[2880,1282]{0,1:T(8,128)(2,1)S(1)}) fusion(f32[2880,1282]{0,1:T(8,128)} %get-tuple-element.128, f32[1282]{0:T(1024)S(1)} %copy-done.24, bf16[2880,641]{0,1:T(8,128)(2,1)S(1)} %copy-done.3, bf16[1282,641]{1,0:T(8,128)(2,1)S(1)} %copy-done.6), kind=kOutput, calls=%fused_computation.13 | convolution fusion | flops 4818264576 | bytes 27498900 | tf_op jit(solution)/shard_map/dot_general | solution.py:62
  934.0 10.7 fusion.47
  944.7 6.2 multiply_reduce_fusion.3
  950.9 8.3 convert_reduce_fusion.2
  959.2 19.7 convolution_convert_fusion
  978.9 13.3 reshape.1722
  992.2 50.2 %reshape.1721 = bf16[1,2,2,720,4,649]{3,2,1,5,4,0:T(2,128)(2,1)} reshape(bf16[2880,2596]{0,1:T(8,128)(2,1)} %convolution_convert_fusion) | data formatting | bytes 29905920 | tf_op jit(solution)/shard_map/reshape | solution.py:174
  1042.5 32.1 %fusion.51 = (bf16[1,2,1,720,4,649]{3,2,1,5,4,0:T(2,128)(2,1)}, bf16[1,2,1,720,4,649]{3,2,1,5,4,0:T(2,128)(2,1)}) fusion(bf16[1,2,2,720,4,649]{3,2,1,5,4,0:T(2,128)(2,1)} %reshape.1721), kind=kLoop, calls=%fused_computation.174 | loop fusion | bytes 29905920 | tf_op jit(solution)/shard_map/slice | solution.py:20
  1074.5 13.6 copy.84
  1093.4 10.5 fusion.45
  1109.2 19.3 fusion.41
  1128.5 8.9 reshape.1723
  1137.4 13.3 copy.85
  1152.0 9.9 fusion.22
  1166.5 93.8 %collective-permute-done.2 = bf16[1,2,1,720,4,649]{3,4,5,2,1,0:T(4,128)(2,1)} collective-permute-done((bf16[1,2,1,720,4,649]{3,4,5,2,1,0:T(4,128)(2,1)}, bf16[1,2,1,720,4,649]{3,4,5,2,1,0:T(4,128)(2,1)}, u32[]{:S(2)}, u32[]{:S(2)}) %collective-permute-start.2) | collective-permute-done | bytes 7476512 | tf_op jit(solution)/shard_map/ppermute | solution.py:24
  1260.3 12.8 copy_dynamic-update-slice_fusion.2
  1273.1 24.1 %copy_dynamic-update-slice_fusion = bf16[1,2,4,720,4,649]{3,1,5,2,4,0:T(2,128)(2,1)} fusion(bf16[1,2,4,720,4,649]{3,1,5,2,4,0:T(2,128)(2,1)} %copy_dynamic-update-slice_fusion.2, bf16[1,2,2,720,4,649]{3,2,1,5,4,0:T(2,128)(2,1)} %reshape.1721), kind=kLoop, calls=%fused_computation.5 | loop fusion | bytes 31899648
  1297.2 27.6 %collective-permute-done.3 = bf16[1,2,1,720,4,649]{3,4,5,2,1,0:T(4,128)(2,1)} collective-permute-done((bf16[1,2,1,720,4,649]{3,4,5,2,1,0:T(4,128)(2,1)}, bf16[1,2,1,720,4,649]{3,4,5,2,1,0:T(4,128)(2,1)}, u32[]{:S(2)}, u32[]{:S(2)}) %collective-permute-start.3) | collective-permute-done | bytes 7476512 | tf_op jit(solution)/shard_map/ppermute | solution.py:26
  1324.8 12.8 copy_dynamic-update-slice_fusion.1
  1337.6 11.2 fusion.50
  1349.0 93.7 %pad_maximum_fusion = bf16[1,2,4,724,4,649]{3,1,5,2,4,0:T(2,128)(2,1)} fusion(bf16[1,2,4,2,4,649]{3,1,5,2,4,0:T(2,128)(2,1)S(1)} %get-tuple-element.40, bf16[1,2,4,720,4,649]{3,1,5,2,4,0:T(2,128)(2,1)} %copy_dynamic-update-slice_fusion.1, bf16[1,2,4,2,4,649]{3,1,5,2,4,0:T(2,128)(2,1)S(1)} %get-tuple-element.39), kind=kLoop, calls=%fused_computation | loop fusion | flops 90216192 | bytes 60144128 | tf_op jit(solution)/shard_map/concatenate | solution.py:52
  1443.0 187.9 %multiply_reduce_fusion = (f32[649]{0:T(1024)S(1)}, f32[2,2,720]{2,0,1:T(2,128)S(1)}, f32[649]{0:T(1024)S(1)}, f32[1,2,2,720,649]{3,1,4,2,0:T(2,128)}) fusion(f32[2,2,720]{2,0,1:T(2,128)S(1)} %copy-done.13, f32[2,2,720]{2,0,1:T(2,128)S(1)} %copy-done.10, f32[1,2,2,720,8]{3,1,4,2,0:T(2,128)S(1)} %copy-done.5, f32[1,2,2,720,641]{3,1,4,2,0:T(2,128)S(1)} %bitcast.246, ...), kind=kLoop, calls=%fused_computation.49 | loop fusion | flops 82237104 | bytes 59854428 | tf_op jit(solution)/shard_map/transpose(jvp())/reduce_sum | solution.py:48
  1630.9 104.6 %concatenate.54 = f32[3312704]{0:T(1024)} concatenate(f32[1664036]{0:T(1024)} %reshape.1723, f32[641]{0:T(1024)S(1)} %copy-done.22, f32[649]{0:T(1024)S(1)} %get-tuple-element.12, f32[649]{0:T(1024)S(1)} %get-tuple-element.16, f32[641]{0:T(1024)S(1)} %copy-done.21, f32[641]{0:T(1024)S(1)} %copy-done.26, f32[821762]{0:T(1024)} %reshape.1724, f32[1282]{0:T(1024)S(1)} %copy-done.23, ...), dimensions={0} | concatenate | bytes 26501632 | tf_op jit(solution)/shard_map/concatenate | solution.py:199
  1735.5 9.9 pad.9
  1747.0 13.9 add_convert_fusion.2
  1760.9 13.7 convert_element_type.685
  1774.6 6.9 copy.80
  1781.6 19.4 fusion.48
  1801.0 13.4 fusion.21
  1819.4 162.2 %all-reduce.5.cloned.1.call-done = f32[3313664]{0:T(1024)} async-done(((f32[3313664]{0:T(1024)}), f32[3313664]{0:T(1024)}) %all-reduce.5.cloned.1.call-update) | async-done | bytes 13254672
  (197 shorter events, 77.7 us)
Async XLA Ops:
  7.2 213.2 %all-gather.3.cloned.1.call-start = ((), (), s32[]{:S(2)}) async-start(), calls=%async_computation | async-start | bytes 13668864 | tf_op jit(solution)/shard_map/all_gather | solution.py:69
  9.1 1972.4 %all-reduce.5.cloned.1.call-start = ((), (), s32[]{:S(2)}) async-start(), calls=%async_computation.1 | async-start | bytes 26509312
  109.4 11.6 copy-start.25
  168.6 20.0 %copy-start.27 = (f32[8,12]{1,0:T(8,128)S(1)}, f32[8,12]{1,0:T(8,128)}, u32[]{:S(2)}) copy-start(f32[8,12]{1,0:T(8,128)} %param.13) | copy-start | bytes 1156
  168.6 24.6 %copy-start.11 = (bf16[1,2,2,720,8]{3,4,2,1,0:T(8,128)(2,1)S(1)}, bf16[1,2,2,720,8]{3,4,2,1,0:T(8,128)(2,1)}, u32[]{:S(2)}) copy-start(bf16[1,2,2,720,8]{3,4,2,1,0:T(8,128)(2,1)} %param.10) | copy-start | bytes 138244
  168.6 24.6 %copy-start.16 = (s32[12]{0:T(128)S(1)}, s32[12]{0:T(128)}, u32[]{:S(2)}) copy-start(s32[12]{0:T(128)} %param.17) | copy-start | bytes 148
  199.7 156.4 %copy-start.9 = (f32[2,2,720]{2,0,1:T(2,128)}, f32[2,2,720]{2,0,1:T(2,128)S(1)}, u32[]{:S(2)}) copy-start(f32[2,2,720]{2,0,1:T(2,128)S(1)} %add_multiply_fusion) | copy-start | bytes 34564
  199.7 156.3 %copy-start.4 = (f32[1,2,2,720,8]{3,1,4,2,0:T(2,128)}, f32[1,2,2,720,8]{3,1,4,2,0:T(2,128)S(1)}, u32[]{:S(2)}) copy-start(f32[1,2,2,720,8]{3,1,4,2,0:T(2,128)S(1)} %copy_convert_fusion.1) | copy-start | bytes 276484
  220.3 135.7 %copy-start.12 = (f32[2,2,720]{2,0,1:T(2,128)}, f32[2,2,720]{2,0,1:T(2,128)S(1)}, u32[]{:S(2)}) copy-start(f32[2,2,720]{2,0,1:T(2,128)S(1)} %fusion.27) | copy-start | bytes 34564
  356.0 19.2 copy-start.17
  356.0 25.5 %slice-start.20 = ((s8[6627328]{0:T(1024)(128)(4,1)}), s8[4194304]{0:T(1024)(128)(4,1)S(1)}, s32[]{:S(2)}) async-start(s8[6627328]{0:T(1024)(128)(4,1)} %bitcast.265), calls=%async_computation.22 | async-start | bytes 8388608
  356.1 25.5 %slice-start.21 = ((s8[6627328]{0:T(1024)(128)(4,1)}), s8[2433024]{0:T(1024)(128)(4,1)S(1)}, s32[]{:S(2)}) async-start(s8[6627328]{0:T(1024)(128)(4,1)} %bitcast.265), calls=%async_computation.23 | async-start | bytes 4866048
  375.3 46.5 %collective-permute-start = (bf16[1,2,1,720,649]{3,1,4,2,0:T(2,128)(2,1)}, bf16[1,2,1,720,649]{3,1,4,2,0:T(2,128)(2,1)}, u32[]{:S(2)}, u32[]{:S(2)}) collective-permute-start(bf16[1,2,1,720,649]{3,1,4,2,0:T(2,128)(2,1)} %get-tuple-element.63), channel_id=1, source_target_pairs={{0,1},{1,2},{2,3},{4,5},{5,6},{6,7},{8,9},{9,10},{10,11},{12,13},{... | collective-permute-start | bytes 5607368 | tf_op jit(solution)/shard_map/ppermute | solution.py:24
  380.2 47.0 %collective-permute-start.1 = (bf16[1,2,1,720,649]{3,1,4,2,0:T(2,128)(2,1)}, bf16[1,2,1,720,649]{3,1,4,2,0:T(2,128)(2,1)}, u32[]{:S(2)}, u32[]{:S(2)}) collective-permute-start(bf16[1,2,1,720,649]{3,1,4,2,0:T(2,128)(2,1)} %get-tuple-element.64), channel_id=1, source_target_pairs={{1,0},{2,1},{3,2},{5,4},{6,5},{7,6},{9,8},{10,9},{11,10},{13,12},{... | collective-permute-start | bytes 5607368 | tf_op jit(solution)/shard_map/ppermute | solution.py:26
  537.5 12.0 copy-start.2
  537.5 26.3 %slice-start.12 = ((s8[7974912]{0:T(1024)(128)(4,1)}), s8[4194304]{0:T(1024)(128)(4,1)S(1)}, s32[]{:S(2)}) async-start(s8[7974912]{0:T(1024)(128)(4,1)} %bitcast.257), calls=%async_computation.14 | async-start | bytes 8388608
  549.5 14.3 slice-start.13
  563.8 27.4 %slice-start.10 = ((s8[7974912]{0:T(1024)(128)(4,1)}), s8[4194304]{0:T(1024)(128)(4,1)S(1)}, s32[]{:S(2)}) async-start(s8[7974912]{0:T(1024)(128)(4,1)} %bitcast.255), calls=%async_computation.12 | async-start | bytes 8388608
  578.2 12.9 slice-start.11
  578.2 27.2 %slice-start.8 = ((s8[7974912]{0:T(1024)(128)(4,1)}), s8[4194304]{0:T(1024)(128)(4,1)S(1)}, s32[]{:S(2)}) async-start(s8[7974912]{0:T(1024)(128)(4,1)} %bitcast.253), calls=%async_computation.10 | async-start | bytes 8388608
  591.2 14.2 slice-start.9
  605.4 27.3 %slice-start.6 = ((s8[7974912]{0:T(1024)(128)(4,1)}), s8[4194304]{0:T(1024)(128)(4,1)S(1)}, s32[]{:S(2)}) async-start(s8[7974912]{0:T(1024)(128)(4,1)} %bitcast.251), calls=%async_computation.8 | async-start | bytes 8388608
  619.7 13.0 slice-start.7
  619.7 27.3 %slice-start.4 = ((s8[7974912]{0:T(1024)(128)(4,1)}), s8[4194304]{0:T(1024)(128)(4,1)S(1)}, s32[]{:S(2)}) async-start(s8[7974912]{0:T(1024)(128)(4,1)} %bitcast.249), calls=%async_computation.6 | async-start | bytes 8388608
  632.7 14.2 slice-start.5
  875.8 19.5 copy-start.8
  875.8 19.5 copy-start.19
  875.8 19.5 copy-start.24
  875.8 19.5 copy-start.29
  894.4 56.5 %copy-start = (f32[2880,641]{0,1:T(8,128)}, f32[2880,641]{0,1:T(8,128)S(1)}, u32[]{:S(2)}) copy-start(f32[2880,641]{0,1:T(8,128)S(1)} %get-tuple-element.126) | copy-start | bytes 22152964
  895.3 15.5 copy-start.3
  895.4 15.4 copy-start.6
  992.2 101.1 %slice-start.2 = ((s8[7630848]{0:T(1024)(128)(4,1)}), s8[3436544]{0:T(1024)(128)(4,1)S(1)}, s32[]{:S(2)}) async-start(s8[7630848]{0:T(1024)(128)(4,1)} %bitcast.247), calls=%async_computation.4 | async-start | bytes 6873088
  1042.5 50.9 %slice-start.3 = ((s8[7630848]{0:T(1024)(128)(4,1)}), s8[4194304]{0:T(1024)(128)(4,1)S(1)}, s32[]{:S(2)}) async-start(s8[7630848]{0:T(1024)(128)(4,1)} %bitcast.247), calls=%async_computation.5 | async-start | bytes 8388608
  1088.1 172.2 %collective-permute-start.2 = (bf16[1,2,1,720,4,649]{3,4,5,2,1,0:T(4,128)(2,1)}, bf16[1,2,1,720,4,649]{3,4,5,2,1,0:T(4,128)(2,1)}, u32[]{:S(2)}, u32[]{:S(2)}) collective-permute-start(bf16[1,2,1,720,4,649]{3,4,5,2,1,0:T(4,128)(2,1)} %copy.84), channel_id=1, source_target_pairs={{0,1},{1,2},{2,3},{4,5},{5,6},{6,7},{8,9},{9,10},{10,11},{12,13},{... | collective-permute-start | bytes 22429448 | tf_op jit(solution)/shard_map/ppermute | solution.py:24
  1128.5 23.5 %slice-start.18 = ((s8[7630848]{0:T(1024)(128)(4,1)}), s8[3436544]{0:T(1024)(128)(4,1)S(1)}, s32[]{:S(2)}) async-start(s8[7630848]{0:T(1024)(128)(4,1)} %bitcast.263), calls=%async_computation.20 | async-start | bytes 6873088
  1137.4 14.6 slice-start.19
  1150.7 174.1 %collective-permute-start.3 = (bf16[1,2,1,720,4,649]{3,4,5,2,1,0:T(4,128)(2,1)}, bf16[1,2,1,720,4,649]{3,4,5,2,1,0:T(4,128)(2,1)}, u32[]{:S(2)}, u32[]{:S(2)}) collective-permute-start(bf16[1,2,1,720,4,649]{3,4,5,2,1,0:T(4,128)(2,1)} %copy.85), channel_id=1, source_target_pairs={{1,0},{2,1},{3,2},{5,4},{6,5},{7,6},{9,8},{10,9},{11,10},{13,12},{... | collective-permute-start | bytes 22429448 | tf_op jit(solution)/shard_map/ppermute | solution.py:26
  1337.6 105.1 %slice-start = ((s8[7876608]{0:T(1024)(128)(4,1)}), s8[4194304]{0:T(1024)(128)(4,1)S(1)}, s32[]{:S(2)}) async-start(s8[7876608]{0:T(1024)(128)(4,1)} %bitcast.245), calls=%async_computation.2 | async-start | bytes 8388608
  1348.8 93.9 %slice-start.1 = ((s8[7876608]{0:T(1024)(128)(4,1)}), s8[3682304]{0:T(1024)(128)(4,1)S(1)}, s32[]{:S(2)}) async-start(s8[7876608]{0:T(1024)(128)(4,1)} %bitcast.245), calls=%async_computation.3 | async-start | bytes 7364608
  1348.8 93.9 %copy-start.5 = (f32[1,2,2,720,8]{3,1,4,2,0:T(2,128)S(1)}, f32[1,2,2,720,8]{3,1,4,2,0:T(2,128)}, u32[]{:S(2)}) copy-start(f32[1,2,2,720,8]{3,1,4,2,0:T(2,128)} %copy-done.4) | copy-start | bytes 276484
  1348.8 93.9 %copy-start.10 = (f32[2,2,720]{2,0,1:T(2,128)S(1)}, f32[2,2,720]{2,0,1:T(2,128)}, u32[]{:S(2)}) copy-start(f32[2,2,720]{2,0,1:T(2,128)} %copy-done.9) | copy-start | bytes 34564
  1348.9 93.9 %copy-start.13 = (f32[2,2,720]{2,0,1:T(2,128)S(1)}, f32[2,2,720]{2,0,1:T(2,128)}, u32[]{:S(2)}) copy-start(f32[2,2,720]{2,0,1:T(2,128)} %copy-done.12) | copy-start | bytes 34564
  1348.9 93.9 %copy-start.18 = (f32[649]{0:T(1024)S(1)}, f32[649]{0:T(1024)}, u32[]{:S(2)}) copy-start(f32[649]{0:T(1024)} %copy-done.17) | copy-start | bytes 7792
  1348.9 93.9 %copy-start.30 = (f32[2]{0:T(128)S(1)}, f32[2]{0:T(128)}, u32[]{:S(2)}) copy-start(f32[2]{0:T(128)} %get-tuple-element.146) | copy-start | bytes 28
  1348.9 93.9 %copy-start.31 = (f32[2]{0:T(128)S(1)}, f32[2]{0:T(128)}, u32[]{:S(2)}) copy-start(f32[2]{0:T(128)} %get-tuple-element.147) | copy-start | bytes 28
  1348.9 93.9 %copy-start.32 = (f32[2]{0:T(128)S(1)}, f32[2]{0:T(128)}, u32[]{:S(2)}) copy-start(f32[2]{0:T(128)} %get-tuple-element.148) | copy-start | bytes 28
  1348.9 93.9 %copy-start.33 = (f32[2]{0:T(128)S(1)}, f32[2]{0:T(128)}, u32[]{:S(2)}) copy-start(f32[2]{0:T(128)} %get-tuple-element.149) | copy-start | bytes 28
  1348.9 93.9 %copy-start.34 = (f32[2]{0:T(128)S(1)}, f32[2]{0:T(128)}, u32[]{:S(2)}) copy-start(f32[2]{0:T(128)} %get-tuple-element.150) | copy-start | bytes 28
  1348.9 93.9 %copy-start.35 = (f32[2]{0:T(128)S(1)}, f32[2]{0:T(128)}, u32[]{:S(2)}) copy-start(f32[2]{0:T(128)} %get-tuple-element.151) | copy-start | bytes 28
  1348.9 93.9 %copy-start.36 = (f32[2]{0:T(128)S(1)}, f32[2]{0:T(128)}, u32[]{:S(2)}) copy-start(f32[2]{0:T(128)} %get-tuple-element.154) | copy-start | bytes 28
  1348.9 93.9 %copy-start.37 = (f32[2]{0:T(128)S(1)}, f32[2]{0:T(128)}, u32[]{:S(2)}) copy-start(f32[2]{0:T(128)} %get-tuple-element.155) | copy-start | bytes 28
  1349.0 93.9 %copy-start.38 = (f32[2]{0:T(128)S(1)}, f32[2]{0:T(128)}, u32[]{:S(2)}) copy-start(f32[2]{0:T(128)} %get-tuple-element.152) | copy-start | bytes 28
  1349.0 93.9 %copy-start.39 = (f32[2]{0:T(128)S(1)}, f32[2]{0:T(128)}, u32[]{:S(2)}) copy-start(f32[2]{0:T(128)} %get-tuple-element.153) | copy-start | bytes 28
  1349.0 93.9 %copy-start.40 = (f32[2]{0:T(128)S(1)}, f32[2]{0:T(128)}, u32[]{:S(2)}) copy-start(f32[2]{0:T(128)} %get-tuple-element.144) | copy-start | bytes 28
  1349.0 93.9 %copy-start.41 = (f32[2]{0:T(128)S(1)}, f32[2]{0:T(128)}, u32[]{:S(2)}) copy-start(f32[2]{0:T(128)} %get-tuple-element.145) | copy-start | bytes 28
  1442.9 188.0 %copy-start.20 = (f32[641]{0:T(1024)S(1)}, f32[641]{0:T(1024)}, u32[]{:S(2)}) copy-start(f32[641]{0:T(1024)} %get-tuple-element.31) | copy-start | bytes 7696
  1442.9 188.0 %copy-start.21 = (f32[641]{0:T(1024)S(1)}, f32[641]{0:T(1024)}, u32[]{:S(2)}) copy-start(f32[641]{0:T(1024)} %get-tuple-element.14) | copy-start | bytes 7696
  1442.9 188.0 %copy-start.22 = (f32[641]{0:T(1024)S(1)}, f32[641]{0:T(1024)}, u32[]{:S(2)}) copy-start(f32[641]{0:T(1024)} %get-tuple-element.34) | copy-start | bytes 7696
  1442.9 188.0 %copy-start.23 = (f32[1282]{0:T(1024)S(1)}, f32[1282]{0:T(1024)}, u32[]{:S(2)}) copy-start(f32[1282]{0:T(1024)} %get-tuple-element.130) | copy-start | bytes 15388
  1442.9 188.0 %copy-start.26 = (f32[641]{0:T(1024)S(1)}, f32[641]{0:T(1024)}, u32[]{:S(2)}) copy-start(f32[641]{0:T(1024)} %get-tuple-element.17) | copy-start | bytes 7696
  1760.9 20.6 %copy-start.15 = (f32[2,2,720]{2,0,1:T(2,128)S(1)}, f32[2,2,720]{2,0,1:T(2,128)}, u32[]{:S(2)}) copy-start(f32[2,2,720]{2,0,1:T(2,128)} %copy-done.14) | copy-start | bytes 34564
  1774.6 26.4 %slice-start.14 = ((s8[7876608]{0:T(1024)(128)(4,1)}), s8[3682304]{0:T(1024)(128)(4,1)S(1)}, s32[]{:S(2)}) async-start(s8[7876608]{0:T(1024)(128)(4,1)} %bitcast.259), calls=%async_computation.16 | async-start | bytes 7364608
  1781.6 19.4 slice-start.15
  (7 other events, 21.3 us)
Sparse Core Ops, SparseCore 0:
  11.5 100.4 all-gather.2
  1745.6 235.8 all-reduce.4
where the time goes:
time: 2010 us; the launch traced here: 1990 us
  other arithmetic  774 us (39%)
  local copies, waits for them, and re-layouts  669 us (33%)
  waiting for transfers between devices  298 us (15%)
  matrix products  138 us (7%)
  between operations  97.7 us (5%)
    reduce_sum x2, other arithmetic, layer_norm(): return centered * lax.rsqrt(variance + 1e-05) * norm_gain + norm_shift  194 us
    convert_element_type x12, local copies, waits for them, and re-layouts, forward_pass(): weighting[None, None, :, None, :, None] * window_part[:, :, :, :, None, :]  165 us
    unnamed x3, waiting for transfers between devices  162 us
    concatenate x2, other arithmetic, wrap_columns(): jnp.concatenate([values[:, :, :, -REACH:], values, values[:, :, :, :REACH...  135 us
    all_gather x1, other arithmetic, forward_pass(): gathered = lax.all_gather(params, ('date', 'lat'), axis=0, tiled=True)  122 us
    convert_element_type x1, other arithmetic, forward_pass(): basis_low = terms.reshape(-1, BASIS * CIN).astype(jnp.bfloat16)  113 us
    concatenate x1, local copies, waits for them, and re-layouts, local(): jnp.concatenate([grad_disco.reshape(-1), grad_conv_bias, grad_first_gain,...  105 us
    ppermute x2, waiting for transfers between devices, extended_2(): lax.ppermute(tail, axis, [(i, (i + 1) % count) for i in range(ends)])  103 us
  transfers between devices with their start and end apart: 6, of which 5 were waited for; matrix products, arithmetic and copies ran while one was open for 17% of the time, Pallas kernels for 0%

commit v1 on v0

v1 whole, which is shorter than its diff:
```python
import functools
import math

import jax
import jax.numpy as jnp
from jax import lax
from jax.experimental import pallas as pl
from jax.experimental.pallas import tpu as pltpu
from jax.sharding import PartitionSpec as P

C = 641
HID = 1282
BASIS = 4
SUPPORT = 12
REACH = 2
CIN = 649
BF16, F32 = jnp.bfloat16, jnp.float32
MESH = pl.DeviceIdType.MESH
LANES = 128
STEP = 16
CP = 656
HP = 1296
WIDE = 768
HL = 1408
UNROLL = 4
VMEM = 60 << 20


OFF_G1=BASIS*CIN*C+C; OFF_S1=OFF_G1+CIN; OFF_G2=OFF_S1+CIN; OFF_S2=OFF_G2+C; OFF_UP=OFF_S2+C; OFF_DN=OFF_UP+(C+1)*HID;
SMALL=((OFF_G1,CIN),(OFF_S1,CIN),(OFF_G2,C),(OFF_S2,C))
MATS=((0,C,BASIS*CIN+1,128,3),(OFF_UP,HID,C+1,64,2),(OFF_DN,C,HID+1,128,2))
F_ROWS=29952
def lane_ids(): return lax.broadcasted_iota(jnp.int32,(8,LANES),1)
def place(base,cols,period,b):
    start=base+cols*b
    return start//LANES, start%LANES
def unpack_kernel(nrow,pad, g_ref, w_ref,wt_ref,up_ref,upt_ref,dn_ref,dnt_ref,small_ref,flat,chunks):
    def fill(s,_):
        flat[pl.ds(nrow*s,pad),:]=g_ref[s].astype(F32); return 0
    lax.fori_loop(0,g_ref.shape[0],fill,0)
    lane=lane_ids()
    def split(base,cols,period,groups):
        J=-(-cols//LANES); pitch=period+8; height=pitch*8*groups+8; last=cols-(J-1)*LANES
        def body(b,_):
            row,s=place(base,cols,period,b)
            back=(LANES-s)%LANES
            for g in range(groups):
                rolled=[pltpu.roll(flat[pl.ds(row+641*8*g+j,8,stride=641),:],back,axis=1) for j in range(J+1)]
                for j in range(J):
                    val=jnp.where(lane<LANES-s,rolled[j],rolled[j+1])
                    if j==J-1: val=jnp.where(lane<last,val,0.0)
                    chunks[pl.ds(j*height+8*g*pitch+b,8,stride=pitch),:]=val
            return 0
        lax.fori_loop(0,period,body,0,unroll=8)
        def border(a,_):
            for j in range(J): chunks[pl.ds(j*height+a*pitch-8,8),:]=chunks[pl.ds(j*height+a*pitch,8),:]
            return 0
        lax.fori_loop(1,8*groups,border,0)
        return J,height,period
    def convert(dst,dst_row,src_row,rows,pad_rows,J,height,period):
        full=rows//16
        def piece(j,r): return chunks[pl.ds(j*height+r//period*(period+8)+r%period,8),:]
        def pair(j,r): return jnp.concatenate([piece(j,r),piece(j,r+8)],axis=0)
        def body(m,_):
            for j in range(J):
                dst[pl.ds(pl.multiple_of(dst_row+16*m,16),16),j*LANES:(j+1)*LANES]=pair(j,src_row+16*m).astype(BF16)
            return 0
        lax.fori_loop(0,full,body,0,unroll=4)
        keep=lax.broadcasted_iota(jnp.int32,(16,LANES),0)<rows-16*full
        for m in range(full,pad_rows//16):
            for j in range(J):
                v=jnp.where(keep,pair(j,src_row+16*m),0.0) if m==full else jnp.zeros((16,LANES),F32)
                dst[dst_row+16*m:dst_row+16*m+16,j*LANES:(j+1)*LANES]=v.astype(BF16)
    J,h,p=split(*MATS[0][:2],*MATS[0][3:])
    for k in range(BASIS):
        convert(w_ref,k*CP,k*CIN,CIN+(k==BASIS-1),CP,J,h,p)
    J,h,p=split(*MATS[1][:2],*MATS[1][3:])
    convert(up_ref,0,0,C+1,CP,J,h,p)
    J,h,p=split(*MATS[2][:2],*MATS[2][3:])
    convert(dn_ref,0,0,HID+1,HP,J,h,p)
    wt_ref[...]=w_ref[:,:CP].T
    upt_ref[...]=up_ref[:,:HP].T
    dnt_ref[...]=dn_ref[:,:CP].T
    for i,(off,n) in enumerate(SMALL):
        row,s=divmod(off,LANES)
        r=pltpu.roll(flat[row:row+8,:],(LANES-s)%LANES,axis=1)
        v=jnp.where(lane<LANES-s,r,pltpu.roll(r,7,axis=0))
        sub=lax.broadcasted_iota(jnp.int32,(8,LANES),0)
        v=jnp.where(sub*LANES+lane<n,v,0.0)
        t=v.T
        for j in range(6):
            rows=min(LANES,CP-j*LANES)
            small_ref[i,j*LANES:j*LANES+rows,:]=jnp.broadcast_to(t[:rows,j:j+1],(rows,LANES))
def unpack(gathered,nrow):
    n,pad,_=gathered.shape
    return pl.pallas_call(functools.partial(unpack_kernel,nrow,pad),
        out_shape=(jax.ShapeDtypeStruct((BASIS*CP,WIDE),BF16),jax.ShapeDtypeStruct((CP,BASIS*CP),BF16),
            jax.ShapeDtypeStruct((CP,HL),BF16),jax.ShapeDtypeStruct((HP,CP),BF16),
            jax.ShapeDtypeStruct((HP,WIDE),BF16),jax.ShapeDtypeStruct((CP,HP),BF16),jax.ShapeDtypeStruct((4,CP,LANES),F32)),
        scratch_shapes=[pltpu.VMEM((F_ROWS,LANES),F32),pltpu.VMEM((6*(136*24+8),LANES),F32)],
        compiler_params=pltpu.CompilerParams(vmem_limit_bytes=VMEM),name="unpack")(gathered)
def pack_kernel(nrow,pad,gd_ref,gu_ref,gn_ref,sm_ref,out_ref,flat,chunks):
    lane=lane_ids(); sub=lax.broadcasted_iota(jnp.int32,(8,LANES),0)
    def gather(src,src_row,dst_row,rows,J,height,last,period):
        full=rows//8
        def cols(m,j):
            v=src[pl.ds(pl.multiple_of(src_row+8*m,8),8),j*LANES:(j+1)*LANES]
            return jnp.where(lane<last,v,0.0) if j==J-1 else v
        def body(m,_):
            r=dst_row+8*m; at=r//period*(period+8)+r%period
            for j in range(J):
                v=cols(m,j)
                chunks[pl.ds(j*height+at+8,8),:]=v
                chunks[pl.ds(j*height+at,8),:]=v
            return 0
        lax.fori_loop(0,full,body,0,unroll=4)
        if rows%8:
            r=dst_row+8*full; at=r//period*(period+8)+r%period
            for j in range(J):
                v=jnp.where(sub<rows-8*full,cols(full,j),0.0)
                chunks[pl.ds(j*height+at+8,8),:]=v
                chunks[pl.ds(j*height+at,8),:]=v
    def clear(J,height,row,period):
        row=row//period*(period+8)+row%period
        count=(height-row)//8
        def body(m,_):
            for j in range(J): chunks[pl.ds(j*height+row+8*m,8),:]=jnp.zeros((8,LANES),F32)
            return 0
        lax.fori_loop(0,count,body,0)
    def merge(base,cols,period,groups):
        J=-(-cols//LANES); pitch=period+8; height=pitch*8*groups+8
        def body(b,tails,rows=J):
            row,s=place(base,cols,period,b)
            new=[]
            for g in range(groups):
                x=[pltpu.roll(chunks[pl.ds(j*height+8*g*pitch+b,8,stride=pitch),:],s,axis=1) for j in range(J)]
                first=lane>=s
                for j in range(J):
                    v=jnp.where(first,x[j],tails[g] if j==0 else x[j-1])
                    if j<rows: flat[pl.ds(row+641*8*g+j,8,stride=641),:]=v
                new.append(jnp.where(s==LANES-1,jnp.where(first,0.0,x[J-1]),v))
            return tuple(new)
        row0=base//LANES
        init=[jnp.zeros((8,LANES),F32)]*groups
        if base%LANES:
            init[0]=jnp.where(sub==0,flat[row0:row0+8,:],0.0)
        tails=lax.fori_loop(0,period-8,body,tuple(init),unroll=8)
        for b in range(period-8,period):
            tails=body(b,tails,J-1 if base%LANES and b==period-1 else J)
        if base%LANES:
            for g in range(groups):
                at=pl.ds(row0+641*(8*g+1),8,stride=641)
                flat[at,:]=flat[at,:]+tails[g]
    h=136*24+8
    for k in range(BASIS): gather(gd_ref,k*CP,k*CIN,CIN+(k==BASIS-1),6,h,1,128)
    clear(6,h,2600,128)
    merge(0,C,128,3)
    h=72*16+8
    gather(gu_ref,0,0,C+1,11,h,2,64)
    clear(11,h,648,64)
    merge(OFF_UP,HID,64,2)
    h=136*16+8
    gather(gn_ref,0,0,HID+1,6,h,1,128)
    clear(6,h,1288,128)
    merge(OFF_DN,C,128,2)
    for i,(off,n) in enumerate(SMALL):
        row,s=divmod(off,LANES)
        r=pltpu.roll(sm_ref[i],s,axis=1)
        prev=pltpu.roll(r,1,axis=0)
        v=jnp.where(lane>=s,r,jnp.where(sub==0,0.0,prev))
        flat[row:row+8,:]=flat[row:row+8,:]+v
    def store(s,_):
        out_ref[s]=flat[pl.ds(nrow*s,pad),:].astype(BF16); return 0
    lax.fori_loop(0,out_ref.shape[0],store,0)
def pack(gd,gu,gn,sm,n,nrow,pad):
    return pl.pallas_call(functools.partial(pack_kernel,nrow,pad),
        out_shape=jax.ShapeDtypeStruct((n,pad,LANES),BF16),
        scratch_shapes=[pltpu.VMEM((F_ROWS,LANES),F32),pltpu.VMEM((6*(136*24+8),LANES),F32)],
        compiler_params=pltpu.CompilerParams(vmem_limit_bytes=VMEM),name="pack")(gd,gu,gn,sm)


def tiled(column):
    return jnp.concatenate([column] * (WIDE // LANES), axis=1)


def lane_of(rows, start=0):
    return lax.broadcasted_iota(jnp.int32, (rows, LANES), 1) + start


def wrapped(chunk, width):
    head, first, last = chunk[:, : WIDE - LANES], chunk[:, :LANES], chunk[:, WIDE - LANES :]
    edge = width - (WIDE - LANES)
    lane = lane_of(chunk.shape[0])
    beyond = jnp.where(
        lane < LANES - REACH, pltpu.roll(first, edge, axis=1), pltpu.roll(last, LANES - edge, axis=1)
    )
    return jnp.concatenate([head, jnp.where(lane < edge, last, beyond)], axis=1)


def cut(chunk, width):
    head, last = chunk[:, : WIDE - LANES], chunk[:, WIDE - LANES :]
    keep = lane_of(chunk.shape[0], WIDE - LANES) < width
    return jnp.concatenate([head, jnp.where(keep, last, 0.0)], axis=1)


def rows_below(count):
    return lax.broadcasted_iota(jnp.int32, (STEP, WIDE), 0) < count


def halves(chunk):
    return chunk[:8] + chunk[8:]


def column_sums(read, channels, count):
    whole = channels // STEP

    def body(m, sums):
        return tuple(a + halves(v) for a, v in zip(sums, read(m)))

    sums = lax.fori_loop(
        0, whole, body, tuple(jnp.zeros((8, WIDE), F32) for _ in range(count)), unroll=UNROLL
    )
    keep = rows_below(channels - whole * STEP)
    sums = [a + halves(jnp.where(keep, v, 0.0)) for a, v in zip(sums, read(whole))]
    return [jnp.sum(a, axis=0, keepdims=True) for a in sums]


def norm_stats(read, channels):
    (total,) = column_sums(lambda m: (read(m),), channels, 1)
    mean = total * (1.0 / channels)

    def squares(m):
        centered = read(m) - mean
        return (centered * centered,)

    (total,) = column_sums(squares, channels, 1)
    return mean, lax.rsqrt(total * (1.0 / channels) + 1e-05)


def each_chunk(body, unroll=None):
    def step(m, _):
        body(m, pl.ds(pl.multiple_of(m * STEP, STEP), STEP))
        return 0

    lax.fori_loop(0, CP // STEP, step, 0, unroll=unroll)


def lift_kernel(rows, lat, width, offsets, bases, psi, lo, own, hi, gain, shift, out, moved, table):
    first_row = lax.axis_index("lat") * rows
    for k in range(BASIS):
        table[SUPPORT + k] = 0
    for p in range(SUPPORT):
        k = bases[p]
        used = table[SUPPORT + k]
        table[k * 3 + used] = p
        table[SUPPORT + k] = used + 1
    for m in range(rows + 2):
        source = lo if m == 0 else hi if m == rows + 1 else own.at[:, m - 1]

        def read(c):
            return source[0, pl.ds(pl.multiple_of(c * STEP, STEP), STEP), :].astype(F32)

        mean, scale = norm_stats(read, CIN)

        def shifts(c, at):
            values = (source[0, at, :].astype(F32) - mean) * scale
            values = values * tiled(gain[at, :]) + tiled(shift[at, :])
            values = wrapped(values, width).astype(BF16)
            for d in range(-REACH, REACH + 1):
                moved[m, d + REACH, at, :] = pltpu.roll(values, -d % WIDE, axis=1) if d else values

        each_chunk(shifts, 1)
    for r in range(rows):
        for k in range(BASIS):
            parts = []
            for q in range(3):
                p = table[k * 3 + q]
                row = first_row + r + offsets[p, 0]
                inside = jnp.logical_and(row >= 0, row < lat)
                weight = jnp.where(inside, psi[first_row + r, p], 0.0)
                parts.append((weight, r + 1 + offsets[p, 0], offsets[p, 1] + REACH))

            def combine(c, at):
                total = None
                for weight, row, d in parts:
                    term = weight * moved[row, d, at, :].astype(F32)
                    total = term if total is None else total + term
                to = pl.ds(pl.multiple_of(k * CP + c * STEP, STEP), STEP)
                out[0, r, to, :] = cut(total, width).astype(BF16)

            each_chunk(combine, 1)
        last = slice(BASIS * CP - STEP, BASIS * CP)
        bias_row = CIN - (CP - STEP)
        sub = lax.broadcasted_iota(jnp.int32, (STEP, WIDE), 0)
        lane = lax.broadcasted_iota(jnp.int32, (STEP, WIDE), 1)
        ones = jnp.where(lane < width, 1.0, 0.0)
        out[0, r, last, :] = jnp.where(sub == bias_row, ones, out[0, r, last, :].astype(F32)).astype(BF16)


def lift(offsets, bases, psi, lo, own, hi, gain, shift, lat, width):
    slabs, rows = own.shape[:2]
    smem = pl.BlockSpec(memory_space=pltpu.SMEM)
    halo = pl.BlockSpec((1, CP, WIDE), lambda s: (s, 0, 0))
    column = pl.BlockSpec((CP, LANES), lambda s: (0, 0))
    return pl.pallas_call(
        functools.partial(lift_kernel, rows, lat, width),
        grid=(slabs,),
        in_specs=[
            smem,
            smem,
            smem,
            halo,
            pl.BlockSpec((1, rows, CP, WIDE), lambda s: (s, 0, 0, 0)),
            halo,
            column,
            column,
        ],
        out_specs=pl.BlockSpec((1, rows, BASIS * CP, WIDE), lambda s: (s, 0, 0, 0)),
        out_shape=jax.ShapeDtypeStruct((slabs, rows, BASIS * CP, WIDE), BF16),
        scratch_shapes=[
            pltpu.VMEM((rows + 2, 2 * REACH + 1, CP, WIDE), BF16),
            pltpu.SMEM((SUPPORT + BASIS,), jnp.int32),
        ],
        compiler_params=pltpu.CompilerParams(vmem_limit_bytes=VMEM),
        name="lift",
    )(offsets, bases, psi, lo, own, hi, gain, shift)


GELU_A = math.sqrt(2.0 / math.pi)
GELU_B = 0.044715


def block_kernel(
    width, basis, x, cot, mask, wt, upt, up, dnt, dn, gain, shift,
    out, gconv, gup, gdn, sums,
    res, second, pre, act, slope, gb, gpre, gsec,
):
    start = pl.program_id(0) == 0

    @pl.when(start)
    def _():
        gup[...] = jnp.zeros_like(gup)
        gdn[...] = jnp.zeros_like(gdn)
        sums[...] = jnp.zeros_like(sums)

    def dot(a, b):
        return jnp.dot(a, b, preferred_element_type=F32)

    res[...] = dot(wt[...], basis[0])

    def add_input(c, at):
        values = x[0, at, :].astype(F32)
        keep = lax.broadcasted_iota(jnp.int32, (STEP, WIDE), 0) + c * STEP < C
        res[at, :] = res[at, :] + jnp.where(keep, values, 0.0)
        gb[at, :] = (cot[0, at, :].astype(F32) * mask[0]).astype(BF16)

    each_chunk(add_input, 1)

    def read(c):
        return res[pl.ds(pl.multiple_of(c * STEP, STEP), STEP), :]

    mean, scale = norm_stats(read, C)

    def normalize(c, at):
        values = (res[at, :] - mean) * scale * tiled(gain[at, :]) + tiled(shift[at, :])
        row = lax.broadcasted_iota(jnp.int32, (STEP, WIDE), 0) + c * STEP
        second[at, :] = jnp.where(row == C, 1.0, values).astype(BF16)

    each_chunk(normalize, 1)
    pre[...] = dot(upt[...], second[...])

    def gelu(c, _):
        at = pl.ds(pl.multiple_of(c * STEP, STEP), STEP)
        v = pre[at, :]
        square = v * v
        bend = jnp.tanh(GELU_A * v * (1.0 + GELU_B * square))
        half = 0.5 * (1.0 + bend)
        row = lax.broadcasted_iota(jnp.int32, (STEP, WIDE), 0) + c * STEP
        act[at, :] = jnp.where(row == HID, 1.0, v * half).astype(BF16)
        rise = GELU_A * (1.0 + 3.0 * GELU_B * square)
        slope[at, :] = half + 0.5 * v * (1.0 - bend * bend) * rise
        return 0

    lax.fori_loop(0, HP // STEP, gelu, 0)
    pre[:CP, :] = dot(dnt[...], act[...])

    def finish(c, at):
        out[0, at, :] = (res[at, :] + pre[at, :]).astype(BF16)

    each_chunk(finish, 1)
    pre[...] = dot(dn[:, :CP], gb[...])

    def back(c, _):
        at = pl.ds(pl.multiple_of(c * STEP, STEP), STEP)
        gpre[at, :] = (pre[at, :] * slope[at, :]).astype(BF16)
        return 0

    lax.fori_loop(0, HP // STEP, back, 0)
    gsec[...] = dot(up[:, :HP], gpre[...])

    def means(c):
        at = pl.ds(pl.multiple_of(c * STEP, STEP), STEP)
        g = gsec[at, :] * tiled(gain[at, :])
        return g, g * ((res[at, :] - mean) * scale)

    flat, along = [v * (1.0 / C) for v in column_sums(means, C, 2)]

    def backward(c, at):
        dm = gsec[at, :]
        xhat = (res[at, :] - mean) * scale
        g = dm * tiled(gain[at, :])
        value = gb[at, :].astype(F32) + scale * (g - flat - xhat * along)
        row = lax.broadcasted_iota(jnp.int32, (STEP, WIDE), 0) + c * STEP
        value = jnp.where(row < C, value, 0.0)
        gconv[0, at, :] = wrapped(value, width).astype(BF16)
        along_lanes(sums.at[0], at, dm * xhat)
        along_lanes(sums.at[1], at, dm)

    each_chunk(backward, 1)

    def outer(a, b):
        return lax.dot_general(a, b, (((1,), (1,)), ((), ())), preferred_element_type=F32)

    gdn[:, :CP] += outer(act[...], gb[...])
    gup[:, :HP] += outer(second[...], gpre[...])


def along_lanes(ref, at, values):
    total = values[:, :LANES]
    for j in range(1, WIDE // LANES):
        total = total + values[:, j * LANES : (j + 1) * LANES]
    ref[at, :] = ref[at, :] + total


def block(basis, x, cot, mask, wt, upt, up, dnt, dn, gain, shift, width):
    count = x.shape[0]

    def per_row(height):
        return pl.BlockSpec((1, height, WIDE), lambda i: (i, 0, 0))

    def whole(a):
        return pl.BlockSpec(a.shape, lambda i: (0,) * len(a.shape), pipeline_mode=pl.Buffered(1))

    outs = (
        jax.ShapeDtypeStruct((count, CP, WIDE), BF16),
        jax.ShapeDtypeStruct((count, CP, WIDE), BF16),
        jax.ShapeDtypeStruct((CP, HL), F32),
        jax.ShapeDtypeStruct((HP, WIDE), F32),
        jax.ShapeDtypeStruct((2, CP, LANES), F32),
    )
    weights = (wt, upt, up, dnt, dn, gain, shift)
    return pl.pallas_call(
        functools.partial(block_kernel, width),
        grid=(count,),
        in_specs=[per_row(BASIS * CP), per_row(CP), per_row(CP), per_row(1)] + [whole(a) for a in weights],
        out_specs=[per_row(CP), per_row(CP)] + [whole(a) for a in outs[2:]],
        out_shape=outs,
        scratch_shapes=[
            pltpu.VMEM((CP, WIDE), F32),
            pltpu.VMEM((CP, WIDE), BF16),
            pltpu.VMEM((HP, WIDE), F32),
            pltpu.VMEM((HP, WIDE), BF16),
            pltpu.VMEM((HP, WIDE), F32),
            pltpu.VMEM((CP, WIDE), BF16),
            pltpu.VMEM((HP, WIDE), BF16),
            pltpu.VMEM((CP, WIDE), F32),
        ],
        compiler_params=pltpu.CompilerParams(vmem_limit_bytes=VMEM),
        name="block",
    )(basis, x, cot, mask, *weights)


def outer_kernel(basis, gconv, out):
    i = pl.program_id(0)
    term = lax.dot_general(basis[0], gconv[0], (((1,), (1,)), ((), ())), preferred_element_type=F32)

    @pl.when(i == 0)
    def _():
        out[:, :CP] = term

    @pl.when(i > 0)
    def _():
        out[:, :CP] += term


def weight_grad(basis, gconv):
    count = basis.shape[0]
    return pl.pallas_call(
        outer_kernel,
        grid=(count,),
        in_specs=[
            pl.BlockSpec((1, BASIS * CP, WIDE), lambda i: (i, 0, 0)),
            pl.BlockSpec((1, CP, WIDE), lambda i: (i, 0, 0)),
        ],
        out_specs=pl.BlockSpec((BASIS * CP, WIDE), lambda i: (0, 0)),
        out_shape=jax.ShapeDtypeStruct((BASIS * CP, WIDE), F32),
        compiler_params=pltpu.CompilerParams(vmem_limit_bytes=VMEM),
        name="weight_grad",
    )(basis, gconv)


def lower_kernel(rows, offsets, bases, psi, gconv, w, own, lo, hi, lifted, place, coef):
    first_row = lax.axis_index("lat") * rows
    span = 2 * REACH + 1
    for n in range(3 * span):
        place[n] = 0
        for r in range(rows):
            coef[r, n] = 0.0
    for p in range(SUPPORT):
        n = (offsets[p, 0] + 1) * span + offsets[p, 1] + REACH
        place[n] = bases[p]
        for r in range(rows):
            coef[r, n] = psi[first_row + r, p]
    for r in range(rows):
        lifted[r] = jnp.dot(w[:, :CP], gconv[0, r], preferred_element_type=F32).astype(BF16)
    for target in range(-1, rows + 1):
        terms = []
        for d in range(-REACH, REACH + 1):
            for o in (-1, 0, 1):
                r = target - o
                if 0 <= r < rows:
                    n = (o + 1) * span + d + REACH
                    terms.append((d, r, coef[r, n], place[n] * CP))

        def gather(c, at):
            total = None
            for d in range(-REACH, REACH + 1):
                part = None
                for e, r, weight, base in terms:
                    if e == d:
                        source = pl.ds(pl.multiple_of(base + c * STEP, STEP), STEP)
                        term = weight * lifted[r, source, :].astype(F32)
                        part = term if part is None else part + term
                if d:
                    part = pltpu.roll(part, d % WIDE, axis=1)
                total = part if total is None else total + part
            if target < 0:
                lo[0, at, :] = total.astype(BF16)
            elif target == rows:
                hi[0, at, :] = total.astype(BF16)
            else:
                own[0, target, at, :] = total

        each_chunk(gather, 1)


def lower(offsets, bases, psi, gconv, w):
    slabs, rows = gconv.shape[:2]
    smem = pl.BlockSpec(memory_space=pltpu.SMEM)
    halo = pl.BlockSpec((1, CP, WIDE), lambda s: (s, 0, 0))
    per_slab = pl.BlockSpec((1, rows, CP, WIDE), lambda s: (s, 0, 0, 0))
    edge = jax.ShapeDtypeStruct((slabs, CP, WIDE), BF16)
    return pl.pallas_call(
        functools.partial(lower_kernel, rows),
        grid=(slabs,),
        in_specs=[
            smem,
            smem,
            smem,
            per_slab,
            pl.BlockSpec(w.shape, lambda s: (0, 0), pipeline_mode=pl.Buffered(1)),
        ],
        out_specs=[per_slab, halo, halo],
        out_shape=(jax.ShapeDtypeStruct((slabs, rows, CP, WIDE), F32), edge, edge),
        scratch_shapes=[
            pltpu.VMEM((rows, BASIS * CP, WIDE), BF16),
            pltpu.SMEM((3 * (2 * REACH + 1),), jnp.int32),
            pltpu.SMEM((rows, 3 * (2 * REACH + 1)), F32),
        ],
        compiler_params=pltpu.CompilerParams(vmem_limit_bytes=VMEM),
        name="lower",
    )(offsets, bases, psi, gconv, w)


def input_kernel(rows, width, x, gconv, own, lo, hi, gain, out, sums, total):
    r = pl.program_id(1)

    @pl.when(jnp.logical_and(pl.program_id(0) == 0, r == 0))
    def _():
        sums[...] = jnp.zeros_like(sums)

    from_below = jnp.where(r == 0, 1.0, 0.0)
    from_above = jnp.where(r == rows - 1, 1.0, 0.0)

    def read(c):
        return x[0, 0, pl.ds(pl.multiple_of(c * STEP, STEP), STEP), :].astype(F32)

    mean, scale = norm_stats(read, CIN)

    def join(c, at):
        halo = lo[0, at, :].astype(F32) * from_below + hi[0, at, :].astype(F32) * from_above
        total[at, :] = own[0, 0, at, :] + halo

    each_chunk(join, 1)

    def means(c):
        at = pl.ds(pl.multiple_of(c * STEP, STEP), STEP)
        g = total[at, :] * tiled(gain[at, :])
        return g, g * ((read(c) - mean) * scale)

    flat, along = [v * (1.0 / CIN) for v in column_sums(means, CIN, 2)]

    def backward(c, at):
        dm = cut(total[at, :], width)
        xhat = (read(c) - mean) * scale
        g = dm * tiled(gain[at, :])
        value = scale * (g - flat - xhat * along) + gconv[0, 0, at, :].astype(F32)
        out[0, 0, at, :] = value.astype(BF16)
        along_lanes(sums.at[0], at, dm * xhat)
        along_lanes(sums.at[1], at, dm)

    each_chunk(backward, 1)


def input_grad(x, gconv, own, lo, hi, gain, width):
    slabs, rows = x.shape[:2]
    per_row = pl.BlockSpec((1, 1, CP, WIDE), lambda s, r: (s, r, 0, 0))
    halo = pl.BlockSpec((1, CP, WIDE), lambda s, r: (s, 0, 0))
    return pl.pallas_call(
        functools.partial(input_kernel, rows, width),
        grid=(slabs, rows),
        in_specs=[per_row, per_row, per_row, halo, halo, pl.BlockSpec((CP, LANES), lambda s, r: (0, 0))],
        out_specs=[per_row, pl.BlockSpec((2, CP, LANES), lambda s, r: (0, 0, 0))],
        out_shape=(
            jax.ShapeDtypeStruct((slabs, rows, CP, WIDE), BF16),
            jax.ShapeDtypeStruct((2, CP, LANES), F32),
        ),
        scratch_shapes=[pltpu.VMEM((CP, WIDE), F32)],
        compiler_params=pltpu.CompilerParams(vmem_limit_bytes=VMEM),
        name="input_grad",
    )(x, gconv, own, lo, hi, gain)


def flip(value, bit):
    return value + (1 - 2 * ((value // (1 << bit)) % 2)) * (1 << bit)


def flipped(value, mask):
    bit = 0
    while mask >> bit:
        if mask >> bit & 1:
            value = flip(value, bit)
        bit += 1
    return value


def span(bits):
    masks = [0]
    for b in bits:
        masks = masks + [m | 1 << b for m in masks]
    return masks


def orders(dates):
    bits = list(range(1, dates.bit_length() - 1))
    return bits + [0], bits[::-1] + [0]


def greet(dates, lats, d, l):
    barrier = pltpu.get_barrier_semaphore()
    count = 0
    for o in range(1, lats):
        pl.semaphore_signal(barrier, inc=1, device_id=(d, lax.rem(l + o, lats)), device_id_type=MESH)
        count += 1
    for b in range(dates.bit_length() - 1):
        pl.semaphore_signal(barrier, inc=1, device_id=(flip(d, b), l), device_id_type=MESH)
        count += 1
    pl.semaphore_wait(barrier, count)


def gather_kernel(dates, lats, src, out, local_sem, z_send, z_recv, send, recv):
    d, l = lax.axis_index("date"), lax.axis_index("lat")
    half = lats // 2
    greet(dates, lats, d, l)
    own = pltpu.make_async_copy(src, out.at[d, l], local_sem)
    own.start()
    z = []
    for o in range(1, lats):
        z.append(
            pltpu.make_async_remote_copy(
                src_ref=src,
                dst_ref=out.at[d, l],
                send_sem=z_send.at[o - 1],
                recv_sem=z_recv.at[o - 1],
                device_id=(d, lax.rem(l + o, lats)),
                device_id_type=MESH,
            )
        )
        z[-1].start()
    own.wait()
    for copy in z:
        copy.wait_recv()
    sent = []

    def cross(h, i, mask):
        order = orders(dates)[h]
        at = span(order[:i]).index(mask)
        block = out.at[flipped(d, mask), pl.ds(h * half, half)]
        slot = (1 << i) - 1 + at
        copy = pltpu.make_async_remote_copy(
            src_ref=block,
            dst_ref=block,
            send_sem=send.at[h, slot],
            recv_sem=recv.at[h, slot],
            device_id=(flip(d, order[i]), l),
            device_id_type=MESH,
        )
        copy.start()
        sent.append(copy)
        return copy

    flights = {}
    steps = dates.bit_length() - 1
    for i in range(steps):
        for h in range(2):
            flights[h, i, 0] = cross(h, i, 0)
    for i in range(steps):
        for at, mask in enumerate(span(orders(dates)[0][:i])):
            for h in range(2):
                order = orders(dates)[h]
                mask = span(order[:i])[at]
                flights[h, i, mask].wait_recv()
                for later in range(i + 1, steps):
                    reached = mask | 1 << order[i]
                    flights[h, later, reached] = cross(h, later, reached)
    for copy in z + sent:
        copy.wait_send()


def gather(shard, dates, lats):
    slots = dates - 1
    return pl.pallas_call(
        functools.partial(gather_kernel, dates, lats),
        in_specs=[pl.BlockSpec(memory_space=pl.ANY)],
        out_specs=pl.BlockSpec(memory_space=pl.ANY),
        out_shape=jax.ShapeDtypeStruct((dates, lats) + shard.shape, shard.dtype),
        scratch_shapes=[
            pltpu.SemaphoreType.DMA(()),
            pltpu.SemaphoreType.DMA((lats - 1,)),
            pltpu.SemaphoreType.DMA((lats - 1,)),
            pltpu.SemaphoreType.DMA((2, slots)),
            pltpu.SemaphoreType.DMA((2, slots)),
        ],
        compiler_params=pltpu.CompilerParams(collective_id=0, has_side_effects=True),
        name="gather_params",
    )(shard)


def scatter_kernel(dates, lats, src, out, parts, mine, others, z_send, z_recv, send, recv):
    d, l = lax.axis_index("date"), lax.axis_index("lat")
    half = lats // 2
    greet(dates, lats, d, l)
    steps = dates.bit_length() - 1
    sent = []
    paths = [order[::-1] for order in orders(dates)]

    def slot_of(h, i, mask):
        later = span(paths[h][i + 1 :][::-1])
        first = sum(1 << (steps - 1 - e) for e in range(i))
        return first + later.index(mask)

    def holder(h, i, mask):
        if i == 0:
            return src.at[flipped(d, mask), pl.ds(h * half, half)]
        return parts.at[h, slot_of(h, i - 1, mask)]

    def cross(h, i, mask):
        bit = paths[h][i]
        slot = slot_of(h, i, mask)
        copy = pltpu.make_async_remote_copy(
            src_ref=holder(h, i, mask | 1 << bit),
            dst_ref=parts.at[h, slot],
            send_sem=send.at[h, slot],
            recv_sem=recv.at[h, slot],
            device_id=(flip(d, bit), l),
            device_id_type=MESH,
        )
        copy.start()
        sent.append(copy)
        return copy

    def left(h, i):
        masks = span(paths[h][i + 1 :][::-1])
        return masks[::-1]

    flights = {}
    for n in range(len(left(0, 0))):
        for h in range(2):
            mask = left(h, 0)[n]
            flights[h, 0, mask] = cross(h, 0, mask)
    for i in range(steps):
        for n in range(len(left(0, i))):
            for h in range(2):
                mask = left(h, i)[n]
                flights[h, i, mask].wait_recv()
                have = holder(h, i, mask)
                got = parts.at[h, slot_of(h, i, mask)]
                for s in range(half):
                    total = have[s].astype(F32) + got[s].astype(F32)
                    if i == steps - 1:
                        mine[h * half + s] = total.astype(BF16)
                    else:
                        got[s] = total.astype(BF16)
                if i + 1 < steps and mask >> paths[h][i + 1] & 1:
                    ahead = mask & ~(1 << paths[h][i + 1])
                    flights[h, i + 1, ahead] = cross(h, i + 1, ahead)
    z = []
    for o in range(1, lats):
        to = lax.rem(l + o, lats)
        z.append(
            pltpu.make_async_remote_copy(
                src_ref=mine.at[to],
                dst_ref=others.at[o - 1],
                send_sem=z_send.at[o - 1],
                recv_sem=z_recv.at[o - 1],
                device_id=(d, to),
                device_id_type=MESH,
            )
        )
        z[-1].start()
    total = mine[l].astype(F32)
    for o in range(1, lats):
        z[o - 1].wait_recv()
        total = total + others[o - 1].astype(F32)
    out[...] = total
    for copy in z + sent:
        copy.wait_send()


def scatter(packed):
    dates, lats, rows, lanes = packed.shape
    slots = dates - 1
    return pl.pallas_call(
        functools.partial(scatter_kernel, dates, lats),
        in_specs=[pl.BlockSpec(memory_space=pltpu.VMEM)],
        out_specs=pl.BlockSpec(memory_space=pltpu.VMEM),
        out_shape=jax.ShapeDtypeStruct((rows, lanes), F32),
        scratch_shapes=[
            pltpu.VMEM((2, slots, lats // 2, rows, lanes), BF16),
            pltpu.VMEM((lats, rows, lanes), BF16),
            pltpu.VMEM((lats - 1, rows, lanes), BF16),
            pltpu.SemaphoreType.DMA((lats - 1,)),
            pltpu.SemaphoreType.DMA((lats - 1,)),
            pltpu.SemaphoreType.DMA((2, slots)),
            pltpu.SemaphoreType.DMA((2, slots)),
        ],
        compiler_params=pltpu.CompilerParams(
            collective_id=1, has_side_effects=True, vmem_limit_bytes=VMEM
        ),
        name="scatter_grads",
    )(packed)


def local(inputs, noise, cotangent, params, psi, step_counts, pixel_mask, offsets, bases):
    samples, steps, rows, width, _ = inputs.shape
    slabs = samples * steps
    dates, lats = lax.axis_size("date"), lax.axis_size("lat")
    lat = rows * lats

    def by_channel(values):
        return jnp.swapaxes(values, 3, 4).reshape(slabs, rows, -1, width)

    def padded(values):
        return jnp.pad(values, ((0, 0), (0, 0), (0, CP - values.shape[2]), (0, WIDE - width)))

    upward = [(i, i + 1) for i in range(lats - 1)]
    downward = [(i + 1, i) for i in range(lats - 1)]
    x = padded(jnp.concatenate([by_channel(inputs), by_channel(noise)], axis=2))
    below = lax.ppermute(x[:, rows - 1], "lat", upward)
    above = lax.ppermute(x[:, 0], "lat", downward)
    lines = params.shape[0] // LANES
    held = -(-lines // STEP) * STEP
    shard = jnp.pad(params.reshape(lines, LANES), ((0, held - lines), (0, 0)))
    gathered = gather(shard, dates, lats).reshape(dates * lats, held, LANES)
    w, wt, up, upt, dn, dnt, small = unpack(gathered, lines)
    cot = padded(by_channel(cotangent)).reshape(slabs * rows, CP, WIDE)
    active = jnp.arange(steps, dtype=jnp.int32)[None, :] < step_counts[:, None]
    mask = active.reshape(slabs, 1, 1) * pixel_mask[None]
    mask = jnp.pad(mask.astype(F32), ((0, 0), (0, 0), (0, WIDE - width)))
    basis = lift(offsets, bases, psi, below, x, above, small[0], small[1], lat, width)
    basis = basis.reshape(slabs * rows, BASIS * CP, WIDE)
    output, gconv, gup, gdn, second_sums = block(
        basis, x.reshape(slabs * rows, CP, WIDE), cot, mask.reshape(slabs * rows, 1, WIDE),
        wt, upt, up, dnt, dn, small[2], small[3], width,
    )
    gconv_rows = gconv.reshape(slabs, rows, CP, WIDE)
    own, to_below, to_above = lower(offsets, bases, psi, gconv_rows, w)
    from_below = lax.ppermute(to_above, "lat", upward)
    from_above = lax.ppermute(to_below, "lat", downward)
    gdisco = weight_grad(basis, gconv)
    grad, first_sums = input_grad(x, gconv_rows, own, from_below, from_above, small[0], width)
    sums = jnp.sum(jnp.concatenate([first_sums, second_sums]), axis=-1)
    valid = jnp.array([CIN, CIN, C, C], jnp.int32)[:, None]
    sums = jnp.where(jnp.arange(CP, dtype=jnp.int32)[None, :] < valid, sums, 0.0)
    sums = jnp.pad(sums, ((0, 0), (0, 8 * LANES - CP))).reshape(4, 8, LANES)
    packed = pack(gdisco, gup, gdn, sums, dates * lats, lines, held)
    summed = scatter(packed.reshape(dates, lats, held, LANES))

    def by_pixel(values):
        values = values.reshape(slabs, rows, CP, WIDE)[:, :, :C, :width]
        return jnp.swapaxes(values.reshape(samples, steps, rows, C, width), 3, 4)

    return by_pixel(output), by_pixel(grad), summed[:lines].reshape(-1)


def solution(mesh):
    field = P("date", None, "lat", None, None)
    flat = P(("date", "lat"))
    return jax.shard_map(
        local,
        mesh=mesh,
        in_specs=(field, field, field, flat, P(), P("date"), P("lat", None), P(), P()),
        out_specs=(field, field, flat),
        check_vma=False,
    )
```

time: 2010 us -> 556 us (0.28)
  other arithmetic: 774 us -> 1.56 us
  local copies, waits for them, and re-layouts: 669 us -> 31.4 us
  Pallas kernels: 0 us -> 474 us
  waiting for transfers between devices: 298 us -> 19.5 us
  matrix products: 138 us -> 0 us
  between operations: 97.7 us -> 1.73 us
    pallas_call x0 -> x9, Pallas kernels: none -> 474 us  [the longest x1 118 us: block(): pl.pallas_call(functools.partial(block_kernel, width), grid=(count,), in_...]
    reduce_sum x9 -> x1, other arithmetic: 273 us -> 0.49 us  [local(): sums = jnp.sum(jnp.concatenate([first_sums, second_sums]), axis=-1)]
    convert_element_type x13 -> x2, other arithmetic: 244 us -> 0.08 us  [the longest x1 0.07 us: local(): mask = jnp.pad(mask.astype(F32), ((0, 0), (0, 0), (0, WIDE - width)))]
    convert_element_type x17 -> x0, local copies, waits for them, and re-layouts: 243 us -> none  [the longest x12 165 us: forward_pass(): weighting[None, None, :, None, :, None] * window_part[:, :, :, :, None, :]]
    unnamed x3 -> x0, waiting for transfers between devices: 162 us -> none
    dot_general x9 -> x0, matrix products: 138 us -> none  [the longest x3 50.5 us: contract_cols(): lax.dot_general(left, right, (((1,), (1,)), ((), ())), preferred_element_...]
    concatenate x2 -> x1, other arithmetic: 135 us -> 0.92 us  [local(): x = padded(jnp.concatenate([by_channel(inputs), by_channel(noise)], axis=2))]
    reshape x10 -> x2, local copies, waits for them, and re-layouts: 130 us -> 2.41 us  [the longest x1 1.79 us: local(): return (by_pixel(output), by_pixel(grad), summed[:lines].reshape(-1))]
  transfers between devices with their start and end apart: 6 -> 4, of which waited for: 5 -> 2; matrix products, arithmetic and copies ran while one was open for 17% -> 3% of each run, Pallas kernels for 0% -> 23%
where the time goes in v1:
time: 556 us; the launch traced here: 546 us
  Pallas kernels  474 us (85%)
  local copies, waits for them, and re-layouts  31.4 us (6%)
  waiting for transfers between devices  19.5 us (4%)
  starting transfers between devices  17 us (3%)
    pallas_call x1, Pallas kernels, block(): pl.pallas_call(functools.partial(block_kernel, width), grid=(count,), in_...  118 us
    pallas_call x1, Pallas kernels, lift(): pl.pallas_call(functools.partial(lift_kernel, rows, lat, width), grid=(sl...  77.9 us
    pallas_call x1, Pallas kernels, gather(): pl.pallas_call(functools.partial(gather_kernel, dates, lats), in_specs=[p...  77.8 us
    pallas_call x1, Pallas kernels, lower(): pl.pallas_call(functools.partial(lower_kernel, rows), grid=(slabs,), in_s...  59.7 us
    pallas_call x1, Pallas kernels, scatter(): pl.pallas_call(functools.partial(scatter_kernel, dates, lats), in_specs=[...  53.4 us
    pallas_call x1, Pallas kernels, unpack(): pl.pallas_call(functools.partial(unpack_kernel, nrow, pad), out_shape=(ja...  24.5 us
    pallas_call x1, Pallas kernels, pack(): pl.pallas_call(functools.partial(pack_kernel, nrow, pad), out_shape=jax.S...  23.8 us
    pallas_call x1, Pallas kernels, weight_grad(): pl.pallas_call(outer_kernel, grid=(count,), in_specs=[pl.BlockSpec((1, BA...  22.1 us
  transfers between devices with their start and end apart: 4, of which 2 were waited for; matrix products, arithmetic and copies ran while one was open for 3% of the time, Pallas kernels for 23%

profile of v1, /device:TPU:4, one launch (start us, length us, event | category | flops | bytes accessed | tf_op | source)
XLA Modules:
  0.0 545.5 jit_solution(5185072146325842300)
XLA Ops:
  0.6 0.0 copy-start.6
  0.6 2.6 copy.25
  3.3 0.0 copy-done.6
  3.3 0.9 fusion.5.own.x
  4.2 0.0 copy-start
  4.2 0.0 copy-start.8
  4.2 0.0 copy-start.7
  4.3 2.4 slice_bitcast_fusion.1
  6.6 0.7 copy-done
  7.3 1.3 collective-permute-start.1
  8.6 5.9 %collective-permute-start = (bf16[2,656,768]{2,1,0:T(8,128)(2,1)}, bf16[2,656,768]{2,1,0:T(8,128)(2,1)}, u32[]{:S(2)}, u32[]{:S(2)}) collective-permute-start(bf16[2,656,768]{2,1,0:T(8,128)(2,1)} %get-tuple-element.41), channel_id=1, source_target_pairs={{0,1},{1,2},{2,3},{4,5},{5,6},{6,7},{8,9},{9,10},{10,11},{12,13},{... | collective-permute-start | bytes 6045704 | tf_op jit(solution)/shard_map/ppermute | solution.py:869
  15.2 0.0 copy-done.8
  15.2 0.7 copy.14.offsets
  15.9 0.0 copy-done.7
  15.9 0.1 multiply_convert_fusion
  16.0 0.0 copy-start.5
  16.0 0.6 reshape.78.mask
  16.6 2.6 copy.20
  19.2 0.0 copy-done.5
  19.2 0.7 pad.21.src
  19.9 2.3 pad.22.clone
  22.3 77.8 %gather_params.1 = bf16[8,4,816,128]{3,2,1,0:T(8,128)(2,1)} custom-call(bf16[816,128]{1,0:T(8,128)(2,1)} %pad.21.src), custom_call_target="tpu_custom_call" | custom-call | tf_op jit(solution)/shard_map/gather_params/pallas_call | solution.py:732
  100.1 24.5 %unpack.1 = (bf16[2624,768]{1,0:T(8,128)(2,1)}, bf16[656,2624]{1,0:T(8,128)(2,1)}, bf16[656,1408]{1,0:T(8,128)(2,1)}, bf16[1296,656]{1,0:T(8,128)(2,1)}, bf16[12...) custom-call(bf16[32,816,128]{2,1,0:T(8,128)(2,1)} %bitcast.55), custom_call_target="tpu_custom_call" | custom-call | tf_op jit(solution)/shard_map/unpack/pallas_call | solution.py:96
  124.6 2.4 slice_bitcast_fusion.4
  127.0 0.0 collective-permute-done.1.hi
  127.0 0.0 copy-start.2
  127.0 0.0 collective-permute-done.lo
  127.0 1.3 copy-done.2
  128.3 77.9 %lift.1 = bf16[2,2,2624,768]{3,2,1,0:T(8,128)(2,1)} custom-call(s32[12,2]{1,0:T(8,128)} %copy.14.offsets, s32[12]{0:T(128)} %bases.3, f32[8,12]{1,0:T(8,128)} %psi.3, bf16[2,656,768]{2,1,0:T(8,128)(2,1)} %collective-permute-done.lo, bf16[2,2,656,768]{3,2,1,0:T(8,128)(2,1)} %copy-done, bf16[2,656,768]{2,1,0:T(8,128)(2,1)} %copy-done.2, ...), custom_call_target="tpu_custom_call" | custom-call | tf_op jit(solution)/shard_map/lift/pallas_call | solution.py:305
  206.2 117.9 %block.1 = (bf16[4,656,768]{2,1,0:T(8,128)(2,1)}, bf16[4,656,768]{2,1,0:T(8,128)(2,1)}, f32[656,1408]{1,0:T(8,128)}, f32[1296,768]{1,0:T(8,128)}, f32[2,656,128]{2,1,0:T(8,128)}) custom-call(bf16[4,2624,768]{2,1,0:T(8,128)(2,1)} %bitcast.49, bf16[4,656,768]{2,1,0:T(8,128)(2,1)} %bitcast.51, bf16[4,656,768]{2,1,0:T(8,128)(2,1)} %bitcast.56, ...), custom_call_target="tpu_custom_call" | custom-call | tf_op jit(solution)/shard_map/block/pallas_call | solution.py:452
  324.1 59.7 %lower.1 = (f32[2,2,656,768]{3,2,1,0:T(8,128)}, bf16[2,656,768]{2,1,0:T(8,128)(2,1)}, bf16[2,656,768]{2,1,0:T(8,128)(2,1)}) custom-call(s32[12,2]{1,0:T(8,128)} %copy.14.offsets, s32[12]{0:T(128)} %bases.3, f32[8,12]{1,0:T(8,128)} %psi.3, bf16[2,2,656,768]{3,2,1,0:T(8,128)(2,1)} %bitcast.52, bf16[2624,768]{1,0:T(8,128)(2,1)} %get-tuple-element.28.w), custom_call_target="tpu_custom_call" | custom-call | tf_op jit(solution)/shard_map/lower/pallas_call | solution.py:553
  383.8 8.3 %collective-permute-start.2 = (bf16[2,656,768]{2,1,0:T(8,128)(2,1)}, bf16[2,656,768]{2,1,0:T(8,128)(2,1)}, u32[]{:S(2)}, u32[]{:S(2)}) collective-permute-start(bf16[2,656,768]{2,1,0:T(8,128)(2,1)} %get-tuple-element.30), channel_id=1, source_target_pairs={{0,1},{1,2},{2,3},{4,5},{5,6},{6,7},{8,9},{9,10},{10,11},{12,13},{... | collective-permute-start | bytes 6045704 | tf_op jit(solution)/shard_map/ppermute | solution.py:888
  392.1 0.0 copy-start.1
  392.1 1.5 collective-permute-start.3
  393.7 22.1 %weight_grad.1.gd_ref = f32[2624,768]{1,0:T(8,128)} custom-call(bf16[4,2624,768]{2,1,0:T(8,128)(2,1)} %bitcast.50, bf16[4,656,768]{2,1,0:T(8,128)(2,1)} %get-tuple-element.27.gconv), custom_call_target="tpu_custom_call" | custom-call | tf_op jit(solution)/shard_map/weight_grad/pallas_call | solution.py:488
  415.8 0.0 copy-done.1
  415.8 0.3 slice.39
  416.0 5.0 copy.26
  421.0 13.8 %collective-permute-done.2.lo = bf16[2,656,768]{2,1,0:T(8,128)(2,1)} collective-permute-done((bf16[2,656,768]{2,1,0:T(8,128)(2,1)}, bf16[2,656,768]{2,1,0:T(8,128)(2,1)}, u32[]{:S(2)}, u32[]{:S(2)}) %collective-permute-start.2) | collective-permute-done | bytes 2015264 | tf_op jit(solution)/shard_map/ppermute | solution.py:888
  434.8 5.7 %collective-permute-done.3.hi = bf16[2,656,768]{2,1,0:T(8,128)(2,1)} collective-permute-done((bf16[2,656,768]{2,1,0:T(8,128)(2,1)}, bf16[2,656,768]{2,1,0:T(8,128)(2,1)}, u32[]{:S(2)}, u32[]{:S(2)}) %collective-permute-start.3) | collective-permute-done | bytes 2015264 | tf_op jit(solution)/shard_map/ppermute | solution.py:889
  440.5 17.3 %input_grad.1 = (bf16[2,2,656,768]{3,2,1,0:T(8,128)(2,1)}, f32[2,656,128]{2,1,0:T(8,128)}) custom-call(bf16[2,2,656,768]{3,2,1,0:T(8,128)(2,1)} %copy-done, bf16[2,2,656,768]{3,2,1,0:T(8,128)(2,1)} %bitcast.53, f32[2,2,656,768]{3,2,1,0:T(8,128)} %get-tuple-element.29.own, bf16[2,656,768]{2,1,0:T(8,128)(2,1)} %collective-permute-done.2.lo, ...), custom_call_target="tpu_custom_call" | custom-call | tf_op jit(solution)/shard_map/input_grad/pallas_call | solution.py:619
  457.8 2.4 slice_bitcast_fusion
  460.2 0.0 copy-start.3
  460.2 0.0 copy-start.4
  460.2 0.0 copy-start.9
  460.2 5.0 copy.18
  465.2 0.0 copy-done.3
  465.2 0.0 copy-done.4
  465.2 0.5 maximum_reduce_fusion
  465.7 0.0 copy-done.9
  465.7 0.1 fusion.6
  465.8 0.6 copy.27
  466.4 23.8 %pack.1 = bf16[32,816,128]{2,1,0:T(8,128)(2,1)} custom-call(f32[2624,768]{1,0:T(8,128)} %weight_grad.1.gd_ref, f32[656,1408]{1,0:T(8,128)} %get-tuple-element.33.gu_ref, f32[1296,768]{1,0:T(8,128)} %get-tuple-element.34.gn_ref, f32[4,8,128]{2,1,0:T(8,128)} %bitcast.62), custom_call_target="tpu_custom_call" | custom-call | tf_op jit(solution)/shard_map/pack/pallas_call | solution.py:176
  490.1 53.4 %scatter_grads.1 = f32[816,128]{1,0:T(8,128)} custom-call(bf16[8,4,816,128]{3,2,1,0:T(8,128)(2,1)} %bitcast.54), custom_call_target="tpu_custom_call" | custom-call | tf_op jit(solution)/shard_map/scatter_grads/pallas_call | solution.py:833
  543.5 1.8 slice_bitcast_fusion.3
  (3 shorter events, 0.0 us)
Async XLA Ops:
  0.6 2.7 copy-start.6
  4.2 3.1 copy-start
  4.2 11.0 %copy-start.8 = (s32[12,2]{0,1:T(2,128)S(1)}, s32[12,2]{0,1:T(2,128)}, u32[]{:S(2)}) copy-start(s32[12,2]{0,1:T(2,128)} %param.17) | copy-start | bytes 292
  4.2 11.7 %copy-start.7 = (s32[2,720]{1,0:T(2,128)S(1)}, s32[2,720]{1,0:T(2,128)}, u32[]{:S(2)}) copy-start(s32[2,720]{1,0:T(2,128)} %param.16) | copy-start | bytes 17284
  7.3 119.7 %collective-permute-start.1 = (bf16[2,656,768]{2,1,0:T(8,128)(2,1)}, bf16[2,656,768]{2,1,0:T(8,128)(2,1)S(1)}, u32[]{:S(2)}, u32[]{:S(2)}) collective-permute-start(bf16[2,656,768]{2,1,0:T(8,128)(2,1)} %get-tuple-element.40), channel_id=1, source_target_pairs={{1,0},{2,1},{3,2},{5,4},{6,5},{7,6},{9,8},{10,9},{11,10},{13,12},{... | collective-permute-start | bytes 6045704 | tf_op jit(solution)/shard_map/ppermute | solution.py:870
  8.6 118.4 %collective-permute-start = (bf16[2,656,768]{2,1,0:T(8,128)(2,1)}, bf16[2,656,768]{2,1,0:T(8,128)(2,1)}, u32[]{:S(2)}, u32[]{:S(2)}) collective-permute-start(bf16[2,656,768]{2,1,0:T(8,128)(2,1)} %get-tuple-element.41), channel_id=1, source_target_pairs={{0,1},{1,2},{2,3},{4,5},{5,6},{6,7},{8,9},{9,10},{10,11},{12,13},{... | collective-permute-start | bytes 6045704 | tf_op jit(solution)/shard_map/ppermute | solution.py:869
  16.0 3.3 copy-start.5
  127.0 1.3 copy-start.2
  383.8 51.0 %collective-permute-start.2 = (bf16[2,656,768]{2,1,0:T(8,128)(2,1)}, bf16[2,656,768]{2,1,0:T(8,128)(2,1)}, u32[]{:S(2)}, u32[]{:S(2)}) collective-permute-start(bf16[2,656,768]{2,1,0:T(8,128)(2,1)} %get-tuple-element.30), channel_id=1, source_target_pairs={{0,1},{1,2},{2,3},{4,5},{5,6},{6,7},{8,9},{9,10},{10,11},{12,13},{... | collective-permute-start | bytes 6045704 | tf_op jit(solution)/shard_map/ppermute | solution.py:888
  392.1 23.7 %copy-start.1 = (bf16[4,656,768]{2,1,0:T(8,128)(2,1)S(1)}, bf16[4,656,768]{2,1,0:T(8,128)(2,1)}, u32[]{:S(2)}) copy-start(bf16[4,656,768]{2,1,0:T(8,128)(2,1)} %get-tuple-element.26) | copy-start | bytes 12091396
  392.1 48.4 %collective-permute-start.3 = (bf16[2,656,768]{2,1,0:T(8,128)(2,1)}, bf16[2,656,768]{2,1,0:T(8,128)(2,1)}, u32[]{:S(2)}, u32[]{:S(2)}) collective-permute-start(bf16[2,656,768]{2,1,0:T(8,128)(2,1)} %get-tuple-element.31), channel_id=1, source_target_pairs={{1,0},{2,1},{3,2},{5,4},{6,5},{7,6},{9,8},{10,9},{11,10},{13,12},{... | collective-permute-start | bytes 6045704 | tf_op jit(solution)/shard_map/ppermute | solution.py:889
  460.2 5.0 copy-start.3
  460.2 5.0 copy-start.4
  460.2 5.5 %copy-start.9 = (s32[4]{0:T(128)S(1)}, s32[4]{0:T(128)}, u32[]{:S(2)}) copy-start(s32[4]{0:T(128)} %constant.8.clone) | copy-start | bytes 52

commit v2 on v1

--- a/solution.py
+++ b/solution.py
@@ -22,7 +22,7 @@
 HP = 1296
 WIDE = 768
 HL = 1408
-UNROLL = 4
+UNROLL = 8
 VMEM = 60 << 20
 
 
@@ -269,7 +269,7 @@
             for d in range(-REACH, REACH + 1):
                 moved[m, d + REACH, at, :] = pltpu.roll(values, -d % WIDE, axis=1) if d else values
 
-        each_chunk(shifts, 1)
+        each_chunk(shifts, 4)
     for r in range(rows):
         for k in range(BASIS):
             parts = []
@@ -288,7 +288,7 @@
                 to = pl.ds(pl.multiple_of(k * CP + c * STEP, STEP), STEP)
                 out[0, r, to, :] = cut(total, width).astype(BF16)
 
-            each_chunk(combine, 1)
+            each_chunk(combine, 4)
         last = slice(BASIS * CP - STEP, BASIS * CP)
         bias_row = CIN - (CP - STEP)
         sub = lax.broadcasted_iota(jnp.int32, (STEP, WIDE), 0)
@@ -354,7 +354,7 @@
         res[at, :] = res[at, :] + jnp.where(keep, values, 0.0)
         gb[at, :] = (cot[0, at, :].astype(F32) * mask[0]).astype(BF16)
 
-    each_chunk(add_input, 1)
+    each_chunk(add_input, 8)
 
     def read(c):
         return res[pl.ds(pl.multiple_of(c * STEP, STEP), STEP), :]
@@ -366,7 +366,7 @@
         row = lax.broadcasted_iota(jnp.int32, (STEP, WIDE), 0) + c * STEP
         second[at, :] = jnp.where(row == C, 1.0, values).astype(BF16)
 
-    each_chunk(normalize, 1)
+    each_chunk(normalize, 8)
     pre[...] = dot(upt[...], second[...])
 
     def gelu(c, _):
@@ -381,13 +381,13 @@
         slope[at, :] = half + 0.5 * v * (1.0 - bend * bend) * rise
         return 0
 
-    lax.fori_loop(0, HP // STEP, gelu, 0)
+    lax.fori_loop(0, HP // STEP, gelu, 0, unroll=8)
     pre[:CP, :] = dot(dnt[...], act[...])
 
     def finish(c, at):
         out[0, at, :] = (res[at, :] + pre[at, :]).astype(BF16)
 
-    each_chunk(finish, 1)
+    each_chunk(finish, 8)
     pre[...] = dot(dn[:, :CP], gb[...])
 
     def back(c, _):
@@ -395,7 +395,7 @@
         gpre[at, :] = (pre[at, :] * slope[at, :]).astype(BF16)
         return 0
 
-    lax.fori_loop(0, HP // STEP, back, 0)
+    lax.fori_loop(0, HP // STEP, back, 0, unroll=8)
     gsec[...] = dot(up[:, :HP], gpre[...])
 
     def means(c):
@@ -416,7 +416,7 @@
         along_lanes(sums.at[0], at, dm * xhat)
         along_lanes(sums.at[1], at, dm)
 
-    each_chunk(backward, 1)
+    each_chunk(backward, 8)
 
     def outer(a, b):
         return lax.dot_general(a, b, (((1,), (1,)), ((), ())), preferred_element_type=F32)
@@ -532,7 +532,7 @@
                         term = weight * lifted[r, source, :].astype(F32)
                         part = term if part is None else part + term
                 if d:
-                    part = pltpu.roll(part, d % WIDE, axis=1)
+                    part = pltpu.roll(part.astype(BF16), d % WIDE, axis=1).astype(F32)
                 total = part if total is None else total + part
             if target < 0:
                 lo[0, at, :] = total.astype(BF16)
@@ -541,7 +541,7 @@
             else:
                 own[0, target, at, :] = total
 
-        each_chunk(gather, 1)
+        each_chunk(gather, 8)
 
 
 def lower(offsets, bases, psi, gconv, w):
@@ -591,7 +591,7 @@
         halo = lo[0, at, :].astype(F32) * from_below + hi[0, at, :].astype(F32) * from_above
         total[at, :] = own[0, 0, at, :] + halo
 
-    each_chunk(join, 1)
+    each_chunk(join, 4)
 
     def means(c):
         at = pl.ds(pl.multiple_of(c * STEP, STEP), STEP)
@@ -609,7 +609,7 @@
         along_lanes(sums.at[0], at, dm * xhat)
         along_lanes(sums.at[1], at, dm)
 
-    each_chunk(backward, 1)
+    each_chunk(backward, 8)
 
 
 def input_grad(x, gconv, own, lo, hi, gain, width):
@@ -656,6 +656,11 @@
     return bits + [0], bits[::-1] + [0]
 
 
+def pieces(rows):
+    cut = rows // (2 * STEP) * STEP
+    return pl.ds(0, cut), pl.ds(cut, rows - cut)
+
+
 def greet(dates, lats, d, l):
     barrier = pltpu.get_barrier_semaphore()
     count = 0
@@ -670,60 +675,61 @@
 
 def gather_kernel(dates, lats, src, out, local_sem, z_send, z_recv, send, recv):
     d, l = lax.axis_index("date"), lax.axis_index("lat")
-    half = lats // 2
+    steps = dates.bit_length() - 1
+    parts = pieces(src.shape[0])
     greet(dates, lats, d, l)
     own = pltpu.make_async_copy(src, out.at[d, l], local_sem)
     own.start()
-    z = []
-    for o in range(1, lats):
-        z.append(
-            pltpu.make_async_remote_copy(
-                src_ref=src,
-                dst_ref=out.at[d, l],
-                send_sem=z_send.at[o - 1],
-                recv_sem=z_recv.at[o - 1],
-                device_id=(d, lax.rem(l + o, lats)),
-                device_id_type=MESH,
-            )
+    sent, arriving, flights = [], {}, {}
+
+    def along(o):
+        copy = pltpu.make_async_remote_copy(
+            src_ref=src,
+            dst_ref=out.at[d, l],
+            send_sem=z_send.at[o - 1],
+            recv_sem=z_recv.at[o - 1],
+            device_id=(d, lax.rem(l + o, lats)),
+            device_id_type=MESH,
         )
-        z[-1].start()
-    own.wait()
-    for copy in z:
-        copy.wait_recv()
-    sent = []
-
-    def cross(h, i, mask):
-        order = orders(dates)[h]
-        at = span(order[:i]).index(mask)
-        block = out.at[flipped(d, mask), pl.ds(h * half, half)]
-        slot = (1 << i) - 1 + at
+        copy.start()
+        sent.append(copy)
+        arriving[o] = copy
+
+    def cross(o, p, i, n):
+        order = orders(dates)[p]
+        block = out.at[flipped(d, span(order[:i])[n]), lax.rem(l - o + lats, lats), parts[p]]
+        slot = (1 << i) - 1 + n
         copy = pltpu.make_async_remote_copy(
-            src_ref=block,
+            src_ref=src.at[parts[p]] if o == 0 and n == 0 else block,
             dst_ref=block,
-            send_sem=send.at[h, slot],
-            recv_sem=recv.at[h, slot],
+            send_sem=send.at[o, p, slot],
+            recv_sem=recv.at[o, p, slot],
             device_id=(flip(d, order[i]), l),
             device_id_type=MESH,
         )
         copy.start()
         sent.append(copy)
-        return copy
-
-    flights = {}
-    steps = dates.bit_length() - 1
-    for i in range(steps):
-        for h in range(2):
-            flights[h, i, 0] = cross(h, i, 0)
-    for i in range(steps):
-        for at, mask in enumerate(span(orders(dates)[0][:i])):
-            for h in range(2):
-                order = orders(dates)[h]
-                mask = span(order[:i])[at]
-                flights[h, i, mask].wait_recv()
-                for later in range(i + 1, steps):
-                    reached = mask | 1 << order[i]
-                    flights[h, later, reached] = cross(h, later, reached)
-    for copy in z + sent:
+        flights[o, p, i, n] = copy
+
+    for wave in range(lats + steps):
+        if wave < lats:
+            if wave:
+                arriving[wave].wait_recv()
+            if wave + 1 < lats:
+                along(wave + 1)
+            for i in range(steps):
+                for p in range(2):
+                    cross(wave, p, i, 0)
+        for i in range(steps)[::-1]:
+            o = wave - 1 - i
+            if 0 <= o < lats:
+                for n in range(1 << i):
+                    for p in range(2):
+                        flights[o, p, i, n].wait_recv()
+                        for later in range(i + 1, steps):
+                            cross(o, p, later, n + (1 << i))
+    own.wait()
+    for copy in sent:
         copy.wait_send()
 
 
@@ -738,92 +744,87 @@
             pltpu.SemaphoreType.DMA(()),
             pltpu.SemaphoreType.DMA((lats - 1,)),
             pltpu.SemaphoreType.DMA((lats - 1,)),
-            pltpu.SemaphoreType.DMA((2, slots)),
-            pltpu.SemaphoreType.DMA((2, slots)),
+            pltpu.SemaphoreType.DMA((lats, 2, slots)),
+            pltpu.SemaphoreType.DMA((lats, 2, slots)),
         ],
         compiler_params=pltpu.CompilerParams(collective_id=0, has_side_effects=True),
         name="gather_params",
     )(shard)
 
 
-def scatter_kernel(dates, lats, src, out, parts, mine, others, z_send, z_recv, send, recv):
+def scatter_kernel(dates, lats, src, out, sums, others, z_send, z_recv, send, recv):
     d, l = lax.axis_index("date"), lax.axis_index("lat")
-    half = lats // 2
+    steps = dates.bit_length() - 1
+    paths = [order[::-1] for order in orders(dates)]
+    parts = pieces(src.shape[2])
     greet(dates, lats, d, l)
-    steps = dates.bit_length() - 1
-    sent = []
-    paths = [order[::-1] for order in orders(dates)]
-
-    def slot_of(h, i, mask):
-        later = span(paths[h][i + 1 :][::-1])
-        first = sum(1 << (steps - 1 - e) for e in range(i))
-        return first + later.index(mask)
-
-    def holder(h, i, mask):
+    sent, flights, z = [], {}, {}
+
+    def left(p, i):
+        return span(paths[p][i + 1 :][::-1])[::-1]
+
+    def slot_of(i, n):
+        return sum(1 << (steps - 1 - e) for e in range(i)) + n
+
+    def held(o, p, i, mask):
         if i == 0:
-            return src.at[flipped(d, mask), pl.ds(h * half, half)]
-        return parts.at[h, slot_of(h, i - 1, mask)]
-
-    def cross(h, i, mask):
-        bit = paths[h][i]
-        slot = slot_of(h, i, mask)
+            return src.at[flipped(d, mask), lax.rem(l + o, lats), parts[p]]
+        return sums.at[o, slot_of(i - 1, left(p, i - 1).index(mask)), parts[p]]
+
+    def cross(o, p, i, n):
+        bit = paths[p][i]
+        slot = slot_of(i, n)
         copy = pltpu.make_async_remote_copy(
-            src_ref=holder(h, i, mask | 1 << bit),
-            dst_ref=parts.at[h, slot],
-            send_sem=send.at[h, slot],
-            recv_sem=recv.at[h, slot],
+            src_ref=held(o, p, i, left(p, i)[n] | 1 << bit),
+            dst_ref=sums.at[o, slot, parts[p]],
+            send_sem=send.at[o, p, slot],
+            recv_sem=recv.at[o, p, slot],
             device_id=(flip(d, bit), l),
             device_id_type=MESH,
         )
         copy.start()
         sent.append(copy)
-        return copy
-
-    def left(h, i):
-        masks = span(paths[h][i + 1 :][::-1])
-        return masks[::-1]
-
-    flights = {}
-    for n in range(len(left(0, 0))):
-        for h in range(2):
-            mask = left(h, 0)[n]
-            flights[h, 0, mask] = cross(h, 0, mask)
-    for i in range(steps):
-        for n in range(len(left(0, i))):
-            for h in range(2):
-                mask = left(h, i)[n]
-                flights[h, i, mask].wait_recv()
-                have = holder(h, i, mask)
-                got = parts.at[h, slot_of(h, i, mask)]
-                for s in range(half):
-                    total = have[s].astype(F32) + got[s].astype(F32)
-                    if i == steps - 1:
-                        mine[h * half + s] = total.astype(BF16)
-                    else:
-                        got[s] = total.astype(BF16)
-                if i + 1 < steps and mask >> paths[h][i + 1] & 1:
-                    ahead = mask & ~(1 << paths[h][i + 1])
-                    flights[h, i + 1, ahead] = cross(h, i + 1, ahead)
-    z = []
-    for o in range(1, lats):
-        to = lax.rem(l + o, lats)
-        z.append(
-            pltpu.make_async_remote_copy(
-                src_ref=mine.at[to],
-                dst_ref=others.at[o - 1],
-                send_sem=z_send.at[o - 1],
-                recv_sem=z_recv.at[o - 1],
-                device_id=(d, to),
+        flights[o, p, i, n] = copy
+
+    def add(o, p, i, n):
+        flights[o, p, i, n].wait_recv()
+        have = held(o, p, i, left(p, i)[n])
+        got = sums.at[o, slot_of(i, n), parts[p]]
+        got[...] = (have[...].astype(F32) + got[...].astype(F32)).astype(BF16)
+        if i + 1 < steps:
+            if n < len(left(p, i + 1)):
+                cross(o, p, i + 1, n)
+        elif o:
+            copy = pltpu.make_async_remote_copy(
+                src_ref=got,
+                dst_ref=others.at[o - 1, parts[p]],
+                send_sem=z_send.at[o - 1, p],
+                recv_sem=z_recv.at[o - 1, p],
+                device_id=(d, lax.rem(l + o, lats)),
                 device_id_type=MESH,
             )
-        )
-        z[-1].start()
-    total = mine[l].astype(F32)
-    for o in range(1, lats):
-        z[o - 1].wait_recv()
-        total = total + others[o - 1].astype(F32)
-    out[...] = total
-    for copy in z + sent:
+            copy.start()
+            sent.append(copy)
+            z[o, p] = copy
+
+    turns = list(range(1, lats)) + [0]
+    for o in turns:
+        for n in range(len(left(0, 0))):
+            for p in range(2):
+                cross(o, p, 0, n)
+    for wave in range(lats + steps - 1):
+        for i in range(steps):
+            if 0 <= wave - i < lats:
+                for n in range(len(left(0, i))):
+                    for p in range(2):
+                        add(turns[wave - i], p, i, n)
+    for p in range(2):
+        total = sums[0, slot_of(steps - 1, 0), parts[p]].astype(F32)
+        for o in range(1, lats):
+            z[o, p].wait_recv()
+            total = total + others[o - 1, parts[p]].astype(F32)
+        out[parts[p]] = total
+    for copy in sent:
         copy.wait_send()
 
 
@@ -836,13 +837,12 @@
         out_specs=pl.BlockSpec(memory_space=pltpu.VMEM),
         out_shape=jax.ShapeDtypeStruct((rows, lanes), F32),
         scratch_shapes=[
-            pltpu.VMEM((2, slots, lats // 2, rows, lanes), BF16),
-            pltpu.VMEM((lats, rows, lanes), BF16),
+            pltpu.VMEM((lats, slots, rows, lanes), BF16),
             pltpu.VMEM((lats - 1, rows, lanes), BF16),
-            pltpu.SemaphoreType.DMA((lats - 1,)),
-            pltpu.SemaphoreType.DMA((lats - 1,)),
-            pltpu.SemaphoreType.DMA((2, slots)),
-            pltpu.SemaphoreType.DMA((2, slots)),
+            pltpu.SemaphoreType.DMA((lats - 1, 2)),
+            pltpu.SemaphoreType.DMA((lats - 1, 2)),
+            pltpu.SemaphoreType.DMA((lats, 2, slots)),
+            pltpu.SemaphoreType.DMA((lats, 2, slots)),
         ],
         compiler_params=pltpu.CompilerParams(
             collective_id=1, has_side_effects=True, vmem_limit_bytes=VMEM

time: 556 us -> 455 us (0.82)
  Pallas kernels: 474 us -> 381 us
  starting transfers between devices: 17 us -> 11.4 us
    pallas_call x1, Pallas kernels: 77.9 us -> 40.4 us  [lift(): pl.pallas_call(functools.partial(lift_kernel, rows, lat, width), grid=(sl...]
    pallas_call x1, Pallas kernels: 59.7 us -> 34.8 us  [lower(): pl.pallas_call(functools.partial(lower_kernel, rows), grid=(slabs,), in_s...]
    pallas_call x1, Pallas kernels: 118 us -> 103 us  [block(): pl.pallas_call(functools.partial(block_kernel, width), grid=(count,), in_...]
    pallas_call x1, Pallas kernels: 53.4 us -> 44 us  [scatter(): pl.pallas_call(functools.partial(scatter_kernel, dates, lats), in_specs=[...]
    pallas_call x1, Pallas kernels: 77.8 us -> 71.7 us  [gather(): pl.pallas_call(functools.partial(gather_kernel, dates, lats), in_specs=[p...]
    ppermute x1, starting transfers between devices: 8.27 us -> 2.62 us  [local(): from_below = lax.ppermute(to_above, 'lat', upward)]
  transfers between devices with their start and end apart: 4 -> 4, of which waited for: 2 -> 2; matrix products, arithmetic and copies ran while one was open for 3% -> 3% of each run, Pallas kernels for 23% -> 27%
where the time goes in v2:
time: 455 us; the launch traced here: 446 us
  Pallas kernels  381 us (84%)
  local copies, waits for them, and re-layouts  31.4 us (7%)
  waiting for transfers between devices  19.8 us (4%)
  starting transfers between devices  11.4 us (3%)
    pallas_call x1, Pallas kernels, block(): pl.pallas_call(functools.partial(block_kernel, width), grid=(count,), in_...  103 us
    pallas_call x1, Pallas kernels, gather(): pl.pallas_call(functools.partial(gather_kernel, dates, lats), in_specs=[p...  71.7 us
    pallas_call x1, Pallas kernels, scatter(): pl.pallas_call(functools.partial(scatter_kernel, dates, lats), in_specs=[...  44 us
    pallas_call x1, Pallas kernels, lift(): pl.pallas_call(functools.partial(lift_kernel, rows, lat, width), grid=(sl...  40.4 us
    pallas_call x1, Pallas kernels, lower(): pl.pallas_call(functools.partial(lower_kernel, rows), grid=(slabs,), in_s...  34.8 us
    pallas_call x1, Pallas kernels, unpack(): pl.pallas_call(functools.partial(unpack_kernel, nrow, pad), out_shape=(ja...  24.5 us
    pallas_call x1, Pallas kernels, pack(): pl.pallas_call(functools.partial(pack_kernel, nrow, pad), out_shape=jax.S...  23.8 us
    pallas_call x1, Pallas kernels, weight_grad(): pl.pallas_call(outer_kernel, grid=(count,), in_specs=[pl.BlockSpec((1, BA...  22.1 us
  transfers between devices with their start and end apart: 4, of which 2 were waited for; matrix products, arithmetic and copies ran while one was open for 3% of the time, Pallas kernels for 27%

profile of v2, /device:TPU:4, one launch (start us, length us, event | category | flops | bytes accessed | tf_op | source)
XLA Modules:
  0.0 446.4 jit_solution(7037030728375162504)
XLA Ops:
  0.6 0.0 copy-start.6
  0.6 2.6 copy.25
  3.3 0.0 copy-done.6
  3.3 0.9 fusion.5.own.x
  4.2 0.0 copy-start
  4.2 0.0 copy-start.8
  4.2 0.0 copy-start.7
  4.3 2.4 slice_bitcast_fusion.1
  6.6 0.7 copy-done
  7.3 1.3 collective-permute-start.1
  8.6 5.9 %collective-permute-start = (bf16[2,656,768]{2,1,0:T(8,128)(2,1)}, bf16[2,656,768]{2,1,0:T(8,128)(2,1)}, u32[]{:S(2)}, u32[]{:S(2)}) collective-permute-start(bf16[2,656,768]{2,1,0:T(8,128)(2,1)} %get-tuple-element.41), channel_id=1, source_target_pairs={{0,1},{1,2},{2,3},{4,5},{5,6},{6,7},{8,9},{9,10},{10,11},{12,13},{... | collective-permute-start | bytes 6045704 | tf_op jit(solution)/shard_map/ppermute | solution.py:869
  15.2 0.0 copy-done.8
  15.2 0.7 copy.14.offsets
  15.9 0.0 copy-done.7
  15.9 0.1 multiply_convert_fusion
  16.0 0.0 copy-start.5
  16.0 0.6 reshape.78.mask
  16.6 2.6 copy.20
  19.2 0.0 copy-done.5
  19.2 0.7 pad.21.src
  19.9 2.3 pad.22.clone
  22.3 71.7 %gather_params.1 = bf16[8,4,816,128]{3,2,1,0:T(8,128)(2,1)} custom-call(bf16[816,128]{1,0:T(8,128)(2,1)} %pad.21.src), custom_call_target="tpu_custom_call" | custom-call | tf_op jit(solution)/shard_map/gather_params/pallas_call | solution.py:738
  94.0 24.5 %unpack.1 = (bf16[2624,768]{1,0:T(8,128)(2,1)}, bf16[656,2624]{1,0:T(8,128)(2,1)}, bf16[656,1408]{1,0:T(8,128)(2,1)}, bf16[1296,656]{1,0:T(8,128)(2,1)}, bf16[12...) custom-call(bf16[32,816,128]{2,1,0:T(8,128)(2,1)} %bitcast.55), custom_call_target="tpu_custom_call" | custom-call | tf_op jit(solution)/shard_map/unpack/pallas_call | solution.py:96
  118.6 2.4 slice_bitcast_fusion.4
  120.9 0.0 collective-permute-done.1.hi
  120.9 0.0 copy-start.2
  120.9 0.0 collective-permute-done.lo
  121.0 1.3 copy-done.2
  122.2 40.4 %lift.1 = bf16[2,2,2624,768]{3,2,1,0:T(8,128)(2,1)} custom-call(s32[12,2]{1,0:T(8,128)} %copy.14.offsets, s32[12]{0:T(128)} %bases.3, f32[8,12]{1,0:T(8,128)} %psi.3, bf16[2,656,768]{2,1,0:T(8,128)(2,1)} %collective-permute-done.lo, bf16[2,2,656,768]{3,2,1,0:T(8,128)(2,1)} %copy-done, bf16[2,656,768]{2,1,0:T(8,128)(2,1)} %copy-done.2, ...), custom_call_target="tpu_custom_call" | custom-call | tf_op jit(solution)/shard_map/lift/pallas_call | solution.py:305
  162.6 102.9 %block.1 = (bf16[4,656,768]{2,1,0:T(8,128)(2,1)}, bf16[4,656,768]{2,1,0:T(8,128)(2,1)}, f32[656,1408]{1,0:T(8,128)}, f32[1296,768]{1,0:T(8,128)}, f32[2,656,128]{2,1,0:T(8,128)}) custom-call(bf16[4,2624,768]{2,1,0:T(8,128)(2,1)} %bitcast.49, bf16[4,656,768]{2,1,0:T(8,128)(2,1)} %bitcast.51, bf16[4,656,768]{2,1,0:T(8,128)(2,1)} %bitcast.56, ...), custom_call_target="tpu_custom_call" | custom-call | tf_op jit(solution)/shard_map/block/pallas_call | solution.py:452
  265.5 34.8 %lower.1 = (f32[2,2,656,768]{3,2,1,0:T(8,128)}, bf16[2,656,768]{2,1,0:T(8,128)(2,1)}, bf16[2,656,768]{2,1,0:T(8,128)(2,1)}) custom-call(s32[12,2]{1,0:T(8,128)} %copy.14.offsets, s32[12]{0:T(128)} %bases.3, f32[8,12]{1,0:T(8,128)} %psi.3, bf16[2,2,656,768]{3,2,1,0:T(8,128)(2,1)} %bitcast.52, bf16[2624,768]{1,0:T(8,128)(2,1)} %get-tuple-element.28.w), custom_call_target="tpu_custom_call" | custom-call | tf_op jit(solution)/shard_map/lower/pallas_call | solution.py:553
  300.4 2.6 collective-permute-start.2
  303.0 0.0 copy-start.1
  303.0 1.5 collective-permute-start.3
  304.6 22.1 %weight_grad.1.gd_ref = f32[2624,768]{1,0:T(8,128)} custom-call(bf16[4,2624,768]{2,1,0:T(8,128)(2,1)} %bitcast.50, bf16[4,656,768]{2,1,0:T(8,128)(2,1)} %get-tuple-element.27.gconv), custom_call_target="tpu_custom_call" | custom-call | tf_op jit(solution)/shard_map/weight_grad/pallas_call | solution.py:488
  326.7 0.0 copy-done.1
  326.7 0.3 slice.39
  326.9 5.0 %copy.26 = bf16[2,2,641,720]{3,1,2,0:T(2,128)(2,1)} copy(bf16[2,2,641,720]{3,2,1,0:T(8,128)(2,1)S(1)} %slice.39) | data formatting | bytes 7384320
  331.9 14.1 %collective-permute-done.2.lo = bf16[2,656,768]{2,1,0:T(8,128)(2,1)} collective-permute-done((bf16[2,656,768]{2,1,0:T(8,128)(2,1)}, bf16[2,656,768]{2,1,0:T(8,128)(2,1)}, u32[]{:S(2)}, u32[]{:S(2)}) %collective-permute-start.2) | collective-permute-done | bytes 2015264 | tf_op jit(solution)/shard_map/ppermute | solution.py:888
  346.0 5.7 %collective-permute-done.3.hi = bf16[2,656,768]{2,1,0:T(8,128)(2,1)} collective-permute-done((bf16[2,656,768]{2,1,0:T(8,128)(2,1)}, bf16[2,656,768]{2,1,0:T(8,128)(2,1)}, u32[]{:S(2)}, u32[]{:S(2)}) %collective-permute-start.3) | collective-permute-done | bytes 2015264 | tf_op jit(solution)/shard_map/ppermute | solution.py:889
  351.7 16.2 %input_grad.1 = (bf16[2,2,656,768]{3,2,1,0:T(8,128)(2,1)}, f32[2,656,128]{2,1,0:T(8,128)}) custom-call(bf16[2,2,656,768]{3,2,1,0:T(8,128)(2,1)} %copy-done, bf16[2,2,656,768]{3,2,1,0:T(8,128)(2,1)} %bitcast.53, f32[2,2,656,768]{3,2,1,0:T(8,128)} %get-tuple-element.29.own, bf16[2,656,768]{2,1,0:T(8,128)(2,1)} %collective-permute-done.2.lo, ...), custom_call_target="tpu_custom_call" | custom-call | tf_op jit(solution)/shard_map/input_grad/pallas_call | solution.py:619
  368.0 2.4 slice_bitcast_fusion
  370.4 0.0 copy-start.3
  370.4 0.0 copy-start.4
  370.4 0.0 copy-start.9
  370.4 5.0 %copy.18 = bf16[1,2,2,720,641]{3,2,4,1,0:T(2,128)(2,1)} copy(bf16[1,2,2,720,641]{3,4,2,1,0:T(8,128)(2,1)S(1)} %slice_bitcast_fusion) | data formatting | bytes 7384320
  375.4 0.0 copy-done.3
  375.4 0.0 copy-done.4
  375.4 0.5 maximum_reduce_fusion
  375.9 0.0 copy-done.9
  375.9 0.1 fusion.6
  375.9 0.6 copy.27
  376.6 23.8 %pack.1 = bf16[32,816,128]{2,1,0:T(8,128)(2,1)} custom-call(f32[2624,768]{1,0:T(8,128)} %weight_grad.1.gd_ref, f32[656,1408]{1,0:T(8,128)} %get-tuple-element.33.gu_ref, f32[1296,768]{1,0:T(8,128)} %get-tuple-element.34.gn_ref, f32[4,8,128]{2,1,0:T(8,128)} %bitcast.62), custom_call_target="tpu_custom_call" | custom-call | tf_op jit(solution)/shard_map/pack/pallas_call | solution.py:176
  400.3 44.0 %scatter_grads.1 = f32[816,128]{1,0:T(8,128)} custom-call(bf16[8,4,816,128]{3,2,1,0:T(8,128)(2,1)} %bitcast.54), custom_call_target="tpu_custom_call" | custom-call | tf_op jit(solution)/shard_map/scatter_grads/pallas_call | solution.py:834
  444.3 1.8 slice_bitcast_fusion.3
  (3 shorter events, 0.0 us)
Async XLA Ops:
  0.6 2.7 copy-start.6
  4.2 3.1 copy-start
  4.2 11.0 %copy-start.8 = (s32[12,2]{0,1:T(2,128)S(1)}, s32[12,2]{0,1:T(2,128)}, u32[]{:S(2)}) copy-start(s32[12,2]{0,1:T(2,128)} %param.17) | copy-start | bytes 292
  4.2 11.7 %copy-start.7 = (s32[2,720]{1,0:T(2,128)S(1)}, s32[2,720]{1,0:T(2,128)}, u32[]{:S(2)}) copy-start(s32[2,720]{1,0:T(2,128)} %param.16) | copy-start | bytes 17284
  7.3 113.6 %collective-permute-start.1 = (bf16[2,656,768]{2,1,0:T(8,128)(2,1)}, bf16[2,656,768]{2,1,0:T(8,128)(2,1)S(1)}, u32[]{:S(2)}, u32[]{:S(2)}) collective-permute-start(bf16[2,656,768]{2,1,0:T(8,128)(2,1)} %get-tuple-element.40), channel_id=1, source_target_pairs={{1,0},{2,1},{3,2},{5,4},{6,5},{7,6},{9,8},{10,9},{11,10},{13,12},{... | collective-permute-start | bytes 6045704 | tf_op jit(solution)/shard_map/ppermute | solution.py:870
  8.6 112.3 %collective-permute-start = (bf16[2,656,768]{2,1,0:T(8,128)(2,1)}, bf16[2,656,768]{2,1,0:T(8,128)(2,1)}, u32[]{:S(2)}, u32[]{:S(2)}) collective-permute-start(bf16[2,656,768]{2,1,0:T(8,128)(2,1)} %get-tuple-element.41), channel_id=1, source_target_pairs={{0,1},{1,2},{2,3},{4,5},{5,6},{6,7},{8,9},{9,10},{10,11},{12,13},{... | collective-permute-start | bytes 6045704 | tf_op jit(solution)/shard_map/ppermute | solution.py:869
  16.0 3.3 copy-start.5
  120.9 1.3 copy-start.2
  300.4 45.6 %collective-permute-start.2 = (bf16[2,656,768]{2,1,0:T(8,128)(2,1)}, bf16[2,656,768]{2,1,0:T(8,128)(2,1)}, u32[]{:S(2)}, u32[]{:S(2)}) collective-permute-start(bf16[2,656,768]{2,1,0:T(8,128)(2,1)} %get-tuple-element.30), channel_id=1, source_target_pairs={{0,1},{1,2},{2,3},{4,5},{5,6},{6,7},{8,9},{9,10},{10,11},{12,13},{... | collective-permute-start | bytes 6045704 | tf_op jit(solution)/shard_map/ppermute | solution.py:888
  303.0 23.7 %copy-start.1 = (bf16[4,656,768]{2,1,0:T(8,128)(2,1)S(1)}, bf16[4,656,768]{2,1,0:T(8,128)(2,1)}, u32[]{:S(2)}) copy-start(bf16[4,656,768]{2,1,0:T(8,128)(2,1)} %get-tuple-element.26) | copy-start | bytes 12091396
  303.0 48.7 %collective-permute-start.3 = (bf16[2,656,768]{2,1,0:T(8,128)(2,1)}, bf16[2,656,768]{2,1,0:T(8,128)(2,1)}, u32[]{:S(2)}, u32[]{:S(2)}) collective-permute-start(bf16[2,656,768]{2,1,0:T(8,128)(2,1)} %get-tuple-element.31), channel_id=1, source_target_pairs={{1,0},{2,1},{3,2},{5,4},{6,5},{7,6},{9,8},{10,9},{11,10},{13,12},{... | collective-permute-start | bytes 6045704 | tf_op jit(solution)/shard_map/ppermute | solution.py:889
  370.4 5.0 %copy-start.3 = (f32[2,656,128]{2,1,0:T(8,128)S(1)}, f32[2,656,128]{2,1,0:T(8,128)}, u32[]{:S(2)}) copy-start(f32[2,656,128]{2,1,0:T(8,128)} %get-tuple-element.36) | copy-start | bytes 2015236
  370.4 5.0 %copy-start.4 = (f32[2,656,128]{2,1,0:T(8,128)S(1)}, f32[2,656,128]{2,1,0:T(8,128)}, u32[]{:S(2)}) copy-start(f32[2,656,128]{2,1,0:T(8,128)} %get-tuple-element.35) | copy-start | bytes 2015236
  370.4 5.5 %copy-start.9 = (s32[4]{0:T(128)S(1)}, s32[4]{0:T(128)}, u32[]{:S(2)}) copy-start(s32[4]{0:T(128)} %constant.8.clone) | copy-start | bytes 52

commit v3 on v2

--- a/solution.py
+++ b/solution.py
@@ -34,7 +34,7 @@
 def place(base,cols,period,b):
     start=base+cols*b
     return start//LANES, start%LANES
-def unpack_kernel(nrow,pad, g_ref, w_ref,wt_ref,up_ref,upt_ref,dn_ref,dnt_ref,small_ref,flat,chunks):
+def unpack_kernel(nrow,pad, g_ref, w_ref,wt_ref,up_ref,upt_ref,dn_ref,dnt_ref,flat,chunks):
     def fill(s,_):
         flat[pl.ds(nrow*s,pad),:]=g_ref[s].astype(F32); return 0
     lax.fori_loop(0,g_ref.shape[0],fill,0)
@@ -81,25 +81,15 @@
     wt_ref[...]=w_ref[:,:CP].T
     upt_ref[...]=up_ref[:,:HP].T
     dnt_ref[...]=dn_ref[:,:CP].T
-    for i,(off,n) in enumerate(SMALL):
-        row,s=divmod(off,LANES)
-        r=pltpu.roll(flat[row:row+8,:],(LANES-s)%LANES,axis=1)
-        v=jnp.where(lane<LANES-s,r,pltpu.roll(r,7,axis=0))
-        sub=lax.broadcasted_iota(jnp.int32,(8,LANES),0)
-        v=jnp.where(sub*LANES+lane<n,v,0.0)
-        t=v.T
-        for j in range(6):
-            rows=min(LANES,CP-j*LANES)
-            small_ref[i,j*LANES:j*LANES+rows,:]=jnp.broadcast_to(t[:rows,j:j+1],(rows,LANES))
 def unpack(gathered,nrow):
     n,pad,_=gathered.shape
     return pl.pallas_call(functools.partial(unpack_kernel,nrow,pad),
         out_shape=(jax.ShapeDtypeStruct((BASIS*CP,WIDE),BF16),jax.ShapeDtypeStruct((CP,BASIS*CP),BF16),
             jax.ShapeDtypeStruct((CP,HL),BF16),jax.ShapeDtypeStruct((HP,CP),BF16),
-            jax.ShapeDtypeStruct((HP,WIDE),BF16),jax.ShapeDtypeStruct((CP,HP),BF16),jax.ShapeDtypeStruct((4,CP,LANES),F32)),
+            jax.ShapeDtypeStruct((HP,WIDE),BF16),jax.ShapeDtypeStruct((CP,HP),BF16)),
         scratch_shapes=[pltpu.VMEM((F_ROWS,LANES),F32),pltpu.VMEM((6*(136*24+8),LANES),F32)],
         compiler_params=pltpu.CompilerParams(vmem_limit_bytes=VMEM),name="unpack")(gathered)
-def pack_kernel(nrow,pad,gd_ref,gu_ref,gn_ref,sm_ref,out_ref,flat,chunks):
+def pack_kernel(nrow,pad,gd_ref,gu_ref,gn_ref,out_ref,flat,chunks):
     lane=lane_ids(); sub=lax.broadcasted_iota(jnp.int32,(8,LANES),0)
     def gather(src,src_row,dst_row,rows,J,height,last,period):
         full=rows//8
@@ -163,20 +153,14 @@
     gather(gn_ref,0,0,HID+1,6,h,1,128)
     clear(6,h,1288,128)
     merge(OFF_DN,C,128,2)
-    for i,(off,n) in enumerate(SMALL):
-        row,s=divmod(off,LANES)
-        r=pltpu.roll(sm_ref[i],s,axis=1)
-        prev=pltpu.roll(r,1,axis=0)
-        v=jnp.where(lane>=s,r,jnp.where(sub==0,0.0,prev))
-        flat[row:row+8,:]=flat[row:row+8,:]+v
     def store(s,_):
         out_ref[s]=flat[pl.ds(nrow*s,pad),:].astype(BF16); return 0
     lax.fori_loop(0,out_ref.shape[0],store,0)
-def pack(gd,gu,gn,sm,n,nrow,pad):
+def pack(gd,gu,gn,n,nrow,pad):
     return pl.pallas_call(functools.partial(pack_kernel,nrow,pad),
         out_shape=jax.ShapeDtypeStruct((n,pad,LANES),BF16),
         scratch_shapes=[pltpu.VMEM((F_ROWS,LANES),F32),pltpu.VMEM((6*(136*24+8),LANES),F32)],
-        compiler_params=pltpu.CompilerParams(vmem_limit_bytes=VMEM),name="pack")(gd,gu,gn,sm)
+        compiler_params=pltpu.CompilerParams(vmem_limit_bytes=VMEM),name="pack")(gd,gu,gn)
 
 
 def tiled(column):
@@ -245,8 +229,31 @@
     lax.fori_loop(0, CP // STEP, step, 0, unroll=unroll)
 
 
-def lift_kernel(rows, lat, width, offsets, bases, psi, lo, own, hi, gain, shift, out, moved, table):
+def spread(source, gain, shift, width, moved):
+    def read(c):
+        return source[pl.ds(pl.multiple_of(c * STEP, STEP), STEP), :].astype(F32)
+
+    mean, scale = norm_stats(read, CIN)
+
+    def shifts(c, at):
+        values = (read(c) - mean) * scale * tiled(gain[at, :]) + tiled(shift[at, :])
+        values = wrapped(values, width).astype(BF16)
+        for d in range(-REACH, REACH + 1):
+            moved[d + REACH, at, :] = pltpu.roll(values, -d % WIDE, axis=1) if d else values
+
+    each_chunk(shifts, 4)
+
+
+def lift_kernel(
+    rows, slab, lat, width, offsets, bases, psi, lo, hi, own, gain, shift, *refs
+):
+    out, moved, table, sems = refs[-4:]
     first_row = lax.axis_index("lat") * rows
+    copies = [
+        pltpu.make_async_copy(own.at[slab, r], moved.at[r + 1], sems.at[r]) for r in range(rows)
+    ]
+    for copy in copies:
+        copy.start()
     for k in range(BASIS):
         table[SUPPORT + k] = 0
     for p in range(SUPPORT):
@@ -254,22 +261,10 @@
         used = table[SUPPORT + k]
         table[k * 3 + used] = p
         table[SUPPORT + k] = used + 1
-    for m in range(rows + 2):
-        source = lo if m == 0 else hi if m == rows + 1 else own.at[:, m - 1]
-
-        def read(c):
-            return source[0, pl.ds(pl.multiple_of(c * STEP, STEP), STEP), :].astype(F32)
-
-        mean, scale = norm_stats(read, CIN)
-
-        def shifts(c, at):
-            values = (source[0, at, :].astype(F32) - mean) * scale
-            values = values * tiled(gain[at, :]) + tiled(shift[at, :])
-            values = wrapped(values, width).astype(BF16)
-            for d in range(-REACH, REACH + 1):
-                moved[m, d + REACH, at, :] = pltpu.roll(values, -d % WIDE, axis=1) if d else values
-
-        each_chunk(shifts, 4)
+    for source, m in ((lo, 0), (hi, rows + 1)):
+        spread(source.at[0], gain, shift, width, moved.at[m])
+    for copy in copies:
+        copy.wait()
     for r in range(rows):
         for k in range(BASIS):
             parts = []
@@ -297,33 +292,28 @@
         out[0, r, last, :] = jnp.where(sub == bias_row, ones, out[0, r, last, :].astype(F32)).astype(BF16)
 
 
-def lift(offsets, bases, psi, lo, own, hi, gain, shift, lat, width):
+def lift(offsets, bases, psi, lo, hi, own, gain, shift, before, slab, lat, width):
     slabs, rows = own.shape[:2]
     smem = pl.BlockSpec(memory_space=pltpu.SMEM)
-    halo = pl.BlockSpec((1, CP, WIDE), lambda s: (s, 0, 0))
+    anywhere = pl.BlockSpec(memory_space=pl.ANY)
+    halo = pl.BlockSpec((1, CP, WIDE), lambda s: (0, 0, 0))
     column = pl.BlockSpec((CP, LANES), lambda s: (0, 0))
     return pl.pallas_call(
-        functools.partial(lift_kernel, rows, lat, width),
-        grid=(slabs,),
-        in_specs=[
-            smem,
-            smem,
-            smem,
-            halo,
-            pl.BlockSpec((1, rows, CP, WIDE), lambda s: (s, 0, 0, 0)),
-            halo,
-            column,
-            column,
-        ],
-        out_specs=pl.BlockSpec((1, rows, BASIS * CP, WIDE), lambda s: (s, 0, 0, 0)),
+        functools.partial(lift_kernel, rows, slab, lat, width),
+        grid=(1,),
+        in_specs=[smem, smem, smem, halo, halo, anywhere, column, column] + [anywhere] * len(before),
+        out_specs=pl.BlockSpec((1, rows, BASIS * CP, WIDE), lambda s: (slab, 0, 0, 0)),
         out_shape=jax.ShapeDtypeStruct((slabs, rows, BASIS * CP, WIDE), BF16),
         scratch_shapes=[
             pltpu.VMEM((rows + 2, 2 * REACH + 1, CP, WIDE), BF16),
             pltpu.SMEM((SUPPORT + BASIS,), jnp.int32),
+            pltpu.SemaphoreType.DMA((rows,)),
         ],
+        input_output_aliases={8: 0} if before else {},
         compiler_params=pltpu.CompilerParams(vmem_limit_bytes=VMEM),
+        cost_estimate=pl.CostEstimate(flops=40 << 20, bytes_accessed=40 << 20, transcendentals=0),
         name="lift",
-    )(offsets, bases, psi, lo, own, hi, gain, shift)
+    )(offsets, bases, psi, lo, hi, own, gain, shift, *before)
 
 
 GELU_A = math.sqrt(2.0 / math.pi)
@@ -673,7 +663,79 @@
     pl.semaphore_wait(barrier, count)
 
 
-def gather_kernel(dates, lats, src, out, local_sem, z_send, z_recv, send, recv):
+def norms_kernel(dates, lats, owner, first, src, out, landed, local_sem, send, recv):
+    d, l = lax.axis_index("date"), lax.axis_index("lat")
+    mine = jnp.logical_and(d == owner[0], l == owner[1])
+    barrier = pltpu.get_barrier_semaphore()
+    others = [(a, b) for a in range(dates) for b in range(lats) if (a, b) != owner]
+
+    def copy_to(n):
+        return pltpu.make_async_remote_copy(
+            src_ref=src,
+            dst_ref=landed,
+            send_sem=send.at[n],
+            recv_sem=recv,
+            device_id=others[n],
+            device_id_type=MESH,
+        )
+
+    @pl.when(mine)
+    def _():
+        pl.semaphore_wait(barrier, len(others))
+        copies = [copy_to(n) for n in range(len(others))]
+        for copy in copies:
+            copy.start()
+        own = pltpu.make_async_copy(src, landed, local_sem)
+        own.start()
+        own.wait()
+        for copy in copies:
+            copy.wait_send()
+
+    @pl.when(jnp.logical_not(mine))
+    def _():
+        pl.semaphore_signal(barrier, inc=1, device_id=owner, device_id_type=MESH)
+        copy_to(0).wait_recv()
+
+    lane = lane_ids()
+    sub = lax.broadcasted_iota(jnp.int32, (8, LANES), 0)
+    lines = landed[...].astype(F32)
+    for i, (off, n) in enumerate(SMALL):
+        row, s = divmod(off - first * LANES, LANES)
+        r = pltpu.roll(lines[row : row + 8], (LANES - s) % LANES, axis=1)
+        v = jnp.where(lane < LANES - s, r, pltpu.roll(r, 7, axis=0))
+        t = jnp.where(sub * LANES + lane < n, v, 0.0).T
+        for j in range(6):
+            rows = min(LANES, CP - j * LANES)
+            out[i, j * LANES : j * LANES + rows, :] = jnp.broadcast_to(t[:rows, j : j + 1], (rows, LANES))
+
+
+def norms(shard, lines, dates, lats):
+    start, end = OFF_G1 // LANES, (OFF_UP - 1) // LANES + 3
+    owner = start // lines
+    row = (start - owner * lines) // STEP * STEP
+    count = -(-(end - owner * lines - row) // STEP) * STEP
+    assert row + count <= shard.shape[0]
+    return pl.pallas_call(
+        functools.partial(norms_kernel, dates, lats, divmod(owner, lats), owner * lines + row),
+        in_specs=[pl.BlockSpec(memory_space=pltpu.VMEM)],
+        out_specs=pl.BlockSpec(memory_space=pltpu.VMEM),
+        out_shape=jax.ShapeDtypeStruct((4, CP, LANES), F32),
+        scratch_shapes=[
+            pltpu.VMEM((count, LANES), BF16),
+            pltpu.SemaphoreType.DMA(()),
+            pltpu.SemaphoreType.DMA((dates * lats - 1,)),
+            pltpu.SemaphoreType.DMA(()),
+        ],
+        compiler_params=pltpu.CompilerParams(
+            collective_id=0, has_side_effects=True, vmem_limit_bytes=VMEM
+        ),
+        name="norms",
+    )(lax.slice_in_dim(shard, row, row + count, axis=0))
+
+
+def gather_kernel(
+    dates, lats, width, src, x, gain, shift, out, moved, local_sem, z_send, z_recv, send, recv, buffers, buffer_sems
+):
     d, l = lax.axis_index("date"), lax.axis_index("lat")
     steps = dates.bit_length() - 1
     parts = pieces(src.shape[0])
@@ -711,6 +773,20 @@
         sent.append(copy)
         flights[o, p, i, n] = copy
 
+    rows = [(s, r) for s in range(x.shape[0]) for r in range(x.shape[1])]
+    saves = []
+
+    def spread_rows():
+        for n, (s, r) in enumerate(rows):
+            if n >= 2:
+                saves[n - 2].wait()
+            spread(x.at[s, r], gain, shift, width, buffers.at[n % 2])
+            save = pltpu.make_async_copy(buffers.at[n % 2], moved.at[s, r], buffer_sems.at[n % 2])
+            save.start()
+            saves.append(save)
+            yield
+
+    aside = spread_rows()
     for wave in range(lats + steps):
         if wave < lats:
             if wave:
@@ -720,6 +796,7 @@
             for i in range(steps):
                 for p in range(2):
                     cross(wave, p, i, 0)
+        next(aside, None)
         for i in range(steps)[::-1]:
             o = wave - 1 - i
             if 0 <= o < lats:
@@ -728,28 +805,41 @@
                         flights[o, p, i, n].wait_recv()
                         for later in range(i + 1, steps):
                             cross(o, p, later, n + (1 << i))
+    for _ in aside:
+        pass
+    for save in saves[-2:]:
+        save.wait()
     own.wait()
     for copy in sent:
         copy.wait_send()
 
 
-def gather(shard, dates, lats):
+def gather(shard, x, gain, shift, dates, lats, width):
     slots = dates - 1
+    moved = x.shape[:2] + (2 * REACH + 1,) + x.shape[2:]
+    anywhere = pl.BlockSpec(memory_space=pl.ANY)
     return pl.pallas_call(
-        functools.partial(gather_kernel, dates, lats),
-        in_specs=[pl.BlockSpec(memory_space=pl.ANY)],
-        out_specs=pl.BlockSpec(memory_space=pl.ANY),
-        out_shape=jax.ShapeDtypeStruct((dates, lats) + shard.shape, shard.dtype),
+        functools.partial(gather_kernel, dates, lats, width),
+        in_specs=[anywhere] + [pl.BlockSpec(memory_space=pltpu.VMEM)] * 3,
+        out_specs=[anywhere, anywhere],
+        out_shape=(
+            jax.ShapeDtypeStruct((dates, lats) + shard.shape, shard.dtype),
+            jax.ShapeDtypeStruct(moved, BF16),
+        ),
         scratch_shapes=[
             pltpu.SemaphoreType.DMA(()),
             pltpu.SemaphoreType.DMA((lats - 1,)),
             pltpu.SemaphoreType.DMA((lats - 1,)),
             pltpu.SemaphoreType.DMA((lats, 2, slots)),
             pltpu.SemaphoreType.DMA((lats, 2, slots)),
+            pltpu.VMEM((2,) + moved[2:], BF16),
+            pltpu.SemaphoreType.DMA((2,)),
         ],
-        compiler_params=pltpu.CompilerParams(collective_id=0, has_side_effects=True),
+        compiler_params=pltpu.CompilerParams(
+            collective_id=2, has_side_effects=True, vmem_limit_bytes=VMEM
+        ),
         name="gather_params",
-    )(shard)
+    )(shard, x, gain, shift)
 
 
 def scatter_kernel(dates, lats, src, out, sums, others, z_send, z_recv, send, recv):
@@ -851,6 +941,20 @@
     )(packed)
 
 
+def add_vectors(packed, vectors, lines):
+    first, lead = divmod(OFF_G1, LANES)
+    count = -(-(lead + vectors.shape[0]) // LANES)
+    extra = jnp.pad(vectors, (lead, count * LANES - lead - vectors.shape[0])).reshape(count, LANES)
+    done = 0
+    while done < count:
+        shard, row = divmod(first + done, lines)
+        amount = min(count - done, lines - row)
+        old = lax.slice(packed, (shard, row, 0), (shard + 1, row + amount, LANES))
+        packed = lax.dynamic_update_slice(packed, old + extra[None, done : done + amount], (shard, row, 0))
+        done += amount
+    return packed
+
+
 def local(inputs, noise, cotangent, params, psi, step_counts, pixel_mask, offsets, bases):
     samples, steps, rows, width, _ = inputs.shape
     slabs = samples * steps
@@ -865,19 +969,31 @@
 
     upward = [(i, i + 1) for i in range(lats - 1)]
     downward = [(i + 1, i) for i in range(lats - 1)]
-    x = padded(jnp.concatenate([by_channel(inputs), by_channel(noise)], axis=2))
-    below = lax.ppermute(x[:, rows - 1], "lat", upward)
-    above = lax.ppermute(x[:, 0], "lat", downward)
     lines = params.shape[0] // LANES
     held = -(-lines // STEP) * STEP
     shard = jnp.pad(params.reshape(lines, LANES), ((0, held - lines), (0, 0)))
-    gathered = gather(shard, dates, lats).reshape(dates * lats, held, LANES)
-    w, wt, up, upt, dn, dnt, small = unpack(gathered, lines)
+    small = norms(shard, lines, dates, lats)
+    shard, inputs, small = lax.optimization_barrier((shard, inputs, small))
+    x = padded(jnp.concatenate([by_channel(inputs), by_channel(noise)], axis=2))
+    edges = [(x[s, rows - 1 :], x[s, :1]) for s in range(slabs)]
+    gathered, moved = gather(shard, x, small[0], small[1], dates, lats, width)
+    gathered = gathered.reshape(dates * lats, held, LANES)
     cot = padded(by_channel(cotangent)).reshape(slabs * rows, CP, WIDE)
     active = jnp.arange(steps, dtype=jnp.int32)[None, :] < step_counts[:, None]
     mask = active.reshape(slabs, 1, 1) * pixel_mask[None]
     mask = jnp.pad(mask.astype(F32), ((0, 0), (0, 0), (0, WIDE - width)))
-    basis = lift(offsets, bases, psi, below, x, above, small[0], small[1], lat, width)
+    matrices = unpack(gathered, lines)
+    halos, done = [], gathered
+    for s in range(slabs):
+        top, bottom, done = lax.optimization_barrier((*edges[s], done))
+        halos.append((lax.ppermute(top, "lat", upward), lax.ppermute(bottom, "lat", downward)))
+        done = halos[-1], matrices
+    matrices = done[1]
+    basis = ()
+    for s in range(slabs):
+        basis = (lift(offsets, bases, psi, *halos[s], moved, small[0], small[1], basis, s, lat, width),)
+    basis = basis[0]
+    w, wt, up, upt, dn, dnt = matrices
     basis = basis.reshape(slabs * rows, BASIS * CP, WIDE)
     output, gconv, gup, gdn, second_sums = block(
         basis, x.reshape(slabs * rows, CP, WIDE), cot, mask.reshape(slabs * rows, 1, WIDE),
@@ -888,12 +1004,11 @@
     from_below = lax.ppermute(to_above, "lat", upward)
     from_above = lax.ppermute(to_below, "lat", downward)
     gdisco = weight_grad(basis, gconv)
+    packed = pack(gdisco, gup, gdn, dates * lats, lines, held)
     grad, first_sums = input_grad(x, gconv_rows, own, from_below, from_above, small[0], width)
     sums = jnp.sum(jnp.concatenate([first_sums, second_sums]), axis=-1)
-    valid = jnp.array([CIN, CIN, C, C], jnp.int32)[:, None]
-    sums = jnp.where(jnp.arange(CP, dtype=jnp.int32)[None, :] < valid, sums, 0.0)
-    sums = jnp.pad(sums, ((0, 0), (0, 8 * LANES - CP))).reshape(4, 8, LANES)
-    packed = pack(gdisco, gup, gdn, sums, dates * lats, lines, held)
+    vectors = jnp.concatenate([sums[0, :CIN], sums[1, :CIN], sums[2, :C], sums[3, :C]])
+    packed = add_vectors(packed, vectors.astype(BF16), lines)
     summed = scatter(packed.reshape(dates, lats, held, LANES))
 
     def by_pixel(values):

time: 455 us -> 421 us (0.925)
  waiting for transfers between devices: 19.8 us -> 0.61 us
  Pallas kernels: 381 us -> 362 us
  starting transfers between devices: 11.4 us -> 17.3 us
    pallas_call x2 -> x4, Pallas kernels: 112 us -> 88.7 us  [the longest x1 44.6 us: gather(): pl.pallas_call(functools.partial(gather_kernel, dates, lats, width), in_s...]
    ppermute x1, waiting for transfers between devices: 14.1 us -> 0.01 us  [local(): from_below = lax.ppermute(to_above, 'lat', upward)]
    ppermute x1, waiting for transfers between devices: 5.7 us -> 0.01 us  [local(): from_above = lax.ppermute(to_below, 'lat', downward)]
    unnamed x27 -> x22, local copies, waits for them, and re-layouts: 18.5 us -> 14.7 us
    ppermute x2 -> x4, starting transfers between devices: 7.2 us -> 9.91 us  [the longest x2 6.87 us: local(): lax.ppermute(top, 'lat', upward)]
  transfers between devices with their start and end apart: 4 -> 6, of which waited for: 2 -> 1; matrix products, arithmetic and copies ran while one was open for 3% -> 3% of each run, Pallas kernels for 27% -> 21%
where the time goes in v3:
time: 421 us; the launch traced here: 414 us
  Pallas kernels  362 us (86%)
  local copies, waits for them, and re-layouts  29 us (7%)
  starting transfers between devices  17.3 us (4%)
    pallas_call x1, Pallas kernels, block(): pl.pallas_call(functools.partial(block_kernel, width), grid=(count,), in_...  103 us
    pallas_call x1, Pallas kernels, scatter(): pl.pallas_call(functools.partial(scatter_kernel, dates, lats), in_specs=[...  48.5 us
    pallas_call x1, Pallas kernels, gather(): pl.pallas_call(functools.partial(gather_kernel, dates, lats, width), in_s...  44.6 us
    pallas_call x1, Pallas kernels, lower(): pl.pallas_call(functools.partial(lower_kernel, rows), grid=(slabs,), in_s...  34.8 us
    pallas_call x2, Pallas kernels, lift(): pl.pallas_call(functools.partial(lift_kernel, rows, slab, lat, width), gr...  32.6 us
    pallas_call x1, Pallas kernels, unpack(): pl.pallas_call(functools.partial(unpack_kernel, nrow, pad), out_shape=(ja...  25.3 us
    pallas_call x1, Pallas kernels, pack(): pl.pallas_call(functools.partial(pack_kernel, nrow, pad), out_shape=jax.S...  23.7 us
    pallas_call x1, Pallas kernels, weight_grad(): pl.pallas_call(outer_kernel, grid=(count,), in_specs=[pl.BlockSpec((1, BA...  22.1 us
  transfers between devices with their start and end apart: 6, of which 1 were waited for; matrix products, arithmetic and copies ran while one was open for 3% of the time, Pallas kernels for 21%

profile of v3, /device:TPU:4, one launch (start us, length us, event | category | flops | bytes accessed | tf_op | source)
XLA Modules:
  0.0 413.8 jit_solution(151256524686831173)
XLA Ops:
  0.6 0.0 copy-start.1
  0.6 1.5 slice_bitcast_fusion.10.src
  2.1 11.5 %norms.1 = f32[4,656,128]{2,1,0:T(8,128)} custom-call(bf16[48,128]{1,0:T(8,128)(2,1)} %slice_bitcast_fusion.10.src), custom_call_target="tpu_custom_call" | custom-call | tf_op jit(solution)/shard_map/norms/pallas_call | solution.py:718
  13.6 1.6 pad.20.src
  15.3 2.4 slice_bitcast_fusion.6
  17.6 0.0 copy-done.1
  17.6 0.0 copy-start.6
  17.6 0.5 copy.24
  18.1 0.3 copy-done.6
  18.4 0.9 fusion.5.x
  19.3 0.0 copy-start
  19.3 1.5 slice_bitcast_fusion.1
  20.8 0.8 copy-done
  21.6 44.6 %gather_params.1 = (bf16[8,4,816,128]{3,2,1,0:T(8,128)(2,1)}, bf16[2,2,5,656,768]{4,3,2,1,0:T(8,128)(2,1)}) custom-call(bf16[816,128]{1,0:T(8,128)(2,1)} %pad.20.src, bf16[2,2,656,768]{3,2,1,0:T(8,128)(2,1)} %copy-done, f32[656,128]{1,0:T(8,128)} %get-tuple-element.67.gain, f32[656,128]{1,0:T(8,128)} %get-tuple-element.66.shift), custom_call_target="tpu_custom_call" | custom-call | tf_op jit(solution)/shard_map/gather_params/pallas_call | solution.py:821
  66.2 0.0 copy-start.8
  66.2 2.3 collective-permute-start
  68.5 1.3 collective-permute-start.1
  69.7 25.3 %unpack.1 = (bf16[2624,768]{1,0:T(8,128)(2,1)}, bf16[656,2624]{1,0:T(8,128)(2,1)}, bf16[656,1408]{1,0:T(8,128)(2,1)}, bf16[1296,656]{1,0:T(8,128)(2,1)}, bf16[12...) custom-call(bf16[32,816,128]{2,1,0:T(8,128)(2,1)} %bitcast.60), custom_call_target="tpu_custom_call" | custom-call | tf_op jit(solution)/shard_map/unpack/pallas_call | solution.py:86
  95.0 0.0 collective-permute-done.lo
  95.0 0.0 collective-permute-done.1.hi
  95.0 4.6 %collective-permute-start.2 = (bf16[1,656,768]{2,1,0:T(8,128)(2,1)S(1)}, bf16[1,656,768]{2,1,0:T(8,128)(2,1)S(1)}, u32[]{:S(2)}, u32[]{:S(2)}) collective-permute-start(bf16[1,656,768]{2,1,0:T(8,128)(2,1)S(1)} %get-tuple-element.40), channel_id=1, source_target_pairs={{0,1},{1,2},{2,3},{4,5},{5,6},{6,7},{8,9},{9,10},{10,11},{12,13},{... | collective-permute-start | bytes 3022856 | tf_op jit(solution)/shard_map/ppermute | solution.py:989
  99.7 1.8 collective-permute-start.3
  101.4 0.0 copy-done.8
  101.4 0.7 copy.15.offsets
  102.1 2.6 copy.21
  104.7 0.0 copy-start.7
  104.7 2.3 pad.22.clone
  107.7 0.0 copy-done.7
  107.7 0.1 multiply_convert_fusion
  107.8 0.6 reshape.81.mask
  108.4 16.3 %lift.2.refs_0_ = bf16[2,2,2624,768]{3,2,1,0:T(8,128)(2,1)} custom-call(s32[12,2]{1,0:T(8,128)} %copy.15.offsets, s32[12]{0:T(128)} %bases.5, f32[8,12]{1,0:T(8,128)} %psi.5, bf16[1,656,768]{2,1,0:T(8,128)(2,1)} %collective-permute-done.lo, bf16[1,656,768]{2,1,0:T(8,128)(2,1)} %collective-permute-done.1.hi, ...), custom_call_target="tpu_custom_call" | custom-call | flops 41943040 | bytes 41943040 | tf_op jit(solution)/shard_map/lift/pallas_call | solution.py:301
  124.8 0.0 collective-permute-done.2.lo
  124.8 0.0 copy-start.4
  124.8 0.6 collective-permute-done.3.hi
  125.4 0.3 copy-done.4
  125.8 16.2 %lift.3 = bf16[2,2,2624,768]{3,2,1,0:T(8,128)(2,1)} custom-call(s32[12,2]{1,0:T(8,128)} %copy.15.offsets, s32[12]{0:T(128)} %bases.5, f32[8,12]{1,0:T(8,128)} %psi.5, bf16[1,656,768]{2,1,0:T(8,128)(2,1)} %copy-done.4, bf16[1,656,768]{2,1,0:T(8,128)(2,1)} %collective-permute-done.3.hi, ...), custom_call_target="tpu_custom_call", output_to_operand_aliasing={{}: (8, {})} | custom-call | flops 41943040 | bytes 41943040 | tf_op jit(solution)/shard_map/lift/pallas_call | solution.py:301
  142.0 102.7 %block.1 = (bf16[4,656,768]{2,1,0:T(8,128)(2,1)}, bf16[4,656,768]{2,1,0:T(8,128)(2,1)}, f32[656,1408]{1,0:T(8,128)}, f32[1296,768]{1,0:T(8,128)}, f32[2,656,128]{2,1,0:T(8,128)}) custom-call(bf16[4,2624,768]{2,1,0:T(8,128)(2,1)} %bitcast.52, bf16[4,656,768]{2,1,0:T(8,128)(2,1)} %bitcast.54, bf16[4,656,768]{2,1,0:T(8,128)(2,1)} %bitcast.58, ...), custom_call_target="tpu_custom_call" | custom-call | tf_op jit(solution)/shard_map/block/pallas_call | solution.py:442
  244.7 34.8 %lower.1 = (f32[2,2,656,768]{3,2,1,0:T(8,128)}, bf16[2,656,768]{2,1,0:T(8,128)(2,1)}, bf16[2,656,768]{2,1,0:T(8,128)(2,1)}) custom-call(s32[12,2]{1,0:T(8,128)} %copy.15.offsets, s32[12]{0:T(128)} %bases.5, f32[8,12]{1,0:T(8,128)} %psi.5, bf16[2,2,656,768]{3,2,1,0:T(8,128)(2,1)} %bitcast.55, bf16[2624,768]{1,0:T(8,128)(2,1)} %get-tuple-element.34.w), custom_call_target="tpu_custom_call" | custom-call | tf_op jit(solution)/shard_map/lower/pallas_call | solution.py:543
  279.5 5.8 %collective-permute-start.4 = (bf16[2,656,768]{2,1,0:T(8,128)(2,1)}, bf16[2,656,768]{2,1,0:T(8,128)(2,1)}, u32[]{:S(2)}, u32[]{:S(2)}) collective-permute-start(bf16[2,656,768]{2,1,0:T(8,128)(2,1)} %get-tuple-element.46), channel_id=1, source_target_pairs={{0,1},{1,2},{2,3},{4,5},{5,6},{6,7},{8,9},{9,10},{10,11},{12,13},{... | collective-permute-start | bytes 6045704 | tf_op jit(solution)/shard_map/ppermute | solution.py:1004
  285.3 0.0 copy-start.3
  285.3 1.5 collective-permute-start.5
  286.9 22.1 %weight_grad.1.gd_ref = f32[2624,768]{1,0:T(8,128)} custom-call(bf16[4,2624,768]{2,1,0:T(8,128)(2,1)} %bitcast.53, bf16[4,656,768]{2,1,0:T(8,128)(2,1)} %get-tuple-element.44.gconv), custom_call_target="tpu_custom_call" | custom-call | tf_op jit(solution)/shard_map/weight_grad/pallas_call | solution.py:478
  309.0 0.0 copy-done.3
  309.0 0.3 slice.92
  309.2 5.0 %copy.25 = bf16[2,2,641,720]{3,1,2,0:T(2,128)(2,1)} copy(bf16[2,2,641,720]{3,2,1,0:T(8,128)(2,1)S(1)} %slice.92) | data formatting | bytes 7384320
  314.2 23.7 %pack.1 = bf16[32,816,128]{2,1,0:T(8,128)(2,1)} custom-call(f32[2624,768]{1,0:T(8,128)} %weight_grad.1.gd_ref, f32[656,1408]{1,0:T(8,128)} %get-tuple-element.49.gu_ref, f32[1296,768]{1,0:T(8,128)} %get-tuple-element.50.gn_ref), custom_call_target="tpu_custom_call" | custom-call | tf_op jit(solution)/shard_map/pack/pallas_call | solution.py:160
  337.9 0.0 collective-permute-done.4.lo
  338.0 0.0 collective-permute-done.5.hi
  338.0 0.0 copy-start.5
  338.0 15.9 %input_grad.1 = (bf16[2,2,656,768]{3,2,1,0:T(8,128)(2,1)}, f32[2,656,128]{2,1,0:T(8,128)}) custom-call(bf16[2,2,656,768]{3,2,1,0:T(8,128)(2,1)} %copy-done, bf16[2,2,656,768]{3,2,1,0:T(8,128)(2,1)} %bitcast.56, f32[2,2,656,768]{3,2,1,0:T(8,128)} %get-tuple-element.45.own, bf16[2,656,768]{2,1,0:T(8,128)(2,1)} %collective-permute-done.4.lo, ...), custom_call_target="tpu_custom_call" | custom-call | tf_op jit(solution)/shard_map/input_grad/pallas_call | solution.py:609
  353.9 0.0 copy-done.5
  353.9 1.6 maximum_reduce_fusion
  355.5 0.1 concatenate.12
  355.6 0.8 slice_add_fusion
  356.4 1.5 dynamic_update_slice.3
  358.0 0.0 copy-start.2
  358.0 48.5 %scatter_grads.1 = f32[816,128]{1,0:T(8,128)} custom-call(bf16[8,4,816,128]{3,2,1,0:T(8,128)(2,1)} %bitcast.57), custom_call_target="tpu_custom_call" | custom-call | tf_op jit(solution)/shard_map/scatter_grads/pallas_call | solution.py:924
  406.5 1.8 slice_bitcast_fusion.5
  408.3 0.0 copy-done.2
  408.3 0.3 slice_bitcast_fusion
  408.5 5.0 %copy.19 = bf16[1,2,2,720,641]{3,2,4,1,0:T(2,128)(2,1)} copy(bf16[1,2,2,720,641]{3,4,2,1,0:T(8,128)(2,1)S(1)} %slice_bitcast_fusion) | data formatting | bytes 7384320
  (4 shorter events, 0.1 us)
Async XLA Ops:
  0.6 17.0 %copy-start.1 = (bf16[1,2,2,720,641]{3,2,4,1,0:T(2,128)(2,1)S(1)}, bf16[1,2,2,720,641]{3,2,4,1,0:T(2,128)(2,1)}, u32[]{:S(2)}) copy-start(bf16[1,2,2,720,641]{3,2,4,1,0:T(2,128)(2,1)} %param.9) | copy-start | bytes 11076484
  17.6 0.8 copy-start.6
  19.3 2.2 copy-start
  66.2 35.2 %copy-start.8 = (s32[12,2]{0,1:T(2,128)S(1)}, s32[12,2]{0,1:T(2,128)}, u32[]{:S(2)}) copy-start(s32[12,2]{0,1:T(2,128)} %param.16) | copy-start | bytes 292
  66.2 28.8 %collective-permute-start = (bf16[1,656,768]{2,1,0:T(8,128)(2,1)}, bf16[1,656,768]{2,1,0:T(8,128)(2,1)}, u32[]{:S(2)}, u32[]{:S(2)}) collective-permute-start(bf16[1,656,768]{2,1,0:T(8,128)(2,1)} %get-tuple-element.32), channel_id=1, source_target_pairs={{0,1},{1,2},{2,3},{4,5},{5,6},{6,7},{8,9},{9,10},{10,11},{12,13},{... | collective-permute-start | bytes 3022856 | tf_op jit(solution)/shard_map/ppermute | solution.py:989
  68.5 26.6 %collective-permute-start.1 = (bf16[1,656,768]{2,1,0:T(8,128)(2,1)S(1)}, bf16[1,656,768]{2,1,0:T(8,128)(2,1)}, u32[]{:S(2)}, u32[]{:S(2)}) collective-permute-start(bf16[1,656,768]{2,1,0:T(8,128)(2,1)S(1)} %get-tuple-element.33), channel_id=1, source_target_pairs={{1,0},{2,1},{3,2},{5,4},{6,5},{7,6},{9,8},{10,9},{11,10},{13,12},{... | collective-permute-start | bytes 3022856 | tf_op jit(solution)/shard_map/ppermute | solution.py:989
  95.0 29.8 %collective-permute-start.2 = (bf16[1,656,768]{2,1,0:T(8,128)(2,1)S(1)}, bf16[1,656,768]{2,1,0:T(8,128)(2,1)S(1)}, u32[]{:S(2)}, u32[]{:S(2)}) collective-permute-start(bf16[1,656,768]{2,1,0:T(8,128)(2,1)S(1)} %get-tuple-element.40), channel_id=1, source_target_pairs={{0,1},{1,2},{2,3},{4,5},{5,6},{6,7},{8,9},{9,10},{10,11},{12,13},{... | collective-permute-start | bytes 3022856 | tf_op jit(solution)/shard_map/ppermute | solution.py:989
  99.7 25.8 %collective-permute-start.3 = (bf16[1,656,768]{2,1,0:T(8,128)(2,1)S(1)}, bf16[1,656,768]{2,1,0:T(8,128)(2,1)}, u32[]{:S(2)}, u32[]{:S(2)}) collective-permute-start(bf16[1,656,768]{2,1,0:T(8,128)(2,1)S(1)} %get-tuple-element.41), channel_id=1, source_target_pairs={{1,0},{2,1},{3,2},{5,4},{6,5},{7,6},{9,8},{10,9},{11,10},{13,12},{... | collective-permute-start | bytes 3022856 | tf_op jit(solution)/shard_map/ppermute | solution.py:989
  104.7 3.0 copy-start.7
  124.8 1.0 copy-start.4
  279.5 58.5 %collective-permute-start.4 = (bf16[2,656,768]{2,1,0:T(8,128)(2,1)}, bf16[2,656,768]{2,1,0:T(8,128)(2,1)}, u32[]{:S(2)}, u32[]{:S(2)}) collective-permute-start(bf16[2,656,768]{2,1,0:T(8,128)(2,1)} %get-tuple-element.46), channel_id=1, source_target_pairs={{0,1},{1,2},{2,3},{4,5},{5,6},{6,7},{8,9},{9,10},{10,11},{12,13},{... | collective-permute-start | bytes 6045704 | tf_op jit(solution)/shard_map/ppermute | solution.py:1004
  285.3 23.7 %copy-start.3 = (bf16[4,656,768]{2,1,0:T(8,128)(2,1)S(1)}, bf16[4,656,768]{2,1,0:T(8,128)(2,1)}, u32[]{:S(2)}) copy-start(bf16[4,656,768]{2,1,0:T(8,128)(2,1)} %get-tuple-element.43) | copy-start | bytes 12091396
  285.3 52.6 %collective-permute-start.5 = (bf16[2,656,768]{2,1,0:T(8,128)(2,1)}, bf16[2,656,768]{2,1,0:T(8,128)(2,1)}, u32[]{:S(2)}, u32[]{:S(2)}) collective-permute-start(bf16[2,656,768]{2,1,0:T(8,128)(2,1)} %get-tuple-element.47), channel_id=1, source_target_pairs={{1,0},{2,1},{3,2},{5,4},{6,5},{7,6},{9,8},{10,9},{11,10},{13,12},{... | collective-permute-start | bytes 6045704 | tf_op jit(solution)/shard_map/ppermute | solution.py:1005
  338.0 15.9 %copy-start.5 = (f32[2,656,128]{2,1,0:T(8,128)S(1)}, f32[2,656,128]{2,1,0:T(8,128)}, u32[]{:S(2)}) copy-start(f32[2,656,128]{2,1,0:T(8,128)} %get-tuple-element.52) | copy-start | bytes 2015236
  358.0 50.3 %copy-start.2 = (bf16[2,2,656,768]{3,2,1,0:T(8,128)(2,1)S(1)}, bf16[2,2,656,768]{3,2,1,0:T(8,128)(2,1)}, u32[]{:S(2)}) copy-start(bf16[2,2,656,768]{3,2,1,0:T(8,128)(2,1)} %get-tuple-element.48) | copy-start | bytes 12091396

commit v4 on v3

--- a/solution.py
+++ b/solution.py
@@ -320,99 +320,280 @@
 GELU_B = 0.044715
 
 
+TILE = 256
+
+
+def weave(*lists):
+    order = []
+    for which, steps in enumerate(lists):
+        for n, step in enumerate(steps):
+            order.append(((n + 0.5) / len(steps), which, n, step))
+    for _, _, _, step in sorted(order, key=lambda entry: entry[:3]):
+        step()
+
+
+class Job:
+    def __init__(self, buffers, weights, totals, mask):
+        self.basis, self.x, self.cot, self.out, self.gconv = buffers[:5]
+        self.res, self.second, self.pre, self.act, self.mid, self.gact, self.gb, self.gpre = buffers[5:]
+        self.wt, self.upt, self.up, self.dnt, self.dn, self.gain, self.shift = weights
+        self.gup, self.gdn, self.sums = totals
+        self.mask = mask
+
+    @staticmethod
+    def at(c):
+        return slice(c * STEP, (c + 1) * STEP)
+
+    @staticmethod
+    def wide(column):
+        return jnp.concatenate([column] * (TILE // LANES), axis=1)
+
+    @staticmethod
+    def only(c, values, channels, other=0.0):
+        if (c + 1) * STEP <= channels:
+            return values
+        row = lax.broadcasted_iota(jnp.int32, (STEP, TILE), 0)
+        return jnp.where(row < channels - c * STEP, values, other)
+
+    def product(self, out, left, right, count):
+        rows = left.shape[0]
+        size = -(-rows // (count * STEP)) * STEP
+
+        def step(start):
+            at = slice(start, min(start + size, rows))
+            values = left[at, : right.shape[0]]
+            out[at, :] = jnp.dot(values, right[...], preferred_element_type=F32)
+
+        return [functools.partial(step, start) for start in range(0, rows, size)]
+
+    def outer(self, out, left, right, count):
+        rows = left.shape[0]
+        size = -(-rows // (count * STEP)) * STEP
+
+        def step(start):
+            at = slice(start, min(start + size, rows))
+            term = lax.dot_general(
+                left[at, :], right[...], (((1,), (1,)), ((), ())), preferred_element_type=F32
+            )
+            out[at, : right.shape[0]] += term
+
+        return [functools.partial(step, start) for start in range(0, rows, size)]
+
+    def m1(self):
+        return self.product(self.res, self.wt, self.basis, 4)
+
+    def v1(self):
+        state = {"sum": jnp.zeros((8, TILE), F32), "square": jnp.zeros((8, TILE), F32)}
+        mask = self.mask()
+
+        def add(c):
+            at = self.at(c)
+            value = self.res[at, :] + self.only(c, self.x[at, :].astype(F32), C)
+            self.res[at, :] = value
+            self.gb[at, :] = (self.cot[at, :].astype(F32) * mask).astype(BF16)
+            state["sum"] = state["sum"] + halves(self.only(c, value, C))
+
+        def mean():
+            self.mean = jnp.sum(state["sum"], axis=0, keepdims=True) * (1.0 / C)
+
+        def square(c):
+            value = self.res[self.at(c), :] - self.mean
+            state["square"] = state["square"] + halves(self.only(c, value * value, C))
+
+        def scale():
+            total = jnp.sum(state["square"], axis=0, keepdims=True)
+            self.scale = lax.rsqrt(total * (1.0 / C) + 1e-05)
+
+        def normalize(c):
+            at = self.at(c)
+            value = (self.res[at, :] - self.mean) * self.scale
+            value = value * self.wide(self.gain[at, :]) + self.wide(self.shift[at, :])
+            row = lax.broadcasted_iota(jnp.int32, (STEP, TILE), 0)
+            if c == C // STEP:
+                value = jnp.where(row == C % STEP, 1.0, value)
+            self.second[at, :] = value.astype(BF16)
+
+        chunks = range(CP // STEP)
+        steps = [functools.partial(add, c) for c in chunks] + [mean]
+        steps += [functools.partial(square, c) for c in chunks] + [scale]
+        return steps + [functools.partial(normalize, c) for c in chunks]
+
+    def m2(self):
+        return self.product(self.pre, self.upt, self.second, 9)
+
+    def v2(self):
+        def gelu(c):
+            at = self.at(c)
+            v = self.pre[at, :]
+            square = v * v
+            bend = jnp.tanh(GELU_A * v * (1.0 + GELU_B * square))
+            half = 0.5 * (1.0 + bend)
+            value = v * half
+            if c == HID // STEP:
+                row = lax.broadcasted_iota(jnp.int32, (STEP, TILE), 0)
+                value = jnp.where(row == HID % STEP, 1.0, value)
+            self.act[at, :] = value.astype(BF16)
+            rise = GELU_A * (1.0 + 3.0 * GELU_B * square)
+            self.pre[at, :] = half + 0.5 * v * (1.0 - bend * bend) * rise
+
+        return [functools.partial(gelu, c) for c in range(HP // STEP)]
+
+    def m3(self):
+        back = self.product(self.gact, self.dn, self.gb, 9)
+        return self.product(self.mid, self.dnt, self.act, 4) + back
+
+    def v3(self):
+        def finish(c):
+            at = self.at(c)
+            self.out[at, :] = (self.res[at, :] + self.mid[at, :]).astype(BF16)
+
+        def back(c):
+            at = self.at(c)
+            self.gpre[at, :] = (self.gact[at, :] * self.pre[at, :]).astype(BF16)
+
+        steps = [functools.partial(finish, c) for c in range(CP // STEP)]
+        return steps + [functools.partial(back, c) for c in range(HP // STEP)]
+
+    def m4(self):
+        return self.product(self.mid, self.up, self.gpre, 4)
+
+    def v4(self):
+        state = {"flat": jnp.zeros((8, TILE), F32), "along": jnp.zeros((8, TILE), F32)}
+
+        def terms(c):
+            at = self.at(c)
+            dm = self.mid[at, :]
+            xhat = (self.res[at, :] - self.mean) * self.scale
+            return dm, xhat, dm * self.wide(self.gain[at, :])
+
+        def means(c):
+            _, xhat, g = terms(c)
+            g = self.only(c, g, C)
+            state["flat"] = state["flat"] + halves(g)
+            state["along"] = state["along"] + halves(g * xhat)
+
+        def join():
+            for name in state:
+                state[name] = jnp.sum(state[name], axis=0, keepdims=True) * (1.0 / C)
+
+        def backward(c):
+            at = self.at(c)
+            dm, xhat, g = terms(c)
+            value = g - state["flat"] - xhat * state["along"]
+            value = self.gb[at, :].astype(F32) + self.scale * value
+            self.gconv[at, :] = self.only(c, value, C).astype(BF16)
+            for n, term in enumerate((dm * xhat, dm)):
+                self.sums[n, at, :] += term[:, :LANES] + term[:, LANES:]
+
+        chunks = range(CP // STEP)
+        steps = [functools.partial(means, c) for c in chunks] + [join]
+        return steps + [functools.partial(backward, c) for c in chunks]
+
+    def m5(self):
+        first = self.outer(self.gdn, self.act, self.gb, 3)
+        return first + self.outer(self.gup, self.second, self.gpre, 2)
+
+
 def block_kernel(
-    width, basis, x, cot, mask, wt, upt, up, dnt, dn, gain, shift,
-    out, gconv, gup, gdn, sums,
-    res, second, pre, act, slope, gb, gpre, gsec,
+    basis, x, cot, mask, wt, upt, up, dnt, dn, gain, shift, out, gconv, gup, gdn, sums, *scratch
 ):
-    start = pl.program_id(0) == 0
-
-    @pl.when(start)
-    def _():
-        gup[...] = jnp.zeros_like(gup)
-        gdn[...] = jnp.zeros_like(gdn)
-        sums[...] = jnp.zeros_like(sums)
-
-    def dot(a, b):
-        return jnp.dot(a, b, preferred_element_type=F32)
-
-    res[...] = dot(wt[...], basis[0])
-
-    def add_input(c, at):
-        values = x[0, at, :].astype(F32)
-        keep = lax.broadcasted_iota(jnp.int32, (STEP, WIDE), 0) + c * STEP < C
-        res[at, :] = res[at, :] + jnp.where(keep, values, 0.0)
-        gb[at, :] = (cot[0, at, :].astype(F32) * mask[0]).astype(BF16)
-
-    each_chunk(add_input, 8)
-
-    def read(c):
-        return res[pl.ds(pl.multiple_of(c * STEP, STEP), STEP), :]
-
-    mean, scale = norm_stats(read, C)
-
-    def normalize(c, at):
-        values = (res[at, :] - mean) * scale * tiled(gain[at, :]) + tiled(shift[at, :])
-        row = lax.broadcasted_iota(jnp.int32, (STEP, WIDE), 0) + c * STEP
-        second[at, :] = jnp.where(row == C, 1.0, values).astype(BF16)
-
-    each_chunk(normalize, 8)
-    pre[...] = dot(upt[...], second[...])
-
-    def gelu(c, _):
-        at = pl.ds(pl.multiple_of(c * STEP, STEP), STEP)
-        v = pre[at, :]
-        square = v * v
-        bend = jnp.tanh(GELU_A * v * (1.0 + GELU_B * square))
-        half = 0.5 * (1.0 + bend)
-        row = lax.broadcasted_iota(jnp.int32, (STEP, WIDE), 0) + c * STEP
-        act[at, :] = jnp.where(row == HID, 1.0, v * half).astype(BF16)
-        rise = GELU_A * (1.0 + 3.0 * GELU_B * square)
-        slope[at, :] = half + 0.5 * v * (1.0 - bend * bend) * rise
+    count = basis.shape[0]
+    tiles = WIDE // TILE
+    in_sems, out_sems = scratch[-2:]
+    per_job = (len(scratch) - 2) // 2
+    sets = [scratch[:per_job], scratch[per_job : 2 * per_job]]
+    for total in (gup, gdn, sums):
+        total[...] = jnp.zeros_like(total)
+
+    def place(i, j):
+        return i // tiles * 2 + j, pl.ds(pl.multiple_of(i % tiles * TILE, TILE), TILE)
+
+    def arrive(i, j):
+        row, lanes = place(i, j)
+        return [
+            pltpu.make_async_copy(source.at[row, :, lanes], sets[j][n], in_sems.at[j, n])
+            for n, source in enumerate((basis, x, cot))
+        ]
+
+    def leave(i, j):
+        row, lanes = place(i, j)
+        return [
+            pltpu.make_async_copy(sets[j][3 + n], target.at[row, :, lanes], out_sems.at[j, n])
+            for n, target in enumerate((out, gconv))
+        ]
+
+    last = count // 2 * tiles - 1
+    for j in range(2):
+        for copy in arrive(0, j):
+            copy.start()
+
+    def pair(i, _):
+        def row_mask(j):
+            row, lanes = place(i, j)
+            return lambda: mask[row, :, lanes]
+
+        weights, totals = (wt, upt, up, dnt, dn, gain, shift), (gup, gdn, sums)
+        a, b = (Job(sets[j], weights, totals, row_mask(j)) for j in range(2))
+        after = jnp.minimum(i + 1, last)
+        coming = [arrive(after, j) for j in range(2)]
+        leaving = [leave(i, j) for j in range(2)]
+        for j in range(2):
+            for copy in arrive(i, j):
+                copy.wait()
+        weave(a.m1())
+        coming[0][0].start()
+        weave(a.v1(), b.m1())
+        coming[1][0].start()
+        for n in (1, 2):
+            coming[0][n].start()
+        weave(a.m2(), b.v1())
+        for n in (1, 2):
+            coming[1][n].start()
+        weave(a.v2(), b.m2())
+        weave(a.m3(), b.v2())
+        weave(a.v3(), b.m3())
+        leaving[0][0].start()
+        weave(a.m4(), b.v3())
+        leaving[1][0].start()
+        weave(a.v4(), b.m4())
+        leaving[0][1].start()
+        weave(a.m5(), b.v4())
+        leaving[1][1].start()
+        weave(b.m5())
+        for copies in leaving:
+            for copy in copies:
+                copy.wait()
         return 0
 
-    lax.fori_loop(0, HP // STEP, gelu, 0, unroll=8)
-    pre[:CP, :] = dot(dnt[...], act[...])
-
-    def finish(c, at):
-        out[0, at, :] = (res[at, :] + pre[at, :]).astype(BF16)
-
-    each_chunk(finish, 8)
-    pre[...] = dot(dn[:, :CP], gb[...])
-
-    def back(c, _):
-        at = pl.ds(pl.multiple_of(c * STEP, STEP), STEP)
-        gpre[at, :] = (pre[at, :] * slope[at, :]).astype(BF16)
-        return 0
-
-    lax.fori_loop(0, HP // STEP, back, 0, unroll=8)
-    gsec[...] = dot(up[:, :HP], gpre[...])
-
-    def means(c):
-        at = pl.ds(pl.multiple_of(c * STEP, STEP), STEP)
-        g = gsec[at, :] * tiled(gain[at, :])
-        return g, g * ((res[at, :] - mean) * scale)
-
-    flat, along = [v * (1.0 / C) for v in column_sums(means, C, 2)]
-
-    def backward(c, at):
-        dm = gsec[at, :]
-        xhat = (res[at, :] - mean) * scale
-        g = dm * tiled(gain[at, :])
-        value = gb[at, :].astype(F32) + scale * (g - flat - xhat * along)
-        row = lax.broadcasted_iota(jnp.int32, (STEP, WIDE), 0) + c * STEP
-        value = jnp.where(row < C, value, 0.0)
-        gconv[0, at, :] = wrapped(value, width).astype(BF16)
-        along_lanes(sums.at[0], at, dm * xhat)
-        along_lanes(sums.at[1], at, dm)
-
-    each_chunk(backward, 8)
-
-    def outer(a, b):
-        return lax.dot_general(a, b, (((1,), (1,)), ((), ())), preferred_element_type=F32)
-
-    gdn[:, :CP] += outer(act[...], gb[...])
-    gup[:, :HP] += outer(second[...], gpre[...])
+    lax.fori_loop(0, last + 1, pair, 0)
+    for j in range(2):
+        for copy in arrive(last, j):
+            copy.wait()
+
+
+def block(basis, x, cot, mask, wt, upt, up, dnt, dn, gain, shift):
+    count = x.shape[0]
+    anywhere = pl.BlockSpec(memory_space=pl.ANY)
+    held = pl.BlockSpec(memory_space=pltpu.VMEM)
+    low, high = pltpu.VMEM((CP, TILE), BF16), pltpu.VMEM((CP, TILE), F32)
+    hidden_low, hidden_high = pltpu.VMEM((HP, TILE), BF16), pltpu.VMEM((HP, TILE), F32)
+    per_job = [pltpu.VMEM((BASIS * CP, TILE), BF16), low, low, low, low]
+    per_job += [high, low, hidden_high, hidden_low, high, hidden_high, low, hidden_low]
+    return pl.pallas_call(
+        block_kernel,
+        in_specs=[anywhere] * 3 + [held] * 8,
+        out_specs=[anywhere] * 2 + [held] * 3,
+        out_shape=(
+            jax.ShapeDtypeStruct((count, CP, WIDE), BF16),
+            jax.ShapeDtypeStruct((count, CP, WIDE), BF16),
+            jax.ShapeDtypeStruct((CP, HL), F32),
+            jax.ShapeDtypeStruct((HP, WIDE), F32),
+            jax.ShapeDtypeStruct((2, CP, LANES), F32),
+        ),
+        scratch_shapes=per_job * 2 + [pltpu.SemaphoreType.DMA((2, 3)), pltpu.SemaphoreType.DMA((2, 2))],
+        compiler_params=pltpu.CompilerParams(vmem_limit_bytes=VMEM),
+        name="block",
+    )(basis, x, cot, mask, wt, upt, up, dnt, dn, gain, shift)
 
 
 def along_lanes(ref, at, values):
@@ -420,44 +601,6 @@
     for j in range(1, WIDE // LANES):
         total = total + values[:, j * LANES : (j + 1) * LANES]
     ref[at, :] = ref[at, :] + total
-
-
-def block(basis, x, cot, mask, wt, upt, up, dnt, dn, gain, shift, width):
-    count = x.shape[0]
-
-    def per_row(height):
-        return pl.BlockSpec((1, height, WIDE), lambda i: (i, 0, 0))
-
-    def whole(a):
-        return pl.BlockSpec(a.shape, lambda i: (0,) * len(a.shape), pipeline_mode=pl.Buffered(1))
-
-    outs = (
-        jax.ShapeDtypeStruct((count, CP, WIDE), BF16),
-        jax.ShapeDtypeStruct((count, CP, WIDE), BF16),
-        jax.ShapeDtypeStruct((CP, HL), F32),
-        jax.ShapeDtypeStruct((HP, WIDE), F32),
-        jax.ShapeDtypeStruct((2, CP, LANES), F32),
-    )
-    weights = (wt, upt, up, dnt, dn, gain, shift)
-    return pl.pallas_call(
-        functools.partial(block_kernel, width),
-        grid=(count,),
-        in_specs=[per_row(BASIS * CP), per_row(CP), per_row(CP), per_row(1)] + [whole(a) for a in weights],
-        out_specs=[per_row(CP), per_row(CP)] + [whole(a) for a in outs[2:]],
-        out_shape=outs,
-        scratch_shapes=[
-            pltpu.VMEM((CP, WIDE), F32),
-            pltpu.VMEM((CP, WIDE), BF16),
-            pltpu.VMEM((HP, WIDE), F32),
-            pltpu.VMEM((HP, WIDE), BF16),
-            pltpu.VMEM((HP, WIDE), F32),
-            pltpu.VMEM((CP, WIDE), BF16),
-            pltpu.VMEM((HP, WIDE), BF16),
-            pltpu.VMEM((CP, WIDE), F32),
-        ],
-        compiler_params=pltpu.CompilerParams(vmem_limit_bytes=VMEM),
-        name="block",
-    )(basis, x, cot, mask, *weights)
 
 
 def outer_kernel(basis, gconv, out):
@@ -489,9 +632,17 @@
     )(basis, gconv)
 
 
-def lower_kernel(rows, offsets, bases, psi, gconv, w, own, lo, hi, lifted, place, coef):
+GROUP = 11 * STEP
+GROUP_STEP = 10 * STEP
+
+
+def lower_kernel(rows, width, offsets, bases, psi, gconv, w, own, lo, hi, *scratch):
+    place, coef, in_sems, w_sems, out_sems = scratch[-5:]
+    per_slab = (len(scratch) - 5) // 2
+    sets = [scratch[:per_slab], scratch[per_slab : 2 * per_slab]]
     first_row = lax.axis_index("lat") * rows
     span = 2 * REACH + 1
+    groups = 1 + (CP - GROUP) // GROUP_STEP
     for n in range(3 * span):
         place[n] = 0
         for r in range(rows):
@@ -501,65 +652,139 @@
         place[n] = bases[p]
         for r in range(rows):
             coef[r, n] = psi[first_row + r, p]
-    for r in range(rows):
-        lifted[r] = jnp.dot(w[:, :CP], gconv[0, r], preferred_element_type=F32).astype(BF16)
-    for target in range(-1, rows + 1):
-        terms = []
-        for d in range(-REACH, REACH + 1):
-            for o in (-1, 0, 1):
-                r = target - o
-                if 0 <= r < rows:
-                    n = (o + 1) * span + d + REACH
-                    terms.append((d, r, coef[r, n], place[n] * CP))
-
-        def gather(c, at):
+
+    def channels(g):
+        return pl.ds(pl.multiple_of(g * GROUP_STEP, STEP), GROUP)
+
+    def weights(j, g):
+        return pltpu.make_async_copy(w.at[:, channels(g), :], sets[j][1], w_sems.at[j])
+
+    def products(j):
+        ring, part, lifted = sets[j][:3]
+
+        def step(r, k):
+            values = jnp.dot(part[k, :, :CP], ring[r], preferred_element_type=F32)
+            lifted[r, k] = values.astype(BF16)
+
+        return [functools.partial(step, r, k) for r in range(rows) for k in range(BASIS)]
+
+    def gathers(j):
+        lifted, inner, below, above = sets[j][2:]
+
+        def step(c, target):
+            at = slice(c * STEP, (c + 1) * STEP)
             total = None
             for d in range(-REACH, REACH + 1):
                 part = None
-                for e, r, weight, base in terms:
-                    if e == d:
-                        source = pl.ds(pl.multiple_of(base + c * STEP, STEP), STEP)
-                        term = weight * lifted[r, source, :].astype(F32)
+                for o in (-1, 0, 1):
+                    r = target - o
+                    if 0 <= r < rows:
+                        n = (o + 1) * span + d + REACH
+                        term = coef[r, n] * lifted[r, place[n], at, :].astype(F32)
                         part = term if part is None else part + term
                 if d:
                     part = pltpu.roll(part.astype(BF16), d % WIDE, axis=1).astype(F32)
                 total = part if total is None else total + part
             if target < 0:
-                lo[0, at, :] = total.astype(BF16)
+                below[at, :] = total.astype(BF16)
             elif target == rows:
-                hi[0, at, :] = total.astype(BF16)
+                above[at, :] = total.astype(BF16)
             else:
-                own[0, target, at, :] = total
-
-        each_chunk(gather, 8)
-
-
-def lower(offsets, bases, psi, gconv, w):
+                inner[target, at, :] = total
+
+        return [functools.partial(step, c, t) for c in range(GROUP // STEP) for t in range(-1, rows + 1)]
+
+    def pair_of_slabs(both, _):
+        def leaving(j, g):
+            slab = both * 2 + j
+            targets = (own.at[slab, :, channels(g), :], lo.at[slab, channels(g), :], hi.at[slab, channels(g), :])
+            return [
+                pltpu.make_async_copy(sets[j][3 + n], target, out_sems.at[j, n])
+                for n, target in enumerate(targets)
+            ]
+
+        rings = [pltpu.make_async_copy(gconv.at[both * 2 + j], sets[j][0], in_sems.at[j]) for j in range(2)]
+        for j in range(2):
+            rings[j].start()
+            weights(j, 0).start()
+        for j in range(2):
+            rings[j].wait()
+            ring = sets[j][0]
+            edge = width - (WIDE - LANES)
+            lane = lane_of(CP)
+            for r in range(rows):
+                first, last = ring[r, :, :LANES].astype(F32), ring[r, :, WIDE - LANES :].astype(F32)
+                beyond = jnp.where(
+                    lane < LANES - REACH,
+                    pltpu.roll(first, edge, axis=1),
+                    pltpu.roll(last, LANES - edge, axis=1),
+                )
+                ring[r, :, WIDE - LANES :] = jnp.where(lane < edge, last, beyond).astype(BF16)
+        weights(0, 0).wait()
+        weave(products(0))
+        weights(0, min(1, groups - 1)).start()
+
+        def group(g, _):
+            after, later = jnp.minimum(g + 1, groups - 1), jnp.minimum(g + 2, groups - 1)
+            def free(j):
+                @pl.when(g > 0)
+                def _():
+                    for copy in leaving(j, jnp.maximum(g - 1, 0)):
+                        copy.wait()
+
+            weights(1, g).wait()
+            free(0)
+            weave(products(1), gathers(0))
+            weights(1, after).start()
+            for copy in leaving(0, g):
+                copy.start()
+            weights(0, after).wait()
+            free(1)
+            weave(products(0), gathers(1))
+            weights(0, later).start()
+            for copy in leaving(1, g):
+                copy.start()
+            return 0
+
+        lax.fori_loop(0, groups, group, 0)
+        for j in range(2):
+            weights(j, groups - 1).wait()
+            for copy in leaving(j, groups - 1):
+                copy.wait()
+        return 0
+
+    lax.fori_loop(0, gconv.shape[0] // 2, pair_of_slabs, 0)
+
+
+def lower(offsets, bases, psi, gconv, w, width):
     slabs, rows = gconv.shape[:2]
     smem = pl.BlockSpec(memory_space=pltpu.SMEM)
-    halo = pl.BlockSpec((1, CP, WIDE), lambda s: (s, 0, 0))
-    per_slab = pl.BlockSpec((1, rows, CP, WIDE), lambda s: (s, 0, 0, 0))
+    anywhere = pl.BlockSpec(memory_space=pl.ANY)
     edge = jax.ShapeDtypeStruct((slabs, CP, WIDE), BF16)
+    per_slab = [
+        pltpu.VMEM((rows, CP, WIDE), BF16),
+        pltpu.VMEM((BASIS, GROUP, WIDE), BF16),
+        pltpu.VMEM((rows, BASIS, GROUP, WIDE), BF16),
+        pltpu.VMEM((rows, GROUP, WIDE), F32),
+        pltpu.VMEM((GROUP, WIDE), BF16),
+        pltpu.VMEM((GROUP, WIDE), BF16),
+    ]
     return pl.pallas_call(
-        functools.partial(lower_kernel, rows),
-        grid=(slabs,),
-        in_specs=[
-            smem,
-            smem,
-            smem,
-            per_slab,
-            pl.BlockSpec(w.shape, lambda s: (0, 0), pipeline_mode=pl.Buffered(1)),
-        ],
-        out_specs=[per_slab, halo, halo],
+        functools.partial(lower_kernel, rows, width),
+        in_specs=[smem, smem, smem, anywhere, anywhere],
+        out_specs=[anywhere] * 3,
         out_shape=(jax.ShapeDtypeStruct((slabs, rows, CP, WIDE), F32), edge, edge),
-        scratch_shapes=[
-            pltpu.VMEM((rows, BASIS * CP, WIDE), BF16),
+        scratch_shapes=per_slab * 2
+        + [
             pltpu.SMEM((3 * (2 * REACH + 1),), jnp.int32),
             pltpu.SMEM((rows, 3 * (2 * REACH + 1)), F32),
+            pltpu.SemaphoreType.DMA((2,)),
+            pltpu.SemaphoreType.DMA((2,)),
+            pltpu.SemaphoreType.DMA((2, 3)),
         ],
         compiler_params=pltpu.CompilerParams(vmem_limit_bytes=VMEM),
         name="lower",
-    )(offsets, bases, psi, gconv, w)
+    )(offsets, bases, psi, gconv, w.reshape(BASIS, CP, WIDE))
 
 
 def input_kernel(rows, width, x, gconv, own, lo, hi, gain, out, sums, total):
@@ -997,10 +1222,10 @@
     basis = basis.reshape(slabs * rows, BASIS * CP, WIDE)
     output, gconv, gup, gdn, second_sums = block(
         basis, x.reshape(slabs * rows, CP, WIDE), cot, mask.reshape(slabs * rows, 1, WIDE),
-        wt, upt, up, dnt, dn, small[2], small[3], width,
+        wt, upt, up, dnt, dn, small[2], small[3],
     )
     gconv_rows = gconv.reshape(slabs, rows, CP, WIDE)
-    own, to_below, to_above = lower(offsets, bases, psi, gconv_rows, w)
+    own, to_below, to_above = lower(offsets, bases, psi, gconv_rows, w, width)
     from_below = lax.ppermute(to_above, "lat", upward)
     from_above = lax.ppermute(to_below, "lat", downward)
     gdisco = weight_grad(basis, gconv)

time: 421 us -> 393 us (0.933); the launches traced: 414 us -> 392 us
  Pallas kernels: 362 us -> 340 us
    pallas_call x2, Pallas kernels: 137 us -> 116 us  [the longest x1 72.5 us: block(): pl.pallas_call(block_kernel, in_specs=[anywhere] * 3 + [held] * 8, out_sp...]
  transfers between devices with their start and end apart: 6 -> 6, of which waited for: 1 -> 1; matrix products, arithmetic and copies ran while one was open for 3% -> 3% of each run, Pallas kernels for 21% -> 22%
where the time goes in v4:
time: 393 us; the launch traced here: 392 us
  Pallas kernels  340 us (87%)
  local copies, waits for them, and re-layouts  28.7 us (7%)
  starting transfers between devices  17.2 us (4%)
    pallas_call x1, Pallas kernels, block(): pl.pallas_call(block_kernel, in_specs=[anywhere] * 3 + [held] * 8, out_sp...  72.5 us
    pallas_call x1, Pallas kernels, scatter(): pl.pallas_call(functools.partial(scatter_kernel, dates, lats), in_specs=[...  48.5 us
    pallas_call x1, Pallas kernels, gather(): pl.pallas_call(functools.partial(gather_kernel, dates, lats, width), in_s...  44.6 us
    pallas_call x1, Pallas kernels, lower(): pl.pallas_call(functools.partial(lower_kernel, rows, width), in_specs=[sm...  43.3 us
    pallas_call x2, Pallas kernels, lift(): pl.pallas_call(functools.partial(lift_kernel, rows, slab, lat, width), gr...  32.6 us
    pallas_call x1, Pallas kernels, unpack(): pl.pallas_call(functools.partial(unpack_kernel, nrow, pad), out_shape=(ja...  25.3 us
    pallas_call x1, Pallas kernels, pack(): pl.pallas_call(functools.partial(pack_kernel, nrow, pad), out_shape=jax.S...  23.7 us
    pallas_call x1, Pallas kernels, weight_grad(): pl.pallas_call(outer_kernel, grid=(count,), in_specs=[pl.BlockSpec((1, BA...  21.9 us
  transfers between devices with their start and end apart: 6, of which 1 were waited for; matrix products, arithmetic and copies ran while one was open for 3% of the time, Pallas kernels for 22%

profile of v4, /device:TPU:4, one launch (start us, length us, event | category | flops | bytes accessed | tf_op | source)
XLA Modules:
  0.0 391.6 jit_solution(8972114718355046437)
XLA Ops:
  0.6 0.0 copy-start.1
  0.6 1.5 slice_bitcast_fusion.10.src
  2.1 11.5 %norms.1 = f32[4,656,128]{2,1,0:T(8,128)} custom-call(bf16[48,128]{1,0:T(8,128)(2,1)} %slice_bitcast_fusion.10.src), custom_call_target="tpu_custom_call" | custom-call | tf_op jit(solution)/shard_map/norms/pallas_call | solution.py:943
  13.6 1.6 pad.20.src
  15.3 2.4 slice_bitcast_fusion.6
  17.6 0.0 copy-done.1
  17.6 0.0 copy-start.6
  17.6 0.5 copy.24
  18.1 0.3 copy-done.6
  18.4 0.9 fusion.5.x
  19.3 0.0 copy-start
  19.3 1.5 slice_bitcast_fusion.1
  20.8 0.8 copy-done
  21.6 44.6 %gather_params.1 = (bf16[8,4,816,128]{3,2,1,0:T(8,128)(2,1)}, bf16[2,2,5,656,768]{4,3,2,1,0:T(8,128)(2,1)}) custom-call(bf16[816,128]{1,0:T(8,128)(2,1)} %pad.20.src, bf16[2,2,656,768]{3,2,1,0:T(8,128)(2,1)} %copy-done, f32[656,128]{1,0:T(8,128)} %get-tuple-element.67.gain, f32[656,128]{1,0:T(8,128)} %get-tuple-element.66.shift), custom_call_target="tpu_custom_call" | custom-call | tf_op jit(solution)/shard_map/gather_params/pallas_call | solution.py:1046
  66.2 0.0 copy-start.8
  66.2 2.3 collective-permute-start
  68.5 1.3 collective-permute-start.1
  69.7 25.3 %unpack.1 = (bf16[2624,768]{1,0:T(8,128)(2,1)}, bf16[656,2624]{1,0:T(8,128)(2,1)}, bf16[656,1408]{1,0:T(8,128)(2,1)}, bf16[1296,656]{1,0:T(8,128)(2,1)}, bf16[12...) custom-call(bf16[32,816,128]{2,1,0:T(8,128)(2,1)} %bitcast.61), custom_call_target="tpu_custom_call" | custom-call | tf_op jit(solution)/shard_map/unpack/pallas_call | solution.py:86
  95.0 0.0 collective-permute-done.lo
  95.0 0.0 collective-permute-done.1.hi
  95.0 4.6 %collective-permute-start.2 = (bf16[1,656,768]{2,1,0:T(8,128)(2,1)S(1)}, bf16[1,656,768]{2,1,0:T(8,128)(2,1)S(1)}, u32[]{:S(2)}, u32[]{:S(2)}) collective-permute-start(bf16[1,656,768]{2,1,0:T(8,128)(2,1)S(1)} %get-tuple-element.40), channel_id=1, source_target_pairs={{0,1},{1,2},{2,3},{4,5},{5,6},{6,7},{8,9},{9,10},{10,11},{12,13},{... | collective-permute-start | bytes 3022856 | tf_op jit(solution)/shard_map/ppermute | solution.py:1214
  99.7 1.7 collective-permute-start.3
  101.3 0.0 copy-done.8
  101.3 0.7 copy.15.offsets
  102.0 2.6 copy.21
  104.6 0.0 copy-start.7
  104.7 2.3 pad.22.clone
  107.6 0.0 copy-done.7
  107.6 0.1 multiply_convert_fusion
  107.7 0.6 reshape.84.mask
  108.3 16.3 %lift.2.refs_0_ = bf16[2,2,2624,768]{3,2,1,0:T(8,128)(2,1)} custom-call(s32[12,2]{1,0:T(8,128)} %copy.15.offsets, s32[12]{0:T(128)} %bases.5, f32[8,12]{1,0:T(8,128)} %psi.5, bf16[1,656,768]{2,1,0:T(8,128)(2,1)} %collective-permute-done.lo, bf16[1,656,768]{2,1,0:T(8,128)(2,1)} %collective-permute-done.1.hi, ...), custom_call_target="tpu_custom_call" | custom-call | flops 41943040 | bytes 41943040 | tf_op jit(solution)/shard_map/lift/pallas_call | solution.py:301
  124.7 0.0 collective-permute-done.2.lo
  124.7 0.0 copy-start.4
  124.7 0.7 collective-permute-done.3.hi
  125.4 0.3 copy-done.4
  125.7 16.2 %lift.3 = bf16[2,2,2624,768]{3,2,1,0:T(8,128)(2,1)} custom-call(s32[12,2]{1,0:T(8,128)} %copy.15.offsets, s32[12]{0:T(128)} %bases.5, f32[8,12]{1,0:T(8,128)} %psi.5, bf16[1,656,768]{2,1,0:T(8,128)(2,1)} %copy-done.4, bf16[1,656,768]{2,1,0:T(8,128)(2,1)} %collective-permute-done.3.hi, ...), custom_call_target="tpu_custom_call", output_to_operand_aliasing={{}: (8, {})} | custom-call | flops 41943040 | bytes 41943040 | tf_op jit(solution)/shard_map/lift/pallas_call | solution.py:301
  141.9 72.5 %block.1 = (bf16[4,656,768]{2,1,0:T(8,128)(2,1)}, bf16[4,656,768]{2,1,0:T(8,128)(2,1)}, f32[656,1408]{1,0:T(8,128)}, f32[1296,768]{1,0:T(8,128)}, f32[2,656,128]{2,1,0:T(8,128)}) custom-call(bf16[4,2624,768]{2,1,0:T(8,128)(2,1)} %bitcast.53, bf16[4,656,768]{2,1,0:T(8,128)(2,1)} %bitcast.55, bf16[4,656,768]{2,1,0:T(8,128)(2,1)} %bitcast.59, ...), custom_call_target="tpu_custom_call" | custom-call | tf_op jit(solution)/shard_map/block/pallas_call | solution.py:582
  214.5 43.3 %lower.1 = (f32[2,2,656,768]{3,2,1,0:T(8,128)}, bf16[2,656,768]{2,1,0:T(8,128)(2,1)}, bf16[2,656,768]{2,1,0:T(8,128)(2,1)}) custom-call(s32[12,2]{1,0:T(8,128)} %copy.15.offsets, s32[12]{0:T(128)} %bases.5, f32[8,12]{1,0:T(8,128)} %psi.5, bf16[2,2,656,768]{3,2,1,0:T(8,128)(2,1)} %bitcast.56, bf16[4,656,768]{2,1,0:T(8,128)(2,1)} %bitcast.62), custom_call_target="tpu_custom_call" | custom-call | tf_op jit(solution)/shard_map/lower/pallas_call | solution.py:772
  257.8 5.8 %collective-permute-start.4 = (bf16[2,656,768]{2,1,0:T(8,128)(2,1)}, bf16[2,656,768]{2,1,0:T(8,128)(2,1)}, u32[]{:S(2)}, u32[]{:S(2)}) collective-permute-start(bf16[2,656,768]{2,1,0:T(8,128)(2,1)} %get-tuple-element.46), channel_id=1, source_target_pairs={{0,1},{1,2},{2,3},{4,5},{5,6},{6,7},{8,9},{9,10},{10,11},{12,13},{... | collective-permute-start | bytes 6045704 | tf_op jit(solution)/shard_map/ppermute | solution.py:1229
  263.6 0.0 copy-start.3
  263.6 1.5 collective-permute-start.5
  265.2 21.9 %weight_grad.1.gd_ref = f32[2624,768]{1,0:T(8,128)} custom-call(bf16[4,2624,768]{2,1,0:T(8,128)(2,1)} %bitcast.54, bf16[4,656,768]{2,1,0:T(8,128)(2,1)} %get-tuple-element.44.gconv), custom_call_target="tpu_custom_call" | custom-call | tf_op jit(solution)/shard_map/weight_grad/pallas_call | solution.py:621
  287.1 0.0 copy-done.3
  287.1 0.3 slice.92
  287.3 5.0 %copy.25 = bf16[2,2,641,720]{3,1,2,0:T(2,128)(2,1)} copy(bf16[2,2,641,720]{3,2,1,0:T(8,128)(2,1)S(1)} %slice.92) | data formatting | bytes 7384320
  292.3 23.7 %pack.1 = bf16[32,816,128]{2,1,0:T(8,128)(2,1)} custom-call(f32[2624,768]{1,0:T(8,128)} %weight_grad.1.gd_ref, f32[656,1408]{1,0:T(8,128)} %get-tuple-element.49.gu_ref, f32[1296,768]{1,0:T(8,128)} %get-tuple-element.50.gn_ref), custom_call_target="tpu_custom_call" | custom-call | tf_op jit(solution)/shard_map/pack/pallas_call | solution.py:160
  316.0 0.0 collective-permute-done.4.lo
  316.0 0.0 collective-permute-done.5.hi
  316.1 0.0 copy-start.5
  316.1 15.9 %input_grad.1 = (bf16[2,2,656,768]{3,2,1,0:T(8,128)(2,1)}, f32[2,656,128]{2,1,0:T(8,128)}) custom-call(bf16[2,2,656,768]{3,2,1,0:T(8,128)(2,1)} %copy-done, bf16[2,2,656,768]{3,2,1,0:T(8,128)(2,1)} %bitcast.57, f32[2,2,656,768]{3,2,1,0:T(8,128)} %get-tuple-element.45.own, bf16[2,656,768]{2,1,0:T(8,128)(2,1)} %collective-permute-done.4.lo, ...), custom_call_target="tpu_custom_call" | custom-call | tf_op jit(solution)/shard_map/input_grad/pallas_call | solution.py:834
  332.0 0.0 copy-done.5
  332.0 1.6 maximum_reduce_fusion
  333.6 0.1 concatenate.12
  333.7 0.8 slice_add_fusion
  334.5 1.3 dynamic_update_slice.3
  335.8 0.0 copy-start.2
  335.8 48.5 %scatter_grads.1 = f32[816,128]{1,0:T(8,128)} custom-call(bf16[8,4,816,128]{3,2,1,0:T(8,128)(2,1)} %bitcast.58), custom_call_target="tpu_custom_call" | custom-call | tf_op jit(solution)/shard_map/scatter_grads/pallas_call | solution.py:1149
  384.3 1.8 slice_bitcast_fusion.5
  386.1 0.0 copy-done.2
  386.1 0.3 slice_bitcast_fusion
  386.4 5.0 %copy.19 = bf16[1,2,2,720,641]{3,2,4,1,0:T(2,128)(2,1)} copy(bf16[1,2,2,720,641]{3,4,2,1,0:T(8,128)(2,1)S(1)} %slice_bitcast_fusion) | data formatting | bytes 7384320
  (4 shorter events, 0.1 us)
Async XLA Ops:
  0.6 17.0 %copy-start.1 = (bf16[1,2,2,720,641]{3,2,4,1,0:T(2,128)(2,1)S(1)}, bf16[1,2,2,720,641]{3,2,4,1,0:T(2,128)(2,1)}, u32[]{:S(2)}) copy-start(bf16[1,2,2,720,641]{3,2,4,1,0:T(2,128)(2,1)} %param.9) | copy-start | bytes 11076484
  17.6 0.8 copy-start.6
  19.3 2.2 copy-start
  66.2 35.2 %copy-start.8 = (s32[12,2]{0,1:T(2,128)S(1)}, s32[12,2]{0,1:T(2,128)}, u32[]{:S(2)}) copy-start(s32[12,2]{0,1:T(2,128)} %param.16) | copy-start | bytes 292
  66.2 28.8 %collective-permute-start = (bf16[1,656,768]{2,1,0:T(8,128)(2,1)}, bf16[1,656,768]{2,1,0:T(8,128)(2,1)}, u32[]{:S(2)}, u32[]{:S(2)}) collective-permute-start(bf16[1,656,768]{2,1,0:T(8,128)(2,1)} %get-tuple-element.32), channel_id=1, source_target_pairs={{0,1},{1,2},{2,3},{4,5},{5,6},{6,7},{8,9},{9,10},{10,11},{12,13},{... | collective-permute-start | bytes 3022856 | tf_op jit(solution)/shard_map/ppermute | solution.py:1214
  68.5 26.6 %collective-permute-start.1 = (bf16[1,656,768]{2,1,0:T(8,128)(2,1)S(1)}, bf16[1,656,768]{2,1,0:T(8,128)(2,1)}, u32[]{:S(2)}, u32[]{:S(2)}) collective-permute-start(bf16[1,656,768]{2,1,0:T(8,128)(2,1)S(1)} %get-tuple-element.33), channel_id=1, source_target_pairs={{1,0},{2,1},{3,2},{5,4},{6,5},{7,6},{9,8},{10,9},{11,10},{13,12},{... | collective-permute-start | bytes 3022856 | tf_op jit(solution)/shard_map/ppermute | solution.py:1214
  95.0 29.7 %collective-permute-start.2 = (bf16[1,656,768]{2,1,0:T(8,128)(2,1)S(1)}, bf16[1,656,768]{2,1,0:T(8,128)(2,1)S(1)}, u32[]{:S(2)}, u32[]{:S(2)}) collective-permute-start(bf16[1,656,768]{2,1,0:T(8,128)(2,1)S(1)} %get-tuple-element.40), channel_id=1, source_target_pairs={{0,1},{1,2},{2,3},{4,5},{5,6},{6,7},{8,9},{9,10},{10,11},{12,13},{... | collective-permute-start | bytes 3022856 | tf_op jit(solution)/shard_map/ppermute | solution.py:1214
  99.7 25.8 %collective-permute-start.3 = (bf16[1,656,768]{2,1,0:T(8,128)(2,1)S(1)}, bf16[1,656,768]{2,1,0:T(8,128)(2,1)}, u32[]{:S(2)}, u32[]{:S(2)}) collective-permute-start(bf16[1,656,768]{2,1,0:T(8,128)(2,1)S(1)} %get-tuple-element.41), channel_id=1, source_target_pairs={{1,0},{2,1},{3,2},{5,4},{6,5},{7,6},{9,8},{10,9},{11,10},{13,12},{... | collective-permute-start | bytes 3022856 | tf_op jit(solution)/shard_map/ppermute | solution.py:1214
  104.6 3.0 copy-start.7
  124.7 1.0 copy-start.4
  257.8 58.3 %collective-permute-start.4 = (bf16[2,656,768]{2,1,0:T(8,128)(2,1)}, bf16[2,656,768]{2,1,0:T(8,128)(2,1)}, u32[]{:S(2)}, u32[]{:S(2)}) collective-permute-start(bf16[2,656,768]{2,1,0:T(8,128)(2,1)} %get-tuple-element.46), channel_id=1, source_target_pairs={{0,1},{1,2},{2,3},{4,5},{5,6},{6,7},{8,9},{9,10},{10,11},{12,13},{... | collective-permute-start | bytes 6045704 | tf_op jit(solution)/shard_map/ppermute | solution.py:1229
  263.6 23.5 %copy-start.3 = (bf16[4,656,768]{2,1,0:T(8,128)(2,1)S(1)}, bf16[4,656,768]{2,1,0:T(8,128)(2,1)}, u32[]{:S(2)}) copy-start(bf16[4,656,768]{2,1,0:T(8,128)(2,1)} %get-tuple-element.43) | copy-start | bytes 12091396
  263.6 52.4 %collective-permute-start.5 = (bf16[2,656,768]{2,1,0:T(8,128)(2,1)}, bf16[2,656,768]{2,1,0:T(8,128)(2,1)}, u32[]{:S(2)}, u32[]{:S(2)}) collective-permute-start(bf16[2,656,768]{2,1,0:T(8,128)(2,1)} %get-tuple-element.47), channel_id=1, source_target_pairs={{1,0},{2,1},{3,2},{5,4},{6,5},{7,6},{9,8},{10,9},{11,10},{13,12},{... | collective-permute-start | bytes 6045704 | tf_op jit(solution)/shard_map/ppermute | solution.py:1230
  316.1 15.9 %copy-start.5 = (f32[2,656,128]{2,1,0:T(8,128)S(1)}, f32[2,656,128]{2,1,0:T(8,128)}, u32[]{:S(2)}) copy-start(f32[2,656,128]{2,1,0:T(8,128)} %get-tuple-element.52) | copy-start | bytes 2015236
  335.8 50.3 %copy-start.2 = (bf16[2,2,656,768]{3,2,1,0:T(8,128)(2,1)S(1)}, bf16[2,2,656,768]{3,2,1,0:T(8,128)(2,1)}, u32[]{:S(2)}) copy-start(bf16[2,2,656,768]{3,2,1,0:T(8,128)(2,1)} %get-tuple-element.48) | copy-start | bytes 12091396

commit v5 on v4

--- a/solution.py
+++ b/solution.py
@@ -23,6 +23,7 @@
 WIDE = 768
 HL = 1408
 UNROLL = 8
+ASIDE = 2
 VMEM = 60 << 20
 
 
@@ -34,6 +35,27 @@
 def place(base,cols,period,b):
     start=base+cols*b
     return start//LANES, start%LANES
+def rolled(values, amount):
+    out = []
+    for n in range(0, len(values), 2):
+        pieces = values[n : n + 2]
+        if len(pieces) == 2:
+            both = jnp.concatenate(pieces, axis=0).astype(BF16)
+            both = pltpu.roll(both, amount, axis=1).astype(F32)
+            out += [both[:8], both[8:]]
+        else:
+            out.append(pltpu.roll(pieces[0].astype(BF16).astype(F32), amount, axis=1))
+    return out
+
+
+def flatten(lists):
+    return [value for values in lists for value in values]
+
+
+def unflat(values, width):
+    return [values[n : n + width] for n in range(0, len(values), width)]
+
+
 def unpack_kernel(nrow,pad, g_ref, w_ref,wt_ref,up_ref,upt_ref,dn_ref,dnt_ref,flat,chunks):
     def fill(s,_):
         flat[pl.ds(nrow*s,pad),:]=g_ref[s].astype(F32); return 0
@@ -44,10 +66,11 @@
         def body(b,_):
             row,s=place(base,cols,period,b)
             back=(LANES-s)%LANES
+            found=[[flat[pl.ds(row+641*8*g+j,8,stride=641),:] for g in range(groups)] for j in range(J+1)]
+            found=unflat(rolled(flatten(found),back),groups)
             for g in range(groups):
-                rolled=[pltpu.roll(flat[pl.ds(row+641*8*g+j,8,stride=641),:],back,axis=1) for j in range(J+1)]
                 for j in range(J):
-                    val=jnp.where(lane<LANES-s,rolled[j],rolled[j+1])
+                    val=jnp.where(lane<LANES-s,found[j][g],found[j+1][g])
                     if j==J-1: val=jnp.where(lane<last,val,0.0)
                     chunks[pl.ds(j*height+8*g*pitch+b,8,stride=pitch),:]=val
             return 0
@@ -122,8 +145,10 @@
         def body(b,tails,rows=J):
             row,s=place(base,cols,period,b)
             new=[]
+            found=[chunks[pl.ds(j*height+8*g*pitch+b,8,stride=pitch),:] for g in range(groups) for j in range(J)]
+            found=unflat(rolled(found,s),J)
             for g in range(groups):
-                x=[pltpu.roll(chunks[pl.ds(j*height+8*g*pitch+b,8,stride=pitch),:],s,axis=1) for j in range(J)]
+                x=found[g]
                 first=lane>=s
                 for j in range(J):
                     v=jnp.where(first,x[j],tails[g] if j==0 else x[j-1])
@@ -787,63 +812,80 @@
     )(offsets, bases, psi, gconv, w.reshape(BASIS, CP, WIDE))
 
 
-def input_kernel(rows, width, x, gconv, own, lo, hi, gain, out, sums, total):
-    r = pl.program_id(1)
-
-    @pl.when(jnp.logical_and(pl.program_id(0) == 0, r == 0))
-    def _():
-        sums[...] = jnp.zeros_like(sums)
-
-    from_below = jnp.where(r == 0, 1.0, 0.0)
-    from_above = jnp.where(r == rows - 1, 1.0, 0.0)
-
-    def read(c):
-        return x[0, 0, pl.ds(pl.multiple_of(c * STEP, STEP), STEP), :].astype(F32)
-
-    mean, scale = norm_stats(read, CIN)
-
-    def join(c, at):
-        halo = lo[0, at, :].astype(F32) * from_below + hi[0, at, :].astype(F32) * from_above
-        total[at, :] = own[0, 0, at, :] + halo
-
-    each_chunk(join, 4)
-
-    def means(c):
-        at = pl.ds(pl.multiple_of(c * STEP, STEP), STEP)
-        g = total[at, :] * tiled(gain[at, :])
-        return g, g * ((read(c) - mean) * scale)
-
-    flat, along = [v * (1.0 / CIN) for v in column_sums(means, CIN, 2)]
-
-    def backward(c, at):
-        dm = cut(total[at, :], width)
-        xhat = (read(c) - mean) * scale
-        g = dm * tiled(gain[at, :])
-        value = scale * (g - flat - xhat * along) + gconv[0, 0, at, :].astype(F32)
-        out[0, 0, at, :] = value.astype(BF16)
-        along_lanes(sums.at[0], at, dm * xhat)
-        along_lanes(sums.at[1], at, dm)
-
-    each_chunk(backward, 8)
-
-
-def input_grad(x, gconv, own, lo, hi, gain, width):
-    slabs, rows = x.shape[:2]
-    per_row = pl.BlockSpec((1, 1, CP, WIDE), lambda s, r: (s, r, 0, 0))
-    halo = pl.BlockSpec((1, CP, WIDE), lambda s, r: (s, 0, 0))
-    return pl.pallas_call(
-        functools.partial(input_kernel, rows, width),
-        grid=(slabs, rows),
-        in_specs=[per_row, per_row, per_row, halo, halo, pl.BlockSpec((CP, LANES), lambda s, r: (0, 0))],
-        out_specs=[per_row, pl.BlockSpec((2, CP, LANES), lambda s, r: (0, 0, 0))],
-        out_shape=(
-            jax.ShapeDtypeStruct((slabs, rows, CP, WIDE), BF16),
-            jax.ShapeDtypeStruct((2, CP, LANES), F32),
-        ),
-        scratch_shapes=[pltpu.VMEM((CP, WIDE), F32)],
-        compiler_params=pltpu.CompilerParams(vmem_limit_bytes=VMEM),
-        name="input_grad",
-    )(x, gconv, own, lo, hi, gain)
+def input_rows(width, x, gconv, own, lo, hi, gain, grad, sums, buffers, in_sems, out_sems):
+    rows = x.shape[1]
+    places = [(s, r) for s in range(x.shape[0]) for r in range(rows)]
+    saves = []
+
+    def loads(n):
+        s, r = places[n]
+        sources = [x.at[s, r], gconv.at[s, r], own.at[s, r]]
+        sources += [lo.at[s]] if r == 0 else []
+        sources += [hi.at[s]] if r == rows - 1 else []
+        slots = [0, 1, 2] + ([3] if r == 0 else []) + ([4] if r == rows - 1 else [])
+        return [
+            pltpu.make_async_copy(source, buffers[n % 2][slot], in_sems.at[n % 2, slot])
+            for source, slot in zip(sources, slots)
+        ]
+
+    flying = loads(0)
+    for copy in flying:
+        copy.start()
+    sums[...] = jnp.zeros_like(sums)
+    for n, (s, r) in enumerate(places):
+        for copy in flying:
+            copy.wait()
+        if n + 1 < len(places):
+            flying = loads(n + 1)
+            for copy in flying:
+                copy.start()
+        here, conv, total, below, above, result = buffers[n % 2]
+
+        def read(c):
+            return here[pl.ds(pl.multiple_of(c * STEP, STEP), STEP), :].astype(F32)
+
+        mean, scale = norm_stats(read, CIN)
+        yield
+
+        if r == 0 or r == rows - 1:
+
+            def join(c, at):
+                value = total[at, :]
+                if r == 0:
+                    value = value + below[at, :].astype(F32)
+                if r == rows - 1:
+                    value = value + above[at, :].astype(F32)
+                total[at, :] = value
+
+            each_chunk(join, 8)
+            yield
+
+        def means(c):
+            at = pl.ds(pl.multiple_of(c * STEP, STEP), STEP)
+            g = total[at, :] * tiled(gain[at, :])
+            return g, g * ((read(c) - mean) * scale)
+
+        flat, along = [v * (1.0 / CIN) for v in column_sums(means, CIN, 2)]
+        yield
+        if n >= 2:
+            saves[n - 2].wait()
+
+        def backward(c, at):
+            dm = cut(total[at, :], width)
+            xhat = (read(c) - mean) * scale
+            g = dm * tiled(gain[at, :])
+            value = scale * (g - flat - xhat * along) + conv[at, :].astype(F32)
+            result[at, :] = value.astype(BF16)
+            along_lanes(sums.at[0], at, dm * xhat)
+            along_lanes(sums.at[1], at, dm)
+
+        each_chunk(backward, 8)
+        save = pltpu.make_async_copy(result, grad.at[s, r], out_sems.at[n % 2])
+        save.start()
+        saves.append(save)
+        yield
+    for save in saves[-2:]:
+        save.wait()
 
 
 def flip(value, bit):
@@ -876,51 +918,35 @@
     return pl.ds(0, cut), pl.ds(cut, rows - cut)
 
 
-def greet(dates, lats, d, l):
+def greet(dates, lats, d, l, owner):
     barrier = pltpu.get_barrier_semaphore()
-    count = 0
-    for o in range(1, lats):
-        pl.semaphore_signal(barrier, inc=1, device_id=(d, lax.rem(l + o, lats)), device_id_type=MESH)
-        count += 1
-    for b in range(dates.bit_length() - 1):
-        pl.semaphore_signal(barrier, inc=1, device_id=(flip(d, b), l), device_id_type=MESH)
-        count += 1
-    pl.semaphore_wait(barrier, count)
-
-
-def norms_kernel(dates, lats, owner, first, src, out, landed, local_sem, send, recv):
-    d, l = lax.axis_index("date"), lax.axis_index("lat")
+    bits = range(dates.bit_length() - 1)
+    peers = [(d, lax.rem(l + o, lats)) for o in range(1, lats)] + [(flip(d, b), l) for b in bits]
+    for peer in peers:
+        pl.semaphore_signal(barrier, inc=1, device_id=peer, device_id_type=MESH)
+    next_to = [(owner[0], b) for b in range(lats) if b != owner[1]] + [(flip(owner[0], b), owner[1]) for b in bits]
+    away = [(a, b) for a in range(dates) for b in range(lats) if (a, b) not in next_to + [owner]]
     mine = jnp.logical_and(d == owner[0], l == owner[1])
-    barrier = pltpu.get_barrier_semaphore()
-    others = [(a, b) for a in range(dates) for b in range(lats) if (a, b) != owner]
-
-    def copy_to(n):
-        return pltpu.make_async_remote_copy(
-            src_ref=src,
-            dst_ref=landed,
-            send_sem=send.at[n],
-            recv_sem=recv,
-            device_id=others[n],
-            device_id_type=MESH,
-        )
+    near = functools.reduce(jnp.logical_or, [jnp.logical_and(d == a, l == b) for a, b in next_to])
+    far = jnp.logical_not(jnp.logical_or(mine, near))
 
     @pl.when(mine)
     def _():
-        pl.semaphore_wait(barrier, len(others))
-        copies = [copy_to(n) for n in range(len(others))]
-        for copy in copies:
-            copy.start()
-        own = pltpu.make_async_copy(src, landed, local_sem)
-        own.start()
-        own.wait()
-        for copy in copies:
-            copy.wait_send()
-
-    @pl.when(jnp.logical_not(mine))
+        for peer in away:
+            pl.semaphore_signal(barrier, inc=1, device_id=peer, device_id_type=MESH)
+        pl.semaphore_wait(barrier, len(peers) + len(away))
+
+    @pl.when(near)
+    def _():
+        pl.semaphore_wait(barrier, len(peers))
+
+    @pl.when(far)
     def _():
         pl.semaphore_signal(barrier, inc=1, device_id=owner, device_id_type=MESH)
-        copy_to(0).wait_recv()
-
+        pl.semaphore_wait(barrier, len(peers) + 1)
+
+
+def read_norms(landed, first, out):
     lane = lane_ids()
     sub = lax.broadcasted_iota(jnp.int32, (8, LANES), 0)
     lines = landed[...].astype(F32)
@@ -934,37 +960,45 @@
             out[i, j * LANES : j * LANES + rows, :] = jnp.broadcast_to(t[:rows, j : j + 1], (rows, LANES))
 
 
-def norms(shard, lines, dates, lats):
+def norm_home(lines, lats):
     start, end = OFF_G1 // LANES, (OFF_UP - 1) // LANES + 3
     owner = start // lines
     row = (start - owner * lines) // STEP * STEP
     count = -(-(end - owner * lines - row) // STEP) * STEP
-    assert row + count <= shard.shape[0]
-    return pl.pallas_call(
-        functools.partial(norms_kernel, dates, lats, divmod(owner, lats), owner * lines + row),
-        in_specs=[pl.BlockSpec(memory_space=pltpu.VMEM)],
-        out_specs=pl.BlockSpec(memory_space=pltpu.VMEM),
-        out_shape=jax.ShapeDtypeStruct((4, CP, LANES), F32),
-        scratch_shapes=[
-            pltpu.VMEM((count, LANES), BF16),
-            pltpu.SemaphoreType.DMA(()),
-            pltpu.SemaphoreType.DMA((dates * lats - 1,)),
-            pltpu.SemaphoreType.DMA(()),
-        ],
-        compiler_params=pltpu.CompilerParams(
-            collective_id=0, has_side_effects=True, vmem_limit_bytes=VMEM
-        ),
-        name="norms",
-    )(lax.slice_in_dim(shard, row, row + count, axis=0))
+    assert row + count <= -(-lines // STEP) * STEP
+    return divmod(owner, lats), owner * lines + row, row, count
 
 
 def gather_kernel(
-    dates, lats, width, src, x, gain, shift, out, moved, local_sem, z_send, z_recv, send, recv, buffers, buffer_sems
+    dates, lats, lines, width, src, x, out, moved, small, local_sem, z_send, z_recv, send, recv,
+    buffers, buffer_sems, landed, norm_sem, norm_send, norm_recv,
 ):
     d, l = lax.axis_index("date"), lax.axis_index("lat")
     steps = dates.bit_length() - 1
     parts = pieces(src.shape[0])
-    greet(dates, lats, d, l)
+    owner, first, row, count = norm_home(lines, lats)
+    mine = jnp.logical_and(d == owner[0], l == owner[1])
+    others = [(a, b) for a in range(dates) for b in range(lats) if (a, b) != owner]
+    window = src.at[pl.ds(row, count)]
+
+    greet(dates, lats, d, l, owner)
+
+    def norms_to(n):
+        return pltpu.make_async_remote_copy(
+            src_ref=window,
+            dst_ref=landed,
+            send_sem=norm_send.at[n],
+            recv_sem=norm_recv,
+            device_id=others[n],
+            device_id_type=MESH,
+        )
+
+    @pl.when(mine)
+    def _():
+        for n in range(len(others)):
+            norms_to(n).start()
+        pltpu.make_async_copy(window, landed, norm_sem).start()
+
     own = pltpu.make_async_copy(src, out.at[d, l], local_sem)
     own.start()
     sent, arriving, flights = [], {}, {}
@@ -1002,10 +1036,19 @@
     saves = []
 
     def spread_rows():
+        @pl.when(mine)
+        def _():
+            pltpu.make_async_copy(window, landed, norm_sem).wait()
+
+        @pl.when(jnp.logical_not(mine))
+        def _():
+            norms_to(0).wait_recv()
+
+        read_norms(landed, first, small)
         for n, (s, r) in enumerate(rows):
             if n >= 2:
                 saves[n - 2].wait()
-            spread(x.at[s, r], gain, shift, width, buffers.at[n % 2])
+            spread(x.at[s, r], small.at[0], small.at[1], width, buffers.at[n % 2])
             save = pltpu.make_async_copy(buffers.at[n % 2], moved.at[s, r], buffer_sems.at[n % 2])
             save.start()
             saves.append(save)
@@ -1038,18 +1081,24 @@
     for copy in sent:
         copy.wait_send()
 
-
-def gather(shard, x, gain, shift, dates, lats, width):
+    @pl.when(mine)
+    def _():
+        for n in range(len(others)):
+            norms_to(n).wait_send()
+
+
+def gather(shard, x, lines, dates, lats, width):
     slots = dates - 1
     moved = x.shape[:2] + (2 * REACH + 1,) + x.shape[2:]
     anywhere = pl.BlockSpec(memory_space=pl.ANY)
     return pl.pallas_call(
-        functools.partial(gather_kernel, dates, lats, width),
-        in_specs=[anywhere] + [pl.BlockSpec(memory_space=pltpu.VMEM)] * 3,
-        out_specs=[anywhere, anywhere],
+        functools.partial(gather_kernel, dates, lats, lines, width),
+        in_specs=[anywhere, pl.BlockSpec(memory_space=pltpu.VMEM)],
+        out_specs=[anywhere, anywhere, pl.BlockSpec(memory_space=pltpu.VMEM)],
         out_shape=(
             jax.ShapeDtypeStruct((dates, lats) + shard.shape, shard.dtype),
             jax.ShapeDtypeStruct(moved, BF16),
+            jax.ShapeDtypeStruct((4, CP, LANES), F32),
         ),
         scratch_shapes=[
             pltpu.SemaphoreType.DMA(()),
@@ -1059,21 +1108,67 @@
             pltpu.SemaphoreType.DMA((lats, 2, slots)),
             pltpu.VMEM((2,) + moved[2:], BF16),
             pltpu.SemaphoreType.DMA((2,)),
+            pltpu.VMEM((norm_home(lines, lats)[3], LANES), BF16),
+            pltpu.SemaphoreType.DMA(()),
+            pltpu.SemaphoreType.DMA((dates * lats - 1,)),
+            pltpu.SemaphoreType.DMA(()),
         ],
         compiler_params=pltpu.CompilerParams(
             collective_id=2, has_side_effects=True, vmem_limit_bytes=VMEM
         ),
         name="gather_params",
-    )(shard, x, gain, shift)
-
-
-def scatter_kernel(dates, lats, src, out, sums, others, z_send, z_recv, send, recv):
+    )(shard, x)
+
+
+def vector_rows(sums, tiny, first):
+    lane = lane_ids()
+    sub = lax.broadcasted_iota(jnp.int32, (8, LANES), 0)
+    tiny[...] = jnp.zeros_like(tiny)
+    for n, (off, channels) in enumerate(SMALL):
+        lines = []
+        for j in range(6):
+            height = min(LANES, CP - j * LANES)
+            block = sums[n // 2][n % 2, j * LANES : j * LANES + height, :]
+            if height < LANES:
+                block = jnp.concatenate([block, jnp.zeros((LANES - height, LANES), F32)], axis=0)
+            lines.append(jnp.sum(block.T, axis=0, keepdims=True))
+        lines = jnp.concatenate(lines + [jnp.zeros((2, LANES), F32)], axis=0)
+        lines = jnp.where(sub * LANES + lane < channels, lines, 0.0)
+        row, s = divmod(off - first * LANES, LANES)
+        r = pltpu.roll(lines, s, axis=1)
+        moved = jnp.where(lane >= s, r, jnp.where(sub == 0, 0.0, pltpu.roll(r, 1, axis=0)))
+        tiny[row : row + 8, :] = tiny[row : row + 8, :] + moved
+
+
+def vector_home(lines, lats):
+    start, end = OFF_G1 // LANES, (OFF_UP - 1) // LANES + 1
+    owner = start // lines
+    row = (start - owner * lines) // 8 * 8
+    count = -(-(end + 8 - owner * lines - row) // 8) * 8
+    assert end <= (owner + 1) * lines
+    return divmod(owner, lats), owner * lines + row, row, count
+
+
+def scatter_kernel(
+    dates, lats, lines, width, src, x, gconv, own, lo, hi, gain, second_sums, out, grad,
+    sums, others, z_send, z_recv, send, recv, first_sums, tiny, landed, tiny_send, tiny_recv,
+    in_sems, out_sems, *row_buffers
+):
     d, l = lax.axis_index("date"), lax.axis_index("lat")
     steps = dates.bit_length() - 1
     paths = [order[::-1] for order in orders(dates)]
     parts = pieces(src.shape[2])
-    greet(dates, lats, d, l)
+    owner, first, row, count = vector_home(lines, lats)
+    mine = jnp.logical_and(d == owner[0], l == owner[1])
+    senders = [(a, b) for a in range(dates) for b in range(lats) if (a, b) != owner]
+
+    greet(dates, lats, d, l, owner)
     sent, flights, z = [], {}, {}
+    half = len(row_buffers) // 2
+    aside = input_rows(
+        width, x, gconv, own, lo, hi, gain, grad, first_sums,
+        [row_buffers[:half], row_buffers[half:]], in_sems, out_sems,
+    )
 
     def left(p, i):
         return span(paths[p][i + 1 :][::-1])[::-1]
@@ -1130,27 +1225,65 @@
     for wave in range(lats + steps - 1):
         for i in range(steps):
             if 0 <= wave - i < lats:
+                if i:
+                    for _ in range(ASIDE):
+                        next(aside, None)
                 for n in range(len(left(0, i))):
                     for p in range(2):
                         add(turns[wave - i], p, i, n)
+    for _ in aside:
+        pass
+    vector_rows((first_sums, second_sums), tiny, first)
+
+    def to_owner(n):
+        return pltpu.make_async_remote_copy(
+            src_ref=tiny,
+            dst_ref=landed.at[n],
+            send_sem=tiny_send,
+            recv_sem=tiny_recv.at[n],
+            device_id=owner,
+            device_id_type=MESH,
+        )
+
+    @pl.when(jnp.logical_not(mine))
+    def _():
+        to_owner(d * lats + l).start()
+
     for p in range(2):
         total = sums[0, slot_of(steps - 1, 0), parts[p]].astype(F32)
         for o in range(1, lats):
             z[o, p].wait_recv()
             total = total + others[o - 1, parts[p]].astype(F32)
         out[parts[p]] = total
+
+    @pl.when(mine)
+    def _():
+        total = tiny[...]
+        for a, b in senders:
+            to_owner(a * lats + b).wait_recv()
+            total = total + landed[a * lats + b]
+        out[row : row + count, :] = out[row : row + count, :] + total
+
+    @pl.when(jnp.logical_not(mine))
+    def _():
+        to_owner(d * lats + l).wait_send()
+
     for copy in sent:
         copy.wait_send()
 
 
-def scatter(packed):
+def scatter(packed, lines, x, gconv, own, lo, hi, gain, second_sums, width):
     dates, lats, rows, lanes = packed.shape
     slots = dates - 1
+    tiny = (vector_home(lines, lats)[3], LANES)
+    anywhere, held = pl.BlockSpec(memory_space=pl.ANY), pl.BlockSpec(memory_space=pltpu.VMEM)
+    low = pltpu.VMEM((CP, WIDE), BF16)
+    row_buffers = [low, low, pltpu.VMEM((CP, WIDE), F32), low, low, low]
     return pl.pallas_call(
-        functools.partial(scatter_kernel, dates, lats),
-        in_specs=[pl.BlockSpec(memory_space=pltpu.VMEM)],
-        out_specs=pl.BlockSpec(memory_space=pltpu.VMEM),
-        out_shape=jax.ShapeDtypeStruct((rows, lanes), F32),
+        functools.partial(scatter_kernel, dates, lats, lines, width),
+        in_specs=[held] + [anywhere] * 5 + [held] * 2,
+        out_specs=[held, anywhere],
+        out_shape=(jax.ShapeDtypeStruct((rows, lanes), F32), jax.ShapeDtypeStruct(x.shape, BF16)),
         scratch_shapes=[
             pltpu.VMEM((lats, slots, rows, lanes), BF16),
             pltpu.VMEM((lats - 1, rows, lanes), BF16),
@@ -1158,26 +1291,20 @@
             pltpu.SemaphoreType.DMA((lats - 1, 2)),
             pltpu.SemaphoreType.DMA((lats, 2, slots)),
             pltpu.SemaphoreType.DMA((lats, 2, slots)),
-        ],
+            pltpu.VMEM((2, CP, LANES), F32),
+            pltpu.VMEM(tiny, F32),
+            pltpu.VMEM((dates * lats,) + tiny, F32),
+            pltpu.SemaphoreType.DMA(()),
+            pltpu.SemaphoreType.DMA((dates * lats,)),
+            pltpu.SemaphoreType.DMA((2, 5)),
+            pltpu.SemaphoreType.DMA((2,)),
+        ]
+        + row_buffers * 2,
         compiler_params=pltpu.CompilerParams(
             collective_id=1, has_side_effects=True, vmem_limit_bytes=VMEM
         ),
         name="scatter_grads",
-    )(packed)
-
-
-def add_vectors(packed, vectors, lines):
-    first, lead = divmod(OFF_G1, LANES)
-    count = -(-(lead + vectors.shape[0]) // LANES)
-    extra = jnp.pad(vectors, (lead, count * LANES - lead - vectors.shape[0])).reshape(count, LANES)
-    done = 0
-    while done < count:
-        shard, row = divmod(first + done, lines)
-        amount = min(count - done, lines - row)
-        old = lax.slice(packed, (shard, row, 0), (shard + 1, row + amount, LANES))
-        packed = lax.dynamic_update_slice(packed, old + extra[None, done : done + amount], (shard, row, 0))
-        done += amount
-    return packed
+    )(packed, x, gconv, own, lo, hi, gain, second_sums)
 
 
 def local(inputs, noise, cotangent, params, psi, step_counts, pixel_mask, offsets, bases):
@@ -1197,11 +1324,9 @@
     lines = params.shape[0] // LANES
     held = -(-lines // STEP) * STEP
     shard = jnp.pad(params.reshape(lines, LANES), ((0, held - lines), (0, 0)))
-    small = norms(shard, lines, dates, lats)
-    shard, inputs, small = lax.optimization_barrier((shard, inputs, small))
     x = padded(jnp.concatenate([by_channel(inputs), by_channel(noise)], axis=2))
     edges = [(x[s, rows - 1 :], x[s, :1]) for s in range(slabs)]
-    gathered, moved = gather(shard, x, small[0], small[1], dates, lats, width)
+    gathered, moved, small = gather(shard, x, lines, dates, lats, width)
     gathered = gathered.reshape(dates * lats, held, LANES)
     cot = padded(by_channel(cotangent)).reshape(slabs * rows, CP, WIDE)
     active = jnp.arange(steps, dtype=jnp.int32)[None, :] < step_counts[:, None]
@@ -1230,11 +1355,10 @@
     from_above = lax.ppermute(to_below, "lat", downward)
     gdisco = weight_grad(basis, gconv)
     packed = pack(gdisco, gup, gdn, dates * lats, lines, held)
-    grad, first_sums = input_grad(x, gconv_rows, own, from_below, from_above, small[0], width)
-    sums = jnp.sum(jnp.concatenate([first_sums, second_sums]), axis=-1)
-    vectors = jnp.concatenate([sums[0, :CIN], sums[1, :CIN], sums[2, :C], sums[3, :C]])
-    packed = add_vectors(packed, vectors.astype(BF16), lines)
-    summed = scatter(packed.reshape(dates, lats, held, LANES))
+    summed, grad = scatter(
+        packed.reshape(dates, lats, held, LANES), lines,
+        x, gconv_rows, own, from_below, from_above, small[0], second_sums, width,
+    )
 
     def by_pixel(values):
         values = values.reshape(slabs, rows, CP, WIDE)[:, :, :C, :width]

time: 393 us -> 364 us (0.926)
  Pallas kernels: 340 us -> 316 us
    pallas_call x4 -> x2, Pallas kernels: 121 us -> 100 us  [the longest x1 50.5 us: gather(): pl.pallas_call(functools.partial(gather_kernel, dates, lats, lines, width...]
    unnamed x22 -> x21, local copies, waits for them, and re-layouts: 14.6 us -> 16.9 us
  transfers between devices with their start and end apart: 6 -> 6, of which waited for: 1 -> 1; matrix products, arithmetic and copies ran while one was open for 3% -> 3% of each run, Pallas kernels for 22% -> 23%
where the time goes in v5:
time: 364 us
  Pallas kernels  316 us (87%)
  local copies, waits for them, and re-layouts  26.3 us (7%)
  starting transfers between devices  17.1 us (5%)
    pallas_call x1, Pallas kernels, block(): pl.pallas_call(block_kernel, in_specs=[anywhere] * 3 + [held] * 8, out_sp...  72.7 us
    pallas_call x1, Pallas kernels, gather(): pl.pallas_call(functools.partial(gather_kernel, dates, lats, lines, width...  50.5 us
    pallas_call x1, Pallas kernels, scatter(): pl.pallas_call(functools.partial(scatter_kernel, dates, lats, lines, widt...  49.5 us
    pallas_call x1, Pallas kernels, lower(): pl.pallas_call(functools.partial(lower_kernel, rows, width), in_specs=[sm...  42.8 us
    pallas_call x2, Pallas kernels, lift(): pl.pallas_call(functools.partial(lift_kernel, rows, slab, lat, width), gr...  32.4 us
    pallas_call x1, Pallas kernels, unpack(): pl.pallas_call(functools.partial(unpack_kernel, nrow, pad), out_shape=(ja...  24.1 us
    pallas_call x1, Pallas kernels, pack(): pl.pallas_call(functools.partial(pack_kernel, nrow, pad), out_shape=jax.S...  22.2 us
    pallas_call x1, Pallas kernels, weight_grad(): pl.pallas_call(outer_kernel, grid=(count,), in_specs=[pl.BlockSpec((1, BA...  21.9 us
  transfers between devices with their start and end apart: 6, of which 1 were waited for; matrix products, arithmetic and copies ran while one was open for 3% of the time, Pallas kernels for 23%

profile of v5, /device:TPU:4, one launch (start us, length us, event | category | flops | bytes accessed | tf_op | source)
XLA Modules:
  0.0 363.6 jit_solution(7924930911203266401)
XLA Ops:
  0.6 0.0 copy-start.5
  0.6 2.6 copy.24
  3.3 0.0 copy-done.5
  3.3 0.9 fusion.5.x
  4.2 0.0 copy-start
  4.2 0.0 copy-start.4
  4.2 1.2 slice_bitcast_fusion.1
  5.5 1.0 copy-done
  6.5 0.0 copy-done.4
  6.5 0.7 pad.17.src
  7.2 50.5 %gather_params.1 = (bf16[8,4,816,128]{3,2,1,0:T(8,128)(2,1)}, bf16[2,2,5,656,768]{4,3,2,1,0:T(8,128)(2,1)}, f32[4,656,128]{2,1,0:T(8,128)}) custom-call(bf16[816,128]{1,0:T(8,128)(2,1)} %pad.17.src, bf16[2,2,656,768]{3,2,1,0:T(8,128)(2,1)} %copy-done), custom_call_target="tpu_custom_call" | custom-call | tf_op jit(solution)/shard_map/gather_params/pallas_call | solution.py:1094
  57.7 0.0 copy-start.7
  57.7 2.4 collective-permute-start
  60.1 1.3 collective-permute-start.1
  61.3 24.1 %unpack.1 = (bf16[2624,768]{1,0:T(8,128)(2,1)}, bf16[656,2624]{1,0:T(8,128)(2,1)}, bf16[656,1408]{1,0:T(8,128)(2,1)}, bf16[1296,656]{1,0:T(8,128)(2,1)}, bf16[12...) custom-call(bf16[32,816,128]{2,1,0:T(8,128)(2,1)} %bitcast.57), custom_call_target="tpu_custom_call" | custom-call | tf_op jit(solution)/shard_map/unpack/pallas_call | solution.py:109
  85.5 0.0 collective-permute-done.lo
  85.5 1.2 collective-permute-done.1.hi
  86.7 4.4 %collective-permute-start.2 = (bf16[1,656,768]{2,1,0:T(8,128)(2,1)S(1)}, bf16[1,656,768]{2,1,0:T(8,128)(2,1)}, u32[]{:S(2)}, u32[]{:S(2)}) collective-permute-start(bf16[1,656,768]{2,1,0:T(8,128)(2,1)S(1)} %get-tuple-element.35), channel_id=1, source_target_pairs={{0,1},{1,2},{2,3},{4,5},{5,6},{6,7},{8,9},{9,10},{10,11},{12,13},{... | collective-permute-start | bytes 3022856 | tf_op jit(solution)/shard_map/ppermute | solution.py:1339
  91.0 1.7 collective-permute-start.3
  92.7 0.0 copy-done.7
  92.7 0.7 copy.15.offsets
  93.4 2.6 copy.21
  96.0 0.0 copy-start.6
  96.0 0.0 copy-start.2
  96.0 2.3 pad.18.clone
  99.0 0.0 copy-done.6
  99.1 0.1 multiply_convert_fusion
  99.1 0.6 reshape.77.mask
  99.8 0.0 copy-done.2
  99.8 1.1 slice_bitcast_fusion.6
  100.8 16.2 %lift.2.refs_0_ = bf16[2,2,2624,768]{3,2,1,0:T(8,128)(2,1)} custom-call(s32[12,2]{1,0:T(8,128)} %copy.15.offsets, s32[12]{0:T(128)} %bases.5, f32[8,12]{1,0:T(8,128)} %psi.5, bf16[1,656,768]{2,1,0:T(8,128)(2,1)} %collective-permute-done.lo, bf16[1,656,768]{2,1,0:T(8,128)(2,1)} %collective-permute-done.1.hi, ...), custom_call_target="tpu_custom_call" | custom-call | flops 41943040 | bytes 41943040 | tf_op jit(solution)/shard_map/lift/pallas_call | solution.py:326
  117.0 0.0 collective-permute-done.2.lo
  117.1 0.0 collective-permute-done.3.hi
  117.1 16.2 %lift.3 = bf16[2,2,2624,768]{3,2,1,0:T(8,128)(2,1)} custom-call(s32[12,2]{1,0:T(8,128)} %copy.15.offsets, s32[12]{0:T(128)} %bases.5, f32[8,12]{1,0:T(8,128)} %psi.5, bf16[1,656,768]{2,1,0:T(8,128)(2,1)} %collective-permute-done.2.lo, bf16[1,656,768]{2,1,0:T(8,128)(2,1)} %collective-permute-done.3.hi, ...), custom_call_target="tpu_custom_call", output_to_operand_aliasing={{}: (8, {})} | custom-call | flops 41943040 | bytes 41943040 | tf_op jit(solution)/shard_map/lift/pallas_call | solution.py:326
  133.3 72.7 %block.1 = (bf16[4,656,768]{2,1,0:T(8,128)(2,1)}, bf16[4,656,768]{2,1,0:T(8,128)(2,1)}, f32[656,1408]{1,0:T(8,128)}, f32[1296,768]{1,0:T(8,128)}, f32[2,656,128]{2,1,0:T(8,128)}) custom-call(bf16[4,2624,768]{2,1,0:T(8,128)(2,1)} %bitcast.49, bf16[4,656,768]{2,1,0:T(8,128)(2,1)} %bitcast.51, bf16[4,656,768]{2,1,0:T(8,128)(2,1)} %bitcast.55, ...), custom_call_target="tpu_custom_call" | custom-call | tf_op jit(solution)/shard_map/block/pallas_call | solution.py:607
  206.0 42.8 %lower.1 = (f32[2,2,656,768]{3,2,1,0:T(8,128)}, bf16[2,656,768]{2,1,0:T(8,128)(2,1)}, bf16[2,656,768]{2,1,0:T(8,128)(2,1)}) custom-call(s32[12,2]{1,0:T(8,128)} %copy.15.offsets, s32[12]{0:T(128)} %bases.5, f32[8,12]{1,0:T(8,128)} %psi.5, bf16[2,2,656,768]{3,2,1,0:T(8,128)(2,1)} %bitcast.52, bf16[4,656,768]{2,1,0:T(8,128)(2,1)} %bitcast.58), custom_call_target="tpu_custom_call" | custom-call | tf_op jit(solution)/shard_map/lower/pallas_call | solution.py:797
  248.9 5.9 %collective-permute-start.4 = (bf16[2,656,768]{2,1,0:T(8,128)(2,1)}, bf16[2,656,768]{2,1,0:T(8,128)(2,1)}, u32[]{:S(2)}, u32[]{:S(2)}) collective-permute-start(bf16[2,656,768]{2,1,0:T(8,128)(2,1)} %get-tuple-element.44), channel_id=1, source_target_pairs={{0,1},{1,2},{2,3},{4,5},{5,6},{6,7},{8,9},{9,10},{10,11},{12,13},{... | collective-permute-start | bytes 6045704 | tf_op jit(solution)/shard_map/ppermute | solution.py:1354
  254.7 0.0 copy-start.1
  254.7 1.5 collective-permute-start.5
  256.3 21.9 %weight_grad.1.gd_ref = f32[2624,768]{1,0:T(8,128)} custom-call(bf16[4,2624,768]{2,1,0:T(8,128)(2,1)} %bitcast.50, bf16[4,656,768]{2,1,0:T(8,128)(2,1)} %get-tuple-element.40.gconv), custom_call_target="tpu_custom_call" | custom-call | tf_op jit(solution)/shard_map/weight_grad/pallas_call | solution.py:646
  278.2 0.0 copy-done.1
  278.2 0.3 slice.51
  278.5 5.0 %copy.25 = bf16[2,2,641,720]{3,1,2,0:T(2,128)(2,1)} copy(bf16[2,2,641,720]{3,2,1,0:T(8,128)(2,1)S(1)} %slice.51) | data formatting | bytes 7384320
  283.5 22.2 %pack.1 = bf16[32,816,128]{2,1,0:T(8,128)(2,1)} custom-call(f32[2624,768]{1,0:T(8,128)} %weight_grad.1.gd_ref, f32[656,1408]{1,0:T(8,128)} %get-tuple-element.41.gu_ref, f32[1296,768]{1,0:T(8,128)} %get-tuple-element.42.gn_ref), custom_call_target="tpu_custom_call" | custom-call | tf_op jit(solution)/shard_map/pack/pallas_call | solution.py:185
  305.7 0.0 collective-permute-done.4.lo
  305.7 0.0 collective-permute-done.5.hi
  305.7 49.5 %scatter_grads.1 = (f32[816,128]{1,0:T(8,128)}, bf16[2,2,656,768]{3,2,1,0:T(8,128)(2,1)}) custom-call(bf16[8,4,816,128]{3,2,1,0:T(8,128)(2,1)} %bitcast.54, bf16[2,2,656,768]{3,2,1,0:T(8,128)(2,1)} %copy-done, bf16[2,2,656,768]{3,2,1,0:T(8,128)(2,1)} %bitcast.53, f32[2,2,656,768]{3,2,1,0:T(8,128)} %get-tuple-element.43.own, ...), custom_call_target="tpu_custom_call" | custom-call | tf_op jit(solution)/shard_map/scatter_grads/pallas_call | solution.py:1282
  355.2 2.4 slice_bitcast_fusion
  357.6 0.0 copy-start.3
  357.6 5.0 %copy.19 = bf16[1,2,2,720,641]{3,2,4,1,0:T(2,128)(2,1)} copy(bf16[1,2,2,720,641]{3,4,2,1,0:T(8,128)(2,1)S(1)} %slice_bitcast_fusion) | data formatting | bytes 7384320
  362.6 0.0 copy-done.3
  362.6 0.8 slice_bitcast_fusion.5
  (2 shorter events, 0.0 us)
Async XLA Ops:
  0.6 2.7 copy-start.5
  4.2 2.2 copy-start
  4.2 2.2 copy-start.4
  57.7 35.0 %copy-start.7 = (s32[12,2]{0,1:T(2,128)S(1)}, s32[12,2]{0,1:T(2,128)}, u32[]{:S(2)}) copy-start(s32[12,2]{0,1:T(2,128)} %param.16) | copy-start | bytes 292
  57.7 27.8 %collective-permute-start = (bf16[1,656,768]{2,1,0:T(8,128)(2,1)}, bf16[1,656,768]{2,1,0:T(8,128)(2,1)}, u32[]{:S(2)}, u32[]{:S(2)}) collective-permute-start(bf16[1,656,768]{2,1,0:T(8,128)(2,1)} %get-tuple-element.27), channel_id=1, source_target_pairs={{0,1},{1,2},{2,3},{4,5},{5,6},{6,7},{8,9},{9,10},{10,11},{12,13},{... | collective-permute-start | bytes 3022856 | tf_op jit(solution)/shard_map/ppermute | solution.py:1339
  60.1 26.6 %collective-permute-start.1 = (bf16[1,656,768]{2,1,0:T(8,128)(2,1)S(1)}, bf16[1,656,768]{2,1,0:T(8,128)(2,1)}, u32[]{:S(2)}, u32[]{:S(2)}) collective-permute-start(bf16[1,656,768]{2,1,0:T(8,128)(2,1)S(1)} %get-tuple-element.28), channel_id=1, source_target_pairs={{1,0},{2,1},{3,2},{5,4},{6,5},{7,6},{9,8},{10,9},{11,10},{13,12},{... | collective-permute-start | bytes 3022856 | tf_op jit(solution)/shard_map/ppermute | solution.py:1339
  86.7 30.4 %collective-permute-start.2 = (bf16[1,656,768]{2,1,0:T(8,128)(2,1)S(1)}, bf16[1,656,768]{2,1,0:T(8,128)(2,1)}, u32[]{:S(2)}, u32[]{:S(2)}) collective-permute-start(bf16[1,656,768]{2,1,0:T(8,128)(2,1)S(1)} %get-tuple-element.35), channel_id=1, source_target_pairs={{0,1},{1,2},{2,3},{4,5},{5,6},{6,7},{8,9},{9,10},{10,11},{12,13},{... | collective-permute-start | bytes 3022856 | tf_op jit(solution)/shard_map/ppermute | solution.py:1339
  91.0 26.1 %collective-permute-start.3 = (bf16[1,656,768]{2,1,0:T(8,128)(2,1)S(1)}, bf16[1,656,768]{2,1,0:T(8,128)(2,1)}, u32[]{:S(2)}, u32[]{:S(2)}) collective-permute-start(bf16[1,656,768]{2,1,0:T(8,128)(2,1)S(1)} %get-tuple-element.36), channel_id=1, source_target_pairs={{1,0},{2,1},{3,2},{5,4},{6,5},{7,6},{9,8},{10,9},{11,10},{13,12},{... | collective-permute-start | bytes 3022856 | tf_op jit(solution)/shard_map/ppermute | solution.py:1339
  96.0 3.0 copy-start.6
  96.0 3.7 %copy-start.2 = (f32[4,656,128]{2,1,0:T(8,128)S(1)}, f32[4,656,128]{2,1,0:T(8,128)}, u32[]{:S(2)}) copy-start(f32[4,656,128]{2,1,0:T(8,128)} %get-tuple-element.38) | copy-start | bytes 4030468
  248.9 56.8 %collective-permute-start.4 = (bf16[2,656,768]{2,1,0:T(8,128)(2,1)}, bf16[2,656,768]{2,1,0:T(8,128)(2,1)}, u32[]{:S(2)}, u32[]{:S(2)}) collective-permute-start(bf16[2,656,768]{2,1,0:T(8,128)(2,1)} %get-tuple-element.44), channel_id=1, source_target_pairs={{0,1},{1,2},{2,3},{4,5},{5,6},{6,7},{8,9},{9,10},{10,11},{12,13},{... | collective-permute-start | bytes 6045704 | tf_op jit(solution)/shard_map/ppermute | solution.py:1354
  254.7 23.5 %copy-start.1 = (bf16[4,656,768]{2,1,0:T(8,128)(2,1)S(1)}, bf16[4,656,768]{2,1,0:T(8,128)(2,1)}, u32[]{:S(2)}) copy-start(bf16[4,656,768]{2,1,0:T(8,128)(2,1)} %get-tuple-element.39) | copy-start | bytes 12091396
  254.7 51.0 %collective-permute-start.5 = (bf16[2,656,768]{2,1,0:T(8,128)(2,1)}, bf16[2,656,768]{2,1,0:T(8,128)(2,1)}, u32[]{:S(2)}, u32[]{:S(2)}) collective-permute-start(bf16[2,656,768]{2,1,0:T(8,128)(2,1)} %get-tuple-element.45), channel_id=1, source_target_pairs={{1,0},{2,1},{3,2},{5,4},{6,5},{7,6},{9,8},{10,9},{11,10},{13,12},{... | collective-permute-start | bytes 6045704 | tf_op jit(solution)/shard_map/ppermute | solution.py:1355
  357.6 5.0 %copy-start.3 = (f32[816,128]{1,0:T(8,128)S(1)}, f32[816,128]{1,0:T(8,128)}, u32[]{:S(2)}) copy-start(f32[816,128]{1,0:T(8,128)} %get-tuple-element.48) | copy-start | bytes 1253380

commit v6 on v5

--- a/solution.py
+++ b/solution.py
@@ -112,80 +112,210 @@
             jax.ShapeDtypeStruct((HP,WIDE),BF16),jax.ShapeDtypeStruct((CP,HP),BF16)),
         scratch_shapes=[pltpu.VMEM((F_ROWS,LANES),F32),pltpu.VMEM((6*(136*24+8),LANES),F32)],
         compiler_params=pltpu.CompilerParams(vmem_limit_bytes=VMEM),name="unpack")(gathered)
-def pack_kernel(nrow,pad,gd_ref,gu_ref,gn_ref,out_ref,flat,chunks):
-    lane=lane_ids(); sub=lax.broadcasted_iota(jnp.int32,(8,LANES),0)
-    def gather(src,src_row,dst_row,rows,J,height,last,period):
-        full=rows//8
-        def cols(m,j):
-            v=src[pl.ds(pl.multiple_of(src_row+8*m,8),8),j*LANES:(j+1)*LANES]
-            return jnp.where(lane<last,v,0.0) if j==J-1 else v
-        def body(m,_):
-            r=dst_row+8*m; at=r//period*(period+8)+r%period
+def chunk_gather(src, chunks, src_row, dst_row, rows, J, height, last, period):
+    lane, sub = lane_ids(), lax.broadcasted_iota(jnp.int32, (8, LANES), 0)
+
+    def step(m):
+        at = dst_row + 8 * m
+        at = at // period * (period + 8) + at % period
+        for j in range(J):
+            v = src[pl.ds(src_row + 8 * m, 8), j * LANES : (j + 1) * LANES]
+            if j == J - 1:
+                v = jnp.where(lane < last, v, 0.0)
+            if isinstance(m, int) and 8 * m + 8 > rows:
+                v = jnp.where(sub < rows - 8 * m, v, 0.0)
+            chunks[pl.ds(j * height + at + 8, 8), :] = v
+            chunks[pl.ds(j * height + at, 8), :] = v
+
+    return step
+
+
+def chunk_clear(chunks, J, height, row, period):
+    row = row // period * (period + 8) + row % period
+
+    def body(m, _):
+        for j in range(J):
+            chunks[pl.ds(j * height + row + 8 * m, 8), :] = jnp.zeros((8, LANES), F32)
+        return 0
+
+    lax.fori_loop(0, (height - row) // 8, body, 0)
+
+
+def line_merge(flat, flat0, chunks, base, cols, period, groups):
+    lane, sub = lane_ids(), lax.broadcasted_iota(jnp.int32, (8, LANES), 0)
+    J, pitch = -(-cols // LANES), period + 8
+    height = pitch * 8 * groups + 8
+    row0 = base // LANES - flat0
+
+    def step(b, tails, last=False):
+        row, s = place(base, cols, period, b)
+        row = row - flat0
+        found = [
+            chunks[pl.ds(j * height + 8 * g * pitch + b, 8, stride=pitch), :]
+            for g in range(groups)
+            for j in range(J)
+        ]
+        found = unflat(rolled(found, s), J)
+        new = []
+        keep = lane >= s
+        for g in range(groups):
+            x = found[g]
             for j in range(J):
-                v=cols(m,j)
-                chunks[pl.ds(j*height+at+8,8),:]=v
-                chunks[pl.ds(j*height+at,8),:]=v
+                v = jnp.where(keep, x[j], tails[g] if j == 0 else x[j - 1])
+                if not (last and j == J - 1):
+                    flat[pl.ds(row + 641 * 8 * g + j, 8, stride=641), :] = v
+            new.append(jnp.where(s == LANES - 1, jnp.where(keep, 0.0, x[J - 1]), v))
+        return tuple(new)
+
+    def first():
+        init = [jnp.zeros((8, LANES), F32)] * groups
+        if base == OFF_DN:
+            init[0] = jnp.where(sub == 0, flat[row0 : row0 + 8, :], 0.0)
+        return tuple(init)
+
+    def finish(tails):
+        if base % LANES:
+            for g in range(groups):
+                at = pl.ds(row0 + 641 * (8 * g + 1), 8, stride=641)
+                flat[at, :] = flat[at, :] + tails[g]
+
+    return step, first, finish
+
+
+FFN_ROW = OFF_UP // LANES // 8 * 8
+FFN_ROWS = OFF_DN // LANES + 641 * 16 + 40 - FFN_ROW
+DISCO_ROWS = 641 * 24 + 16
+
+
+def grads_kernel(nrow, basis, gconv, gup, gdn, out, *refs):
+    low, conv, gd, flat, ffn, chunks, gu, gn, stage, in_sems, ffn_sems, out_sems = refs
+    count = basis.shape[0]
+    shards, pad = out.shape[:2]
+
+    def loads(i):
+        return [
+            pltpu.make_async_copy(basis.at[i], low.at[i % 2], in_sems.at[i % 2, 0]),
+            pltpu.make_async_copy(gconv.at[i], conv.at[i % 2], in_sems.at[i % 2, 1]),
+        ]
+
+    weights = [pltpu.make_async_copy(a, b, ffn_sems.at[n]) for n, (a, b) in enumerate(((gup, gu), (gdn, gn)))]
+    flying = {}
+    for i in range(min(2, count)):
+        flying[i] = loads(i)
+        for copy in flying[i]:
+            copy.start()
+        weights[i].start()
+
+    def outer(i, n):
+        if n == 0:
+            for copy in flying[i]:
+                copy.wait()
+        at = slice(n * CP, (n + 1) * CP)
+        term = lax.dot_general(
+            low[i % 2, at, :], conv[i % 2], (((1,), (1,)), ((), ())), preferred_element_type=F32
+        )
+        if i:
+            gd[at, :CP] += term
+        else:
+            gd[at, :CP] = term
+        if n == BASIS - 1 and i + 2 < count:
+            flying[i + 2] = loads(i + 2)
+            for copy in flying[i + 2]:
+                copy.start()
+
+    def lay(n, src, rows, J, height, last, base, cols, period, groups):
+        state = {}
+        copy = chunk_gather(src, chunks, 0, 0, rows, J, height, last, period)
+        step, first, finish = line_merge(ffn, FFN_ROW, chunks, base, cols, period, groups)
+        pieces = -(-rows // 8)
+
+        def begin():
+            weights[n].wait()
+
+        def gather(start):
+            for m in range(start, min(start + 4, pieces)):
+                copy(m)
+
+        def ready():
+            chunk_clear(chunks, J, height, 8 * pieces, period)
+            state["tails"] = first()
+
+        def merge(b):
+            state["tails"] = step(b, state["tails"], last=base % LANES and b == period - 1)
+
+        def done():
+            finish(state["tails"])
+
+        steps = [begin] + [functools.partial(gather, m) for m in range(0, pieces, 4)] + [ready]
+        return steps + [functools.partial(merge, b) for b in range(period)] + [done]
+
+    products = [functools.partial(outer, i, n) for i in range(count) for n in range(BASIS)]
+    for n in range(2):
+        if n >= count:
+            weights[n].start()
+    up_steps = lay(0, gu, C + 1, 11, 72 * 16 + 8, 2, OFF_UP, HID, 64, 2)
+    down_steps = lay(1, gn, HID + 1, 6, 136 * 16 + 8, 1, OFF_DN, C, 128, 2)
+    weave(products, up_steps + down_steps)
+
+    height = 136 * 24 + 8
+    for k in range(BASIS):
+        rows = CIN + (k == BASIS - 1)
+        copy = chunk_gather(gd, chunks, k * CP, k * CIN, rows, 6, height, 1, 128)
+
+        def body(m, _):
+            copy(m)
             return 0
-        lax.fori_loop(0,full,body,0,unroll=4)
-        if rows%8:
-            r=dst_row+8*full; at=r//period*(period+8)+r%period
-            for j in range(J):
-                v=jnp.where(sub<rows-8*full,cols(full,j),0.0)
-                chunks[pl.ds(j*height+at+8,8),:]=v
-                chunks[pl.ds(j*height+at,8),:]=v
-    def clear(J,height,row,period):
-        row=row//period*(period+8)+row%period
-        count=(height-row)//8
-        def body(m,_):
-            for j in range(J): chunks[pl.ds(j*height+row+8*m,8),:]=jnp.zeros((8,LANES),F32)
-            return 0
-        lax.fori_loop(0,count,body,0)
-    def merge(base,cols,period,groups):
-        J=-(-cols//LANES); pitch=period+8; height=pitch*8*groups+8
-        def body(b,tails,rows=J):
-            row,s=place(base,cols,period,b)
-            new=[]
-            found=[chunks[pl.ds(j*height+8*g*pitch+b,8,stride=pitch),:] for g in range(groups) for j in range(J)]
-            found=unflat(rolled(found,s),J)
-            for g in range(groups):
-                x=found[g]
-                first=lane>=s
-                for j in range(J):
-                    v=jnp.where(first,x[j],tails[g] if j==0 else x[j-1])
-                    if j<rows: flat[pl.ds(row+641*8*g+j,8,stride=641),:]=v
-                new.append(jnp.where(s==LANES-1,jnp.where(first,0.0,x[J-1]),v))
-            return tuple(new)
-        row0=base//LANES
-        init=[jnp.zeros((8,LANES),F32)]*groups
-        if base%LANES:
-            init[0]=jnp.where(sub==0,flat[row0:row0+8,:],0.0)
-        tails=lax.fori_loop(0,period-8,body,tuple(init),unroll=8)
-        for b in range(period-8,period):
-            tails=body(b,tails,J-1 if base%LANES and b==period-1 else J)
-        if base%LANES:
-            for g in range(groups):
-                at=pl.ds(row0+641*(8*g+1),8,stride=641)
-                flat[at,:]=flat[at,:]+tails[g]
-    h=136*24+8
-    for k in range(BASIS): gather(gd_ref,k*CP,k*CIN,CIN+(k==BASIS-1),6,h,1,128)
-    clear(6,h,2600,128)
-    merge(0,C,128,3)
-    h=72*16+8
-    gather(gu_ref,0,0,C+1,11,h,2,64)
-    clear(11,h,648,64)
-    merge(OFF_UP,HID,64,2)
-    h=136*16+8
-    gather(gn_ref,0,0,HID+1,6,h,1,128)
-    clear(6,h,1288,128)
-    merge(OFF_DN,C,128,2)
-    def store(s,_):
-        out_ref[s]=flat[pl.ds(nrow*s,pad),:].astype(BF16); return 0
-    lax.fori_loop(0,out_ref.shape[0],store,0)
-def pack(gd,gu,gn,n,nrow,pad):
-    return pl.pallas_call(functools.partial(pack_kernel,nrow,pad),
-        out_shape=jax.ShapeDtypeStruct((n,pad,LANES),BF16),
-        scratch_shapes=[pltpu.VMEM((F_ROWS,LANES),F32),pltpu.VMEM((6*(136*24+8),LANES),F32)],
-        compiler_params=pltpu.CompilerParams(vmem_limit_bytes=VMEM),name="pack")(gd,gu,gn)
+
+        lax.fori_loop(0, rows // 8, body, 0, unroll=4)
+        copy(rows // 8)
+    chunk_clear(chunks, 6, height, 2600, 128)
+    step, first, _ = line_merge(flat, 0, chunks, 0, C, 128, 3)
+    lax.fori_loop(0, 128, step, first(), unroll=8)
+    seam = OFF_UP // LANES
+    for shard in range(shards):
+        if nrow * shard < seam < nrow * shard + pad:
+            amount = nrow * shard + pad - seam
+            flat[seam : seam + amount, :] = ffn[seam - FFN_ROW : seam - FFN_ROW + amount, :]
+    slots = stage.shape[0]
+
+    def save(shard, slot):
+        return pltpu.make_async_copy(stage.at[slot], out.at[shard], out_sems.at[slot])
+
+    for shard in range(shards):
+        slot = shard % slots
+        if shard >= slots:
+            save(shard - slots, slot).wait()
+        source, start = (flat, nrow * shard) if nrow * shard < seam else (ffn, nrow * shard - FFN_ROW)
+        stage[slot] = source[start : start + pad, :].astype(BF16)
+        save(shard, slot).start()
+    for shard in range(max(shards - slots, 0), shards):
+        save(shard, shard % slots).wait()
+
+
+def grads(basis, gconv, gup, gdn, n, nrow, pad):
+    anywhere = pl.BlockSpec(memory_space=pl.ANY)
+    return pl.pallas_call(
+        functools.partial(grads_kernel, nrow),
+        in_specs=[anywhere] * 4,
+        out_specs=anywhere,
+        out_shape=jax.ShapeDtypeStruct((n, pad, LANES), BF16),
+        scratch_shapes=[
+            pltpu.VMEM((2, BASIS * CP, WIDE), BF16),
+            pltpu.VMEM((2, CP, WIDE), BF16),
+            pltpu.VMEM((BASIS * CP, WIDE), F32),
+            pltpu.VMEM((DISCO_ROWS, LANES), F32),
+            pltpu.VMEM((FFN_ROWS, LANES), F32),
+            pltpu.VMEM((6 * (136 * 24 + 8), LANES), F32),
+            pltpu.VMEM(gup.shape, F32),
+            pltpu.VMEM(gdn.shape, F32),
+            pltpu.VMEM((4, pad, LANES), BF16),
+            pltpu.SemaphoreType.DMA((2, 2)),
+            pltpu.SemaphoreType.DMA((2,)),
+            pltpu.SemaphoreType.DMA((4,)),
+        ],
+        compiler_params=pltpu.CompilerParams(vmem_limit_bytes=VMEM),
+        name="grads",
+    )(basis, gconv, gup, gdn)
 
 
 def tiled(column):
@@ -628,35 +758,6 @@
     ref[at, :] = ref[at, :] + total
 
 
-def outer_kernel(basis, gconv, out):
-    i = pl.program_id(0)
-    term = lax.dot_general(basis[0], gconv[0], (((1,), (1,)), ((), ())), preferred_element_type=F32)
-
-    @pl.when(i == 0)
-    def _():
-        out[:, :CP] = term
-
-    @pl.when(i > 0)
-    def _():
-        out[:, :CP] += term
-
-
-def weight_grad(basis, gconv):
-    count = basis.shape[0]
-    return pl.pallas_call(
-        outer_kernel,
-        grid=(count,),
-        in_specs=[
-            pl.BlockSpec((1, BASIS * CP, WIDE), lambda i: (i, 0, 0)),
-            pl.BlockSpec((1, CP, WIDE), lambda i: (i, 0, 0)),
-        ],
-        out_specs=pl.BlockSpec((BASIS * CP, WIDE), lambda i: (0, 0)),
-        out_shape=jax.ShapeDtypeStruct((BASIS * CP, WIDE), F32),
-        compiler_params=pltpu.CompilerParams(vmem_limit_bytes=VMEM),
-        name="weight_grad",
-    )(basis, gconv)
-
-
 GROUP = 11 * STEP
 GROUP_STEP = 10 * STEP
 
@@ -812,7 +913,7 @@
     )(offsets, bases, psi, gconv, w.reshape(BASIS, CP, WIDE))
 
 
-def input_rows(width, x, gconv, own, lo, hi, gain, grad, sums, buffers, in_sems, out_sems):
+def input_rows(width, x, gconv, own, lo, hi, gain, grad, sums, buffers, in_sems, out_sems, arrived):
     rows = x.shape[1]
     places = [(s, r) for s in range(x.shape[0]) for r in range(rows)]
     saves = []
@@ -820,8 +921,8 @@
     def loads(n):
         s, r = places[n]
         sources = [x.at[s, r], gconv.at[s, r], own.at[s, r]]
-        sources += [lo.at[s]] if r == 0 else []
-        sources += [hi.at[s]] if r == rows - 1 else []
+        sources += [lo.at[0]] if r == 0 and s == 0 else []
+        sources += [hi.at[0]] if r == rows - 1 and s == 0 else []
         slots = [0, 1, 2] + ([3] if r == 0 else []) + ([4] if r == rows - 1 else [])
         return [
             pltpu.make_async_copy(source, buffers[n % 2][slot], in_sems.at[n % 2, slot])
@@ -840,6 +941,9 @@
             for copy in flying:
                 copy.start()
         here, conv, total, below, above, result = buffers[n % 2]
+        if s:
+            below = arrived(s, 0) if r == 0 else None
+            above = arrived(s, 1) if r == rows - 1 else None
 
         def read(c):
             return here[pl.ds(pl.multiple_of(c * STEP, STEP), STEP), :].astype(F32)
@@ -1150,9 +1254,9 @@
 
 
 def scatter_kernel(
-    dates, lats, lines, width, src, x, gconv, own, lo, hi, gain, second_sums, out, grad,
+    dates, lats, lines, width, src, x, gconv, own, lo, hi, to_below, to_above, gain, second_sums, out, grad,
     sums, others, z_send, z_recv, send, recv, first_sums, tiny, landed, tiny_send, tiny_recv,
-    in_sems, out_sems, *row_buffers
+    in_sems, out_sems, halo, halo_send, halo_recv, *row_buffers
 ):
     d, l = lax.axis_index("date"), lax.axis_index("lat")
     steps = dates.bit_length() - 1
@@ -1165,9 +1269,32 @@
     greet(dates, lats, d, l, owner)
     sent, flights, z = [], {}, {}
     half = len(row_buffers) // 2
+    gets = [l > 0, l < lats - 1]
+
+    def halo_copy(slab, way):
+        return pltpu.make_async_remote_copy(
+            src_ref=(to_below if way else to_above).at[slab],
+            dst_ref=halo.at[slab - 1, way],
+            send_sem=halo_send.at[slab - 1, way],
+            recv_sem=halo_recv.at[slab - 1, way],
+            device_id=(d, lax.rem(l + (lats - 1 if way else 1), lats)),
+            device_id_type=MESH,
+        )
+
+    def arrived(slab, way):
+        @pl.when(gets[way])
+        def _():
+            halo_copy(slab, way).wait_recv()
+
+        @pl.when(jnp.logical_not(gets[way]))
+        def _():
+            halo[slab - 1, way] = jnp.zeros_like(halo[slab - 1, way])
+
+        return halo.at[slab - 1, way]
+
     aside = input_rows(
         width, x, gconv, own, lo, hi, gain, grad, first_sums,
-        [row_buffers[:half], row_buffers[half:]], in_sems, out_sems,
+        [row_buffers[:half], row_buffers[half:]], in_sems, out_sems, arrived,
     )
 
     def left(p, i):
@@ -1222,6 +1349,13 @@
         for n in range(len(left(0, 0))):
             for p in range(2):
                 cross(o, p, 0, n)
+    for slab in range(1, x.shape[0]):
+        for way in range(2):
+
+            @pl.when(gets[1 - way])
+            def _():
+                halo_copy(slab, way).start()
+
     for wave in range(lats + steps - 1):
         for i in range(steps):
             if 0 <= wave - i < lats:
@@ -1270,9 +1404,15 @@
 
     for copy in sent:
         copy.wait_send()
-
-
-def scatter(packed, lines, x, gconv, own, lo, hi, gain, second_sums, width):
+    for slab in range(1, x.shape[0]):
+        for way in range(2):
+
+            @pl.when(gets[1 - way])
+            def _():
+                halo_copy(slab, way).wait_send()
+
+
+def scatter(packed, lines, x, gconv, own, lo, hi, to_below, to_above, gain, second_sums, width):
     dates, lats, rows, lanes = packed.shape
     slots = dates - 1
     tiny = (vector_home(lines, lats)[3], LANES)
@@ -1281,7 +1421,7 @@
     row_buffers = [low, low, pltpu.VMEM((CP, WIDE), F32), low, low, low]
     return pl.pallas_call(
         functools.partial(scatter_kernel, dates, lats, lines, width),
-        in_specs=[held] + [anywhere] * 5 + [held] * 2,
+        in_specs=[held] + [anywhere] * 7 + [held] * 2,
         out_specs=[held, anywhere],
         out_shape=(jax.ShapeDtypeStruct((rows, lanes), F32), jax.ShapeDtypeStruct(x.shape, BF16)),
         scratch_shapes=[
@@ -1298,13 +1438,16 @@
             pltpu.SemaphoreType.DMA((dates * lats,)),
             pltpu.SemaphoreType.DMA((2, 5)),
             pltpu.SemaphoreType.DMA((2,)),
+            pltpu.VMEM((max(x.shape[0] - 1, 1), 2, CP, WIDE), BF16),
+            pltpu.SemaphoreType.DMA((max(x.shape[0] - 1, 1), 2)),
+            pltpu.SemaphoreType.DMA((max(x.shape[0] - 1, 1), 2)),
         ]
         + row_buffers * 2,
         compiler_params=pltpu.CompilerParams(
             collective_id=1, has_side_effects=True, vmem_limit_bytes=VMEM
         ),
         name="scatter_grads",
-    )(packed, x, gconv, own, lo, hi, gain, second_sums)
+    )(packed, x, gconv, own, lo, hi, to_below, to_above, gain, second_sums)
 
 
 def local(inputs, noise, cotangent, params, psi, step_counts, pixel_mask, offsets, bases):
@@ -1351,13 +1494,12 @@
     )
     gconv_rows = gconv.reshape(slabs, rows, CP, WIDE)
     own, to_below, to_above = lower(offsets, bases, psi, gconv_rows, w, width)
-    from_below = lax.ppermute(to_above, "lat", upward)
-    from_above = lax.ppermute(to_below, "lat", downward)
-    gdisco = weight_grad(basis, gconv)
-    packed = pack(gdisco, gup, gdn, dates * lats, lines, held)
+    from_below = lax.ppermute(to_above[:1], "lat", upward)
+    from_above = lax.ppermute(to_below[:1], "lat", downward)
+    packed = grads(basis, gconv, gup, gdn, dates * lats, lines, held)
     summed, grad = scatter(
         packed.reshape(dates, lats, held, LANES), lines,
-        x, gconv_rows, own, from_below, from_above, small[0], second_sums, width,
+        x, gconv_rows, own, from_below, from_above, to_below, to_above, small[0], second_sums, width,
     )
 
     def by_pixel(values):

time: 364 us -> 354 us (0.973); the launches traced: 364 us -> 348 us
  Pallas kernels: 316 us -> 298 us
  local copies, waits for them, and re-layouts: 26.3 us -> 30.3 us
    pallas_call x2 -> x1, Pallas kernels: 44.2 us -> 32.9 us  [grads(): pl.pallas_call(functools.partial(grads_kernel, nrow), in_specs=[anywhere]...]
    pallas_call x1, Pallas kernels: 42.8 us -> 32.2 us  [lower(): pl.pallas_call(functools.partial(lower_kernel, rows, width), in_specs=[sm...]
    pallas_call x1, Pallas kernels: 49.5 us -> 54 us  [scatter(): pl.pallas_call(functools.partial(scatter_kernel, dates, lats, lines, widt...]
    unnamed x21 -> x25, local copies, waits for them, and re-layouts: 16.9 us -> 18.2 us
  transfers between devices with their start and end apart: 6 -> 6, of which waited for: 1 -> 2; matrix products, arithmetic and copies ran while one was open for 3% -> 4% of each run, Pallas kernels for 23% -> 21%
where the time goes in v6:
time: 354 us; the launch traced here: 348 us
  Pallas kernels  298 us (84%)
  local copies, waits for them, and re-layouts  30.3 us (9%)
  starting transfers between devices  15.1 us (4%)
    pallas_call x1, Pallas kernels, block(): pl.pallas_call(block_kernel, in_specs=[anywhere] * 3 + [held] * 8, out_sp...  72.3 us
    pallas_call x1, Pallas kernels, scatter(): pl.pallas_call(functools.partial(scatter_kernel, dates, lats, lines, widt...  54 us
    pallas_call x1, Pallas kernels, gather(): pl.pallas_call(functools.partial(gather_kernel, dates, lats, lines, width...  50.6 us
    pallas_call x1, Pallas kernels, grads(): pl.pallas_call(functools.partial(grads_kernel, nrow), in_specs=[anywhere]...  32.9 us
    pallas_call x2, Pallas kernels, lift(): pl.pallas_call(functools.partial(lift_kernel, rows, slab, lat, width), gr...  32.4 us
    pallas_call x1, Pallas kernels, lower(): pl.pallas_call(functools.partial(lower_kernel, rows, width), in_specs=[sm...  32.2 us
    pallas_call x1, Pallas kernels, unpack(): pl.pallas_call(functools.partial(unpack_kernel, nrow, pad), out_shape=(ja...  24.2 us
    unnamed x25, local copies, waits for them, and re-layouts  18.2 us
  transfers between devices with their start and end apart: 6, of which 2 were waited for; matrix products, arithmetic and copies ran while one was open for 4% of the time, Pallas kernels for 21%

profile of v6, /device:TPU:4, one launch (start us, length us, event | category | flops | bytes accessed | tf_op | source)
XLA Modules:
  0.0 348.1 jit_solution(17777658836501372076)
XLA Ops:
  0.6 0.0 copy-start.7
  0.6 2.6 copy.24
  3.3 0.0 copy-done.7
  3.3 0.9 fusion.5.x
  4.2 0.0 copy-start
  4.2 0.0 copy-start.6
  4.2 1.2 slice_bitcast_fusion.1
  5.5 1.0 copy-done
  6.5 0.0 copy-done.6
  6.5 0.7 pad.17.src
  7.2 50.6 %gather_params.1 = (bf16[8,4,816,128]{3,2,1,0:T(8,128)(2,1)}, bf16[2,2,5,656,768]{4,3,2,1,0:T(8,128)(2,1)}, f32[4,656,128]{2,1,0:T(8,128)}) custom-call(bf16[816,128]{1,0:T(8,128)(2,1)} %pad.17.src, bf16[2,2,656,768]{3,2,1,0:T(8,128)(2,1)} %copy-done), custom_call_target="tpu_custom_call" | custom-call | tf_op jit(solution)/shard_map/gather_params/pallas_call | solution.py:1198
  57.7 0.0 copy-start.9
  57.7 2.3 collective-permute-start
  60.0 1.3 collective-permute-start.1
  61.3 24.2 %unpack.1 = (bf16[2624,768]{1,0:T(8,128)(2,1)}, bf16[656,2624]{1,0:T(8,128)(2,1)}, bf16[656,1408]{1,0:T(8,128)(2,1)}, bf16[1296,656]{1,0:T(8,128)(2,1)}, bf16[12...) custom-call(bf16[32,816,128]{2,1,0:T(8,128)(2,1)} %bitcast.57), custom_call_target="tpu_custom_call" | custom-call | tf_op jit(solution)/shard_map/unpack/pallas_call | solution.py:109
  85.5 0.0 collective-permute-done.lo
  85.5 1.2 collective-permute-done.1.hi
  86.6 4.4 %collective-permute-start.2 = (bf16[1,656,768]{2,1,0:T(8,128)(2,1)S(1)}, bf16[1,656,768]{2,1,0:T(8,128)(2,1)}, u32[]{:S(2)}, u32[]{:S(2)}) collective-permute-start(bf16[1,656,768]{2,1,0:T(8,128)(2,1)S(1)} %get-tuple-element.35), channel_id=1, source_target_pairs={{0,1},{1,2},{2,3},{4,5},{5,6},{6,7},{8,9},{9,10},{10,11},{12,13},{... | collective-permute-start | bytes 3022856 | tf_op jit(solution)/shard_map/ppermute | solution.py:1482
  91.0 1.5 collective-permute-start.3
  92.5 0.0 copy-done.9
  92.5 0.7 copy.15.offsets
  93.2 2.6 copy.21
  95.8 0.0 copy-start.8
  95.8 0.0 copy-start.2
  95.8 2.3 pad.18.clone
  98.8 0.0 copy-done.8
  98.8 0.1 multiply_convert_fusion
  98.9 0.6 reshape.77.mask
  99.5 0.0 copy-done.2
  99.5 1.1 slice_bitcast_fusion.6
  100.6 16.2 %lift.2.refs_0_ = bf16[2,2,2624,768]{3,2,1,0:T(8,128)(2,1)} custom-call(s32[12,2]{1,0:T(8,128)} %copy.15.offsets, s32[12]{0:T(128)} %bases.5, f32[8,12]{1,0:T(8,128)} %psi.5, bf16[1,656,768]{2,1,0:T(8,128)(2,1)} %collective-permute-done.lo, bf16[1,656,768]{2,1,0:T(8,128)(2,1)} %collective-permute-done.1.hi, ...), custom_call_target="tpu_custom_call" | custom-call | flops 41943040 | bytes 41943040 | tf_op jit(solution)/shard_map/lift/pallas_call | solution.py:456
  116.8 0.0 collective-permute-done.2.lo
  116.8 0.3 collective-permute-done.3.hi
  117.1 16.2 %lift.3 = bf16[2,2,2624,768]{3,2,1,0:T(8,128)(2,1)} custom-call(s32[12,2]{1,0:T(8,128)} %copy.15.offsets, s32[12]{0:T(128)} %bases.5, f32[8,12]{1,0:T(8,128)} %psi.5, bf16[1,656,768]{2,1,0:T(8,128)(2,1)} %collective-permute-done.2.lo, bf16[1,656,768]{2,1,0:T(8,128)(2,1)} %collective-permute-done.3.hi, ...), custom_call_target="tpu_custom_call", output_to_operand_aliasing={{}: (8, {})} | custom-call | flops 41943040 | bytes 41943040 | tf_op jit(solution)/shard_map/lift/pallas_call | solution.py:456
  133.2 72.3 %block.1 = (bf16[4,656,768]{2,1,0:T(8,128)(2,1)}, bf16[4,656,768]{2,1,0:T(8,128)(2,1)}, f32[656,1408]{1,0:T(8,128)}, f32[1296,768]{1,0:T(8,128)}, f32[2,656,128]{2,1,0:T(8,128)}) custom-call(bf16[4,2624,768]{2,1,0:T(8,128)(2,1)} %bitcast.49, bf16[4,656,768]{2,1,0:T(8,128)(2,1)} %bitcast.51, bf16[4,656,768]{2,1,0:T(8,128)(2,1)} %bitcast.55, ...), custom_call_target="tpu_custom_call" | custom-call | tf_op jit(solution)/shard_map/block/pallas_call | solution.py:737
  205.5 32.2 %lower.1 = (f32[2,2,656,768]{3,2,1,0:T(8,128)}, bf16[2,656,768]{2,1,0:T(8,128)(2,1)}, bf16[2,656,768]{2,1,0:T(8,128)(2,1)}) custom-call(s32[12,2]{1,0:T(8,128)} %copy.15.offsets, s32[12]{0:T(128)} %bases.5, f32[8,12]{1,0:T(8,128)} %psi.5, bf16[2,2,656,768]{3,2,1,0:T(8,128)(2,1)} %bitcast.52, bf16[4,656,768]{2,1,0:T(8,128)(2,1)} %bitcast.58), custom_call_target="tpu_custom_call" | custom-call | tf_op jit(solution)/shard_map/lower/pallas_call | solution.py:898
  237.7 0.0 copy-start.1
  237.8 1.4 slice.51
  239.2 4.5 %collective-permute-start.4 = (bf16[1,656,768]{2,1,0:T(8,128)(2,1)S(1)}, bf16[1,656,768]{2,1,0:T(8,128)(2,1)S(1)}, u32[]{:S(2)}, u32[]{:S(2)}) collective-permute-start(bf16[1,656,768]{2,1,0:T(8,128)(2,1)S(1)} %slice.51), channel_id=1, source_target_pairs={{0,1},{1,2},{2,3},{4,5},{5,6},{6,7},{8,9},{9,10},{10,11},{12,13},{... | collective-permute-start | bytes 3022856 | tf_op jit(solution)/shard_map/ppermute | solution.py:1497
  243.7 1.3 slice.52
  245.0 1.3 collective-permute-start.5
  246.3 0.0 copy-done.1
  246.3 0.3 slice.59
  246.5 5.0 %copy.25 = bf16[2,2,641,720]{3,1,2,0:T(2,128)(2,1)} copy(bf16[2,2,641,720]{3,2,1,0:T(8,128)(2,1)S(1)} %slice.59) | data formatting | bytes 7384320
  251.5 32.9 %grads.1 = bf16[32,816,128]{2,1,0:T(8,128)(2,1)} custom-call(bf16[4,2624,768]{2,1,0:T(8,128)(2,1)} %bitcast.50, bf16[4,656,768]{2,1,0:T(8,128)(2,1)} %get-tuple-element.40.gconv, f32[656,1408]{1,0:T(8,128)} %get-tuple-element.41.gup, f32[1296,768]{1,0:T(8,128)} %get-tuple-element.42.gdn), custom_call_target="tpu_custom_call" | custom-call | tf_op jit(solution)/shard_map/grads/pallas_call | solution.py:297
  284.4 0.0 collective-permute-done.4.lo
  284.4 0.0 copy-start.3
  284.4 0.0 collective-permute-done.5.hi
  284.4 0.0 copy-start.4
  284.4 0.9 copy-done.3
  285.3 0.4 copy-done.4
  285.7 54.0 %scatter_grads.1 = (f32[816,128]{1,0:T(8,128)}, bf16[2,2,656,768]{3,2,1,0:T(8,128)(2,1)}) custom-call(bf16[8,4,816,128]{3,2,1,0:T(8,128)(2,1)} %bitcast.54, bf16[2,2,656,768]{3,2,1,0:T(8,128)(2,1)} %copy-done, bf16[2,2,656,768]{3,2,1,0:T(8,128)(2,1)} %bitcast.53, f32[2,2,656,768]{3,2,1,0:T(8,128)} %get-tuple-element.43.own, bf16[1,656,768]{2,1,0:T(8,128)(2,1)} %copy-done.3, ...), custom_call_target="tpu_custom_call" | custom-call | tf_op jit(solution)/shard_map/scatter_grads/pallas_call | solution.py:1422
  339.7 2.4 slice_bitcast_fusion
  342.1 0.0 copy-start.5
  342.1 5.0 %copy.19 = bf16[1,2,2,720,641]{3,2,4,1,0:T(2,128)(2,1)} copy(bf16[1,2,2,720,641]{3,4,2,1,0:T(8,128)(2,1)S(1)} %slice_bitcast_fusion) | data formatting | bytes 7384320
  347.0 0.0 copy-done.5
  347.0 0.8 slice_bitcast_fusion.5
  (2 shorter events, 0.0 us)
Async XLA Ops:
  0.6 2.7 copy-start.7
  4.2 2.2 copy-start
  4.2 2.2 copy-start.6
  57.7 34.7 %copy-start.9 = (s32[12,2]{0,1:T(2,128)S(1)}, s32[12,2]{0,1:T(2,128)}, u32[]{:S(2)}) copy-start(s32[12,2]{0,1:T(2,128)} %param.16) | copy-start | bytes 292
  57.7 27.7 %collective-permute-start = (bf16[1,656,768]{2,1,0:T(8,128)(2,1)}, bf16[1,656,768]{2,1,0:T(8,128)(2,1)}, u32[]{:S(2)}, u32[]{:S(2)}) collective-permute-start(bf16[1,656,768]{2,1,0:T(8,128)(2,1)} %get-tuple-element.27), channel_id=1, source_target_pairs={{0,1},{1,2},{2,3},{4,5},{5,6},{6,7},{8,9},{9,10},{10,11},{12,13},{... | collective-permute-start | bytes 3022856 | tf_op jit(solution)/shard_map/ppermute | solution.py:1482
  60.0 26.6 %collective-permute-start.1 = (bf16[1,656,768]{2,1,0:T(8,128)(2,1)S(1)}, bf16[1,656,768]{2,1,0:T(8,128)(2,1)}, u32[]{:S(2)}, u32[]{:S(2)}) collective-permute-start(bf16[1,656,768]{2,1,0:T(8,128)(2,1)S(1)} %get-tuple-element.28), channel_id=1, source_target_pairs={{1,0},{2,1},{3,2},{5,4},{6,5},{7,6},{9,8},{10,9},{11,10},{13,12},{... | collective-permute-start | bytes 3022856 | tf_op jit(solution)/shard_map/ppermute | solution.py:1482
  86.6 30.2 %collective-permute-start.2 = (bf16[1,656,768]{2,1,0:T(8,128)(2,1)S(1)}, bf16[1,656,768]{2,1,0:T(8,128)(2,1)}, u32[]{:S(2)}, u32[]{:S(2)}) collective-permute-start(bf16[1,656,768]{2,1,0:T(8,128)(2,1)S(1)} %get-tuple-element.35), channel_id=1, source_target_pairs={{0,1},{1,2},{2,3},{4,5},{5,6},{6,7},{8,9},{9,10},{10,11},{12,13},{... | collective-permute-start | bytes 3022856 | tf_op jit(solution)/shard_map/ppermute | solution.py:1482
  91.0 26.1 %collective-permute-start.3 = (bf16[1,656,768]{2,1,0:T(8,128)(2,1)S(1)}, bf16[1,656,768]{2,1,0:T(8,128)(2,1)}, u32[]{:S(2)}, u32[]{:S(2)}) collective-permute-start(bf16[1,656,768]{2,1,0:T(8,128)(2,1)S(1)} %get-tuple-element.36), channel_id=1, source_target_pairs={{1,0},{2,1},{3,2},{5,4},{6,5},{7,6},{9,8},{10,9},{11,10},{13,12},{... | collective-permute-start | bytes 3022856 | tf_op jit(solution)/shard_map/ppermute | solution.py:1482
  95.8 3.0 copy-start.8
  95.8 3.7 %copy-start.2 = (f32[4,656,128]{2,1,0:T(8,128)S(1)}, f32[4,656,128]{2,1,0:T(8,128)}, u32[]{:S(2)}) copy-start(f32[4,656,128]{2,1,0:T(8,128)} %get-tuple-element.38) | copy-start | bytes 4030468
  237.7 8.5 %copy-start.1 = (bf16[4,656,768]{2,1,0:T(8,128)(2,1)S(1)}, bf16[4,656,768]{2,1,0:T(8,128)(2,1)}, u32[]{:S(2)}) copy-start(bf16[4,656,768]{2,1,0:T(8,128)(2,1)} %get-tuple-element.39) | copy-start | bytes 12091396
  239.2 45.2 %collective-permute-start.4 = (bf16[1,656,768]{2,1,0:T(8,128)(2,1)S(1)}, bf16[1,656,768]{2,1,0:T(8,128)(2,1)S(1)}, u32[]{:S(2)}, u32[]{:S(2)}) collective-permute-start(bf16[1,656,768]{2,1,0:T(8,128)(2,1)S(1)} %slice.51), channel_id=1, source_target_pairs={{0,1},{1,2},{2,3},{4,5},{5,6},{6,7},{8,9},{9,10},{10,11},{12,13},{... | collective-permute-start | bytes 3022856 | tf_op jit(solution)/shard_map/ppermute | solution.py:1497
  245.0 39.4 %collective-permute-start.5 = (bf16[1,656,768]{2,1,0:T(8,128)(2,1)S(1)}, bf16[1,656,768]{2,1,0:T(8,128)(2,1)S(1)}, u32[]{:S(2)}, u32[]{:S(2)}) collective-permute-start(bf16[1,656,768]{2,1,0:T(8,128)(2,1)S(1)} %slice.52), channel_id=1, source_target_pairs={{1,0},{2,1},{3,2},{5,4},{6,5},{7,6},{9,8},{10,9},{11,10},{13,12},{... | collective-permute-start | bytes 3022856 | tf_op jit(solution)/shard_map/ppermute | solution.py:1498
  284.4 1.0 copy-start.3
  284.4 1.3 copy-start.4
  342.1 5.0 %copy-start.5 = (f32[816,128]{1,0:T(8,128)S(1)}, f32[816,128]{1,0:T(8,128)}, u32[]{:S(2)}) copy-start(f32[816,128]{1,0:T(8,128)} %get-tuple-element.48) | copy-start | bytes 1253380

commit v7 on v6

--- a/solution.py
+++ b/solution.py
@@ -24,6 +24,7 @@
 HL = 1408
 UNROLL = 8
 ASIDE = 2
+PARTS = 2
 VMEM = 60 << 20
 
 
@@ -56,10 +57,22 @@
     return [values[n : n + width] for n in range(0, len(values), width)]
 
 
-def unpack_kernel(nrow,pad, g_ref, w_ref,wt_ref,up_ref,upt_ref,dn_ref,dnt_ref,flat,chunks):
+def unpack_kernel(nrow,pad,g_ref,w_out,wt_out,up_out,upt_out,dn_out,dnt_out,held,w_ref,wt_ref,up_ref,upt_ref,dn_ref,dnt_ref,flat,chunks,in_sems,out_sems):
+    shards=held.shape[0]
+    parts=[pl.ds(n*shards//4,(n+1)*shards//4-n*shards//4) for n in range(4)]
+    loads=[pltpu.make_async_copy(g_ref.at[part],held.at[part],in_sems.at[n]) for n,part in enumerate(parts)]
+    for copy in loads:
+        copy.start()
+    saves=[]
+    def save(source,target):
+        copy=pltpu.make_async_copy(source,target,out_sems.at[len(saves)])
+        copy.start()
+        saves.append(copy)
     def fill(s,_):
-        flat[pl.ds(nrow*s,pad),:]=g_ref[s].astype(F32); return 0
-    lax.fori_loop(0,g_ref.shape[0],fill,0)
+        flat[pl.ds(nrow*s,pad),:]=held[s].astype(F32); return 0
+    for n,copy in enumerate(loads):
+        copy.wait()
+        lax.fori_loop(n*shards//4,(n+1)*shards//4,fill,0)
     lane=lane_ids()
     def split(base,cols,period,groups):
         J=-(-cols//LANES); pitch=period+8; height=pitch*8*groups+8; last=cols-(J-1)*LANES
@@ -97,21 +110,35 @@
     J,h,p=split(*MATS[0][:2],*MATS[0][3:])
     for k in range(BASIS):
         convert(w_ref,k*CP,k*CIN,CIN+(k==BASIS-1),CP,J,h,p)
+    save(w_ref,w_out)
+    wt_ref[...]=w_ref[:,:CP].T
+    save(wt_ref,wt_out)
     J,h,p=split(*MATS[1][:2],*MATS[1][3:])
     convert(up_ref,0,0,C+1,CP,J,h,p)
+    save(up_ref,up_out)
+    upt_ref[...]=up_ref[:,:HP].T
+    save(upt_ref,upt_out)
     J,h,p=split(*MATS[2][:2],*MATS[2][3:])
     convert(dn_ref,0,0,HID+1,HP,J,h,p)
-    wt_ref[...]=w_ref[:,:CP].T
-    upt_ref[...]=up_ref[:,:HP].T
+    save(dn_ref,dn_out)
     dnt_ref[...]=dn_ref[:,:CP].T
+    save(dnt_ref,dnt_out)
+    for copy in saves:
+        copy.wait()
+
+
 def unpack(gathered,nrow):
-    n,pad,_=gathered.shape
-    return pl.pallas_call(functools.partial(unpack_kernel,nrow,pad),
-        out_shape=(jax.ShapeDtypeStruct((BASIS*CP,WIDE),BF16),jax.ShapeDtypeStruct((CP,BASIS*CP),BF16),
-            jax.ShapeDtypeStruct((CP,HL),BF16),jax.ShapeDtypeStruct((HP,CP),BF16),
-            jax.ShapeDtypeStruct((HP,WIDE),BF16),jax.ShapeDtypeStruct((CP,HP),BF16)),
-        scratch_shapes=[pltpu.VMEM((F_ROWS,LANES),F32),pltpu.VMEM((6*(136*24+8),LANES),F32)],
+    shapes=[(BASIS*CP,WIDE),(CP,BASIS*CP),(CP,HL),(HP,CP),(HP,WIDE),(CP,HP)]
+    anywhere=pl.BlockSpec(memory_space=pl.ANY)
+    return pl.pallas_call(functools.partial(unpack_kernel,nrow,gathered.shape[1]),
+        in_specs=[anywhere],
+        out_specs=[anywhere]*6,
+        out_shape=tuple(jax.ShapeDtypeStruct(shape,BF16) for shape in shapes),
+        scratch_shapes=[pltpu.VMEM(gathered.shape,BF16)]+[pltpu.VMEM(shape,BF16) for shape in shapes]
+        +[pltpu.VMEM((F_ROWS,LANES),F32),pltpu.VMEM((6*(136*24+8),LANES),F32),pltpu.SemaphoreType.DMA((4,)),pltpu.SemaphoreType.DMA((6,))],
         compiler_params=pltpu.CompilerParams(vmem_limit_bytes=VMEM),name="unpack")(gathered)
+
+
 def chunk_gather(src, chunks, src_row, dst_row, rows, J, height, last, period):
     lane, sub = lane_ids(), lax.broadcasted_iota(jnp.int32, (8, LANES), 0)
 
@@ -389,6 +416,7 @@
         return source[pl.ds(pl.multiple_of(c * STEP, STEP), STEP), :].astype(F32)
 
     mean, scale = norm_stats(read, CIN)
+    yield
 
     def shifts(c, at):
         values = (read(c) - mean) * scale * tiled(gain[at, :]) + tiled(shift[at, :])
@@ -396,72 +424,97 @@
         for d in range(-REACH, REACH + 1):
             moved[d + REACH, at, :] = pltpu.roll(values, -d % WIDE, axis=1) if d else values
 
-    each_chunk(shifts, 4)
-
-
-def lift_kernel(
-    rows, slab, lat, width, offsets, bases, psi, lo, hi, own, gain, shift, *refs
-):
-    out, moved, table, sems = refs[-4:]
+    def step(m, _):
+        shifts(m, pl.ds(pl.multiple_of(m * STEP, STEP), STEP))
+        return 0
+
+    chunks = CP // STEP
+    for n in range(PARTS):
+        lax.fori_loop(n * chunks // PARTS, (n + 1) * chunks // PARTS, step, 0, unroll=4)
+        yield
+
+
+def points_of(bases):
+    named = [bases[p] for p in range(SUPPORT)]
+    ranks = []
+    for p in range(SUPPORT):
+        rank = jnp.int32(0)
+        for before in range(p):
+            rank = rank + jnp.where(named[before] == named[p], 1, 0)
+        ranks.append(rank)
+    picks = {}
+    for k in range(BASIS):
+        for q in range(3):
+            pick = jnp.int32(0)
+            for p in range(SUPPORT):
+                pick = pick + jnp.where(jnp.logical_and(named[p] == k, ranks[p] == q), p, 0)
+            picks[k, q] = pick
+    return picks
+
+
+def combine_row(r, first_row, lat, width, offsets, picks, psi, moved, out):
+    for k in range(BASIS):
+        parts = []
+        for q in range(3):
+            p = picks[k, q]
+            row = first_row + r + offsets[p, 0]
+            inside = jnp.logical_and(row >= 0, row < lat)
+            weight = jnp.where(inside, psi[first_row + r, p], 0.0)
+            parts.append((weight, r + 1 + offsets[p, 0], offsets[p, 1] + REACH))
+
+        def combine(c, at):
+            total = None
+            for weight, row, d in parts:
+                term = weight * moved[row, d, at, :].astype(F32)
+                total = term if total is None else total + term
+            to = pl.ds(pl.multiple_of(k * CP + c * STEP, STEP), STEP)
+            out[to, :] = cut(total, width).astype(BF16)
+
+        each_chunk(combine, 4)
+    last = slice(BASIS * CP - STEP, BASIS * CP)
+    bias_row = CIN - (CP - STEP)
+    sub = lax.broadcasted_iota(jnp.int32, (STEP, WIDE), 0)
+    lane = lax.broadcasted_iota(jnp.int32, (STEP, WIDE), 1)
+    ones = jnp.where(lane < width, 1.0, 0.0)
+    out[last, :] = jnp.where(sub == bias_row, ones, out[last, :].astype(F32)).astype(BF16)
+
+
+def lift_kernel(rows, slab, lat, width, offsets, bases, psi, lo, hi, own, gain, shift, *refs):
+    out, moved, built, sems, out_sems = refs[-5:]
     first_row = lax.axis_index("lat") * rows
     copies = [
         pltpu.make_async_copy(own.at[slab, r], moved.at[r + 1], sems.at[r]) for r in range(rows)
     ]
     for copy in copies:
         copy.start()
-    for k in range(BASIS):
-        table[SUPPORT + k] = 0
-    for p in range(SUPPORT):
-        k = bases[p]
-        used = table[SUPPORT + k]
-        table[k * 3 + used] = p
-        table[SUPPORT + k] = used + 1
+    picks = points_of(bases)
     for source, m in ((lo, 0), (hi, rows + 1)):
-        spread(source.at[0], gain, shift, width, moved.at[m])
+        for _ in spread(source.at[0], gain, shift, width, moved.at[m]):
+            pass
     for copy in copies:
         copy.wait()
+    saves = []
     for r in range(rows):
-        for k in range(BASIS):
-            parts = []
-            for q in range(3):
-                p = table[k * 3 + q]
-                row = first_row + r + offsets[p, 0]
-                inside = jnp.logical_and(row >= 0, row < lat)
-                weight = jnp.where(inside, psi[first_row + r, p], 0.0)
-                parts.append((weight, r + 1 + offsets[p, 0], offsets[p, 1] + REACH))
-
-            def combine(c, at):
-                total = None
-                for weight, row, d in parts:
-                    term = weight * moved[row, d, at, :].astype(F32)
-                    total = term if total is None else total + term
-                to = pl.ds(pl.multiple_of(k * CP + c * STEP, STEP), STEP)
-                out[0, r, to, :] = cut(total, width).astype(BF16)
-
-            each_chunk(combine, 4)
-        last = slice(BASIS * CP - STEP, BASIS * CP)
-        bias_row = CIN - (CP - STEP)
-        sub = lax.broadcasted_iota(jnp.int32, (STEP, WIDE), 0)
-        lane = lax.broadcasted_iota(jnp.int32, (STEP, WIDE), 1)
-        ones = jnp.where(lane < width, 1.0, 0.0)
-        out[0, r, last, :] = jnp.where(sub == bias_row, ones, out[0, r, last, :].astype(F32)).astype(BF16)
+        combine_row(r, first_row, lat, width, offsets, picks, psi, moved, built.at[r])
+        saves.append(pltpu.make_async_copy(built.at[r], out.at[slab, r], out_sems.at[r]))
+        saves[r].start()
+    for save in saves:
+        save.wait()
 
 
 def lift(offsets, bases, psi, lo, hi, own, gain, shift, before, slab, lat, width):
     slabs, rows = own.shape[:2]
     smem = pl.BlockSpec(memory_space=pltpu.SMEM)
-    anywhere = pl.BlockSpec(memory_space=pl.ANY)
-    halo = pl.BlockSpec((1, CP, WIDE), lambda s: (0, 0, 0))
-    column = pl.BlockSpec((CP, LANES), lambda s: (0, 0))
+    anywhere, held = pl.BlockSpec(memory_space=pl.ANY), pl.BlockSpec(memory_space=pltpu.VMEM)
     return pl.pallas_call(
         functools.partial(lift_kernel, rows, slab, lat, width),
-        grid=(1,),
-        in_specs=[smem, smem, smem, halo, halo, anywhere, column, column] + [anywhere] * len(before),
-        out_specs=pl.BlockSpec((1, rows, BASIS * CP, WIDE), lambda s: (slab, 0, 0, 0)),
+        in_specs=[smem, smem, smem, held, held, anywhere, held, held] + [anywhere] * len(before),
+        out_specs=anywhere,
         out_shape=jax.ShapeDtypeStruct((slabs, rows, BASIS * CP, WIDE), BF16),
         scratch_shapes=[
             pltpu.VMEM((rows + 2, 2 * REACH + 1, CP, WIDE), BF16),
-            pltpu.SMEM((SUPPORT + BASIS,), jnp.int32),
+            pltpu.VMEM((rows, BASIS * CP, WIDE), BF16),
+            pltpu.SemaphoreType.DMA((rows,)),
             pltpu.SemaphoreType.DMA((rows,)),
         ],
         input_output_aliases={8: 0} if before else {},
@@ -762,7 +815,7 @@
 GROUP_STEP = 10 * STEP
 
 
-def lower_kernel(rows, width, offsets, bases, psi, gconv, w, own, lo, hi, *scratch):
+def lower_kernel(rows, width, offsets, bases, psi, gconv, w, own, lo0, hi0, lo1, hi1, *scratch):
     place, coef, in_sems, w_sems, out_sems = scratch[-5:]
     per_slab = (len(scratch) - 5) // 2
     sets = [scratch[:per_slab], scratch[per_slab : 2 * per_slab]]
@@ -823,7 +876,8 @@
     def pair_of_slabs(both, _):
         def leaving(j, g):
             slab = both * 2 + j
-            targets = (own.at[slab, :, channels(g), :], lo.at[slab, channels(g), :], hi.at[slab, channels(g), :])
+            lo, hi = ((lo0, hi0), (lo1, hi1))[j]
+            targets = (own.at[slab, :, channels(g), :], lo.at[both, channels(g), :], hi.at[both, channels(g), :])
             return [
                 pltpu.make_async_copy(sets[j][3 + n], target, out_sems.at[j, n])
                 for n, target in enumerate(targets)
@@ -886,7 +940,7 @@
     slabs, rows = gconv.shape[:2]
     smem = pl.BlockSpec(memory_space=pltpu.SMEM)
     anywhere = pl.BlockSpec(memory_space=pl.ANY)
-    edge = jax.ShapeDtypeStruct((slabs, CP, WIDE), BF16)
+    edge = jax.ShapeDtypeStruct((slabs // 2, CP, WIDE), BF16)
     per_slab = [
         pltpu.VMEM((rows, CP, WIDE), BF16),
         pltpu.VMEM((BASIS, GROUP, WIDE), BF16),
@@ -898,8 +952,8 @@
     return pl.pallas_call(
         functools.partial(lower_kernel, rows, width),
         in_specs=[smem, smem, smem, anywhere, anywhere],
-        out_specs=[anywhere] * 3,
-        out_shape=(jax.ShapeDtypeStruct((slabs, rows, CP, WIDE), F32), edge, edge),
+        out_specs=[anywhere] * 5,
+        out_shape=(jax.ShapeDtypeStruct((slabs, rows, CP, WIDE), F32),) + (edge,) * 4,
         scratch_shapes=per_slab * 2
         + [
             pltpu.SMEM((3 * (2 * REACH + 1),), jnp.int32),
@@ -921,8 +975,8 @@
     def loads(n):
         s, r = places[n]
         sources = [x.at[s, r], gconv.at[s, r], own.at[s, r]]
-        sources += [lo.at[0]] if r == 0 and s == 0 else []
-        sources += [hi.at[0]] if r == rows - 1 and s == 0 else []
+        sources += [lo.at[s // 2]] if r == 0 and s % 2 == 0 else []
+        sources += [hi.at[s // 2]] if r == rows - 1 and s % 2 == 0 else []
         slots = [0, 1, 2] + ([3] if r == 0 else []) + ([4] if r == rows - 1 else [])
         return [
             pltpu.make_async_copy(source, buffers[n % 2][slot], in_sems.at[n % 2, slot])
@@ -941,7 +995,7 @@
             for copy in flying:
                 copy.start()
         here, conv, total, below, above, result = buffers[n % 2]
-        if s:
+        if s % 2:
             below = arrived(s, 0) if r == 0 else None
             above = arrived(s, 1) if r == rows - 1 else None
 
@@ -1074,8 +1128,8 @@
 
 
 def gather_kernel(
-    dates, lats, lines, width, src, x, out, moved, small, local_sem, z_send, z_recv, send, recv,
-    buffers, buffer_sems, landed, norm_sem, norm_send, norm_recv,
+    dates, lats, lines, width, src, x, out, moved, small, halo, local_sem, z_send, z_recv, send, recv,
+    buffers, buffer_sems, landed, norm_sem, norm_send, norm_recv, halo_send, halo_recv,
 ):
     d, l = lax.axis_index("date"), lax.axis_index("lat")
     steps = dates.bit_length() - 1
@@ -1152,26 +1206,46 @@
         for n, (s, r) in enumerate(rows):
             if n >= 2:
                 saves[n - 2].wait()
-            spread(x.at[s, r], small.at[0], small.at[1], width, buffers.at[n % 2])
+            yield from spread(x.at[s, r], small.at[0], small.at[1], width, buffers.at[n % 2])
             save = pltpu.make_async_copy(buffers.at[n % 2], moved.at[s, r], buffer_sems.at[n % 2])
             save.start()
             saves.append(save)
             yield
 
+    def halo_copy(way):
+        return pltpu.make_async_remote_copy(
+            src_ref=x.at[0, 0 if way else x.shape[1] - 1],
+            dst_ref=halo.at[way],
+            send_sem=halo_send.at[way],
+            recv_sem=halo_recv.at[way],
+            device_id=(d, lax.rem(l + (lats - 1 if way else 1), lats)),
+            device_id_type=MESH,
+        )
+
+    sends = [l < lats - 1, l > 0]
     aside = spread_rows()
     for wave in range(lats + steps):
         if wave < lats:
             if wave:
                 arriving[wave].wait_recv()
-            if wave + 1 < lats:
-                along(wave + 1)
+            if wave == 0:
+                for o in range(1, lats):
+                    along(o)
             for i in range(steps):
                 for p in range(2):
                     cross(wave, p, i, 0)
+            if wave == 0:
+                for way in range(2):
+
+                    @pl.when(sends[way])
+                    def _():
+                        halo_copy(way).start()
+
         next(aside, None)
         for i in range(steps)[::-1]:
             o = wave - 1 - i
             if 0 <= o < lats:
+                next(aside, None)
                 for n in range(1 << i):
                     for p in range(2):
                         flights[o, p, i, n].wait_recv()
@@ -1181,6 +1255,22 @@
         pass
     for save in saves[-2:]:
         save.wait()
+    blank = buffers.at[0, 0]
+    blank[...] = jnp.zeros_like(blank)
+    for way in range(2):
+
+        @pl.when(sends[1 - way])
+        def _():
+            halo_copy(way).wait_recv()
+
+        @pl.when(jnp.logical_not(sends[1 - way]))
+        def _():
+            pltpu.sync_copy(blank, halo.at[way])
+
+        @pl.when(sends[way])
+        def _():
+            halo_copy(way).wait_send()
+
     own.wait()
     for copy in sent:
         copy.wait_send()
@@ -1198,11 +1288,12 @@
     return pl.pallas_call(
         functools.partial(gather_kernel, dates, lats, lines, width),
         in_specs=[anywhere, pl.BlockSpec(memory_space=pltpu.VMEM)],
-        out_specs=[anywhere, anywhere, pl.BlockSpec(memory_space=pltpu.VMEM)],
+        out_specs=[anywhere, anywhere, pl.BlockSpec(memory_space=pltpu.VMEM), anywhere],
         out_shape=(
             jax.ShapeDtypeStruct((dates, lats) + shard.shape, shard.dtype),
             jax.ShapeDtypeStruct(moved, BF16),
             jax.ShapeDtypeStruct((4, CP, LANES), F32),
+            jax.ShapeDtypeStruct((2,) + x.shape[2:], BF16),
         ),
         scratch_shapes=[
             pltpu.SemaphoreType.DMA(()),
@@ -1216,6 +1307,8 @@
             pltpu.SemaphoreType.DMA(()),
             pltpu.SemaphoreType.DMA((dates * lats - 1,)),
             pltpu.SemaphoreType.DMA(()),
+            pltpu.SemaphoreType.DMA((2,)),
+            pltpu.SemaphoreType.DMA((2,)),
         ],
         compiler_params=pltpu.CompilerParams(
             collective_id=2, has_side_effects=True, vmem_limit_bytes=VMEM
@@ -1273,10 +1366,10 @@
 
     def halo_copy(slab, way):
         return pltpu.make_async_remote_copy(
-            src_ref=(to_below if way else to_above).at[slab],
-            dst_ref=halo.at[slab - 1, way],
-            send_sem=halo_send.at[slab - 1, way],
-            recv_sem=halo_recv.at[slab - 1, way],
+            src_ref=(to_below if way else to_above).at[slab // 2],
+            dst_ref=halo.at[slab // 2, way],
+            send_sem=halo_send.at[slab // 2, way],
+            recv_sem=halo_recv.at[slab // 2, way],
             device_id=(d, lax.rem(l + (lats - 1 if way else 1), lats)),
             device_id_type=MESH,
         )
@@ -1288,9 +1381,9 @@
 
         @pl.when(jnp.logical_not(gets[way]))
         def _():
-            halo[slab - 1, way] = jnp.zeros_like(halo[slab - 1, way])
-
-        return halo.at[slab - 1, way]
+            halo[slab // 2, way] = jnp.zeros_like(halo[slab // 2, way])
+
+        return halo.at[slab // 2, way]
 
     aside = input_rows(
         width, x, gconv, own, lo, hi, gain, grad, first_sums,
@@ -1349,7 +1442,7 @@
         for n in range(len(left(0, 0))):
             for p in range(2):
                 cross(o, p, 0, n)
-    for slab in range(1, x.shape[0]):
+    for slab in range(1, x.shape[0], 2):
         for way in range(2):
 
             @pl.when(gets[1 - way])
@@ -1388,7 +1481,8 @@
         for o in range(1, lats):
             z[o, p].wait_recv()
             total = total + others[o - 1, parts[p]].astype(F32)
-        out[parts[p]] = total
+        amount = min(parts[p].start + parts[p].size, lines) - parts[p].start
+        out[pl.ds(parts[p].start, amount)] = total[:amount]
 
     @pl.when(mine)
     def _():
@@ -1404,7 +1498,7 @@
 
     for copy in sent:
         copy.wait_send()
-    for slab in range(1, x.shape[0]):
+    for slab in range(1, x.shape[0], 2):
         for way in range(2):
 
             @pl.when(gets[1 - way])
@@ -1423,7 +1517,7 @@
         functools.partial(scatter_kernel, dates, lats, lines, width),
         in_specs=[held] + [anywhere] * 7 + [held] * 2,
         out_specs=[held, anywhere],
-        out_shape=(jax.ShapeDtypeStruct((rows, lanes), F32), jax.ShapeDtypeStruct(x.shape, BF16)),
+        out_shape=(jax.ShapeDtypeStruct((lines, lanes), F32), jax.ShapeDtypeStruct(x.shape, BF16)),
         scratch_shapes=[
             pltpu.VMEM((lats, slots, rows, lanes), BF16),
             pltpu.VMEM((lats - 1, rows, lanes), BF16),
@@ -1438,9 +1532,9 @@
             pltpu.SemaphoreType.DMA((dates * lats,)),
             pltpu.SemaphoreType.DMA((2, 5)),
             pltpu.SemaphoreType.DMA((2,)),
-            pltpu.VMEM((max(x.shape[0] - 1, 1), 2, CP, WIDE), BF16),
-            pltpu.SemaphoreType.DMA((max(x.shape[0] - 1, 1), 2)),
-            pltpu.SemaphoreType.DMA((max(x.shape[0] - 1, 1), 2)),
+            pltpu.VMEM((x.shape[0] // 2, 2, CP, WIDE), BF16),
+            pltpu.SemaphoreType.DMA((x.shape[0] // 2, 2)),
+            pltpu.SemaphoreType.DMA((x.shape[0] // 2, 2)),
         ]
         + row_buffers * 2,
         compiler_params=pltpu.CompilerParams(
@@ -1469,19 +1563,18 @@
     shard = jnp.pad(params.reshape(lines, LANES), ((0, held - lines), (0, 0)))
     x = padded(jnp.concatenate([by_channel(inputs), by_channel(noise)], axis=2))
     edges = [(x[s, rows - 1 :], x[s, :1]) for s in range(slabs)]
-    gathered, moved, small = gather(shard, x, lines, dates, lats, width)
+    gathered, moved, small, halo = gather(shard, x, lines, dates, lats, width)
     gathered = gathered.reshape(dates * lats, held, LANES)
     cot = padded(by_channel(cotangent)).reshape(slabs * rows, CP, WIDE)
     active = jnp.arange(steps, dtype=jnp.int32)[None, :] < step_counts[:, None]
     mask = active.reshape(slabs, 1, 1) * pixel_mask[None]
     mask = jnp.pad(mask.astype(F32), ((0, 0), (0, 0), (0, WIDE - width)))
     matrices = unpack(gathered, lines)
-    halos, done = [], gathered
-    for s in range(slabs):
+    halos, done = [(halo[:1], halo[1:])], halo
+    for s in range(1, slabs):
         top, bottom, done = lax.optimization_barrier((*edges[s], done))
         halos.append((lax.ppermute(top, "lat", upward), lax.ppermute(bottom, "lat", downward)))
-        done = halos[-1], matrices
-    matrices = done[1]
+        done = halos[-1]
     basis = ()
     for s in range(slabs):
         basis = (lift(offsets, bases, psi, *halos[s], moved, small[0], small[1], basis, s, lat, width),)
@@ -1493,9 +1586,9 @@
         wt, upt, up, dnt, dn, small[2], small[3],
     )
     gconv_rows = gconv.reshape(slabs, rows, CP, WIDE)
-    own, to_below, to_above = lower(offsets, bases, psi, gconv_rows, w, width)
-    from_below = lax.ppermute(to_above[:1], "lat", upward)
-    from_above = lax.ppermute(to_below[:1], "lat", downward)
+    own, below_even, above_even, to_below, to_above = lower(offsets, bases, psi, gconv_rows, w, width)
+    from_below = lax.ppermute(above_even, "lat", upward)
+    from_above = lax.ppermute(below_even, "lat", downward)
     packed = grads(basis, gconv, gup, gdn, dates * lats, lines, held)
     summed, grad = scatter(
         packed.reshape(dates, lats, held, LANES), lines,
@@ -1506,7 +1599,7 @@
         values = values.reshape(slabs, rows, CP, WIDE)[:, :, :C, :width]
         return jnp.swapaxes(values.reshape(samples, steps, rows, C, width), 3, 4)
 
-    return by_pixel(output), by_pixel(grad), summed[:lines].reshape(-1)
+    return by_pixel(output), by_pixel(grad), summed.reshape(-1)
 
 
 def solution(mesh):

time: 354 us -> 337 us (0.952)
  Pallas kernels: 298 us -> 289 us
  local copies, waits for them, and re-layouts: 30.3 us -> 25.4 us
    pallas_call x3, Pallas kernels: 56.5 us -> 51.6 us  [the longest x2 30.5 us: lift(): pl.pallas_call(functools.partial(lift_kernel, rows, slab, lat, width), in...]
    pallas_call x1, Pallas kernels: 50.6 us -> 46.7 us  [gather(): pl.pallas_call(functools.partial(gather_kernel, dates, lats, lines, width...]
    unnamed x25 -> x26, local copies, waits for them, and re-layouts: 18.2 us -> 14.6 us
  transfers between devices with their start and end apart: 6 -> 4, of which waited for: 2 -> 0; matrix products, arithmetic and copies ran while one was open for 4% -> 4% of each run, Pallas kernels for 21% -> 21%
where the time goes in v7:
time: 337 us; the launch traced here: 333 us
  Pallas kernels  289 us (86%)
  local copies, waits for them, and re-layouts  25.4 us (8%)
  starting transfers between devices  15.1 us (4%)
    pallas_call x1, Pallas kernels, block(): pl.pallas_call(block_kernel, in_specs=[anywhere] * 3 + [held] * 8, out_sp...  72.3 us
    pallas_call x1, Pallas kernels, scatter(): pl.pallas_call(functools.partial(scatter_kernel, dates, lats, lines, widt...  53.5 us
    pallas_call x1, Pallas kernels, gather(): pl.pallas_call(functools.partial(gather_kernel, dates, lats, lines, width...  46.7 us
    pallas_call x1, Pallas kernels, grads(): pl.pallas_call(functools.partial(grads_kernel, nrow), in_specs=[anywhere]...  33 us
    pallas_call x1, Pallas kernels, lower(): pl.pallas_call(functools.partial(lower_kernel, rows, width), in_specs=[sm...  32.1 us
    pallas_call x2, Pallas kernels, lift(): pl.pallas_call(functools.partial(lift_kernel, rows, slab, lat, width), in...  30.5 us
    pallas_call x1, Pallas kernels, unpack(): pl.pallas_call(functools.partial(unpack_kernel, nrow, gathered.shape[1]),...  21.1 us
    unnamed x26, local copies, waits for them, and re-layouts  14.6 us
  transfers between devices with their start and end apart: 4, of which 0 were waited for; matrix products, arithmetic and copies ran while one was open for 4% of the time, Pallas kernels for 21%

profile of v7, /device:TPU:4, one launch (start us, length us, event | category | flops | bytes accessed | tf_op | source)
XLA Modules:
  0.0 332.8 jit_solution(3867107849311386265)
XLA Ops:
  0.6 0.0 copy-start.7
  0.6 2.6 copy.24
  3.3 0.0 copy-done.7
  3.3 0.9 fusion.5.x
  4.2 0.0 copy-start
  4.2 0.0 copy-start.6
  4.2 0.0 copy-start.9
  4.3 1.5 slice_bitcast_fusion.1
  5.7 0.0 copy-done.6
  5.7 1.2 pad.17.src
  6.9 0.0 copy-done
  6.9 46.7 %gather_params.1 = (bf16[8,4,816,128]{3,2,1,0:T(8,128)(2,1)}, bf16[2,2,5,656,768]{4,3,2,1,0:T(8,128)(2,1)}, f32[4,656,128]{2,1,0:T(8,128)}, bf16[2,656,768]{2,1,0:T(8,128)(2,1)}) custom-call(bf16[816,128]{1,0:T(8,128)(2,1)} %pad.17.src, bf16[2,2,656,768]{3,2,1,0:T(8,128)(2,1)} %copy-done), custom_call_target="tpu_custom_call" | custom-call | tf_op jit(solution)/shard_map/gather_params/pallas_call | solution.py:1288
  53.6 6.8 %collective-permute-start = (bf16[1,656,768]{2,1,0:T(8,128)(2,1)}, bf16[1,656,768]{2,1,0:T(8,128)(2,1)}, u32[]{:S(2)}, u32[]{:S(2)}) collective-permute-start(bf16[1,656,768]{2,1,0:T(8,128)(2,1)} %get-tuple-element.28), channel_id=1, source_target_pairs={{0,1},{1,2},{2,3},{4,5},{5,6},{6,7},{8,9},{9,10},{10,11},{12,13},{... | collective-permute-start | bytes 3022856 | tf_op jit(solution)/shard_map/ppermute | solution.py:1576
  60.4 1.5 collective-permute-start.1
  61.9 0.0 copy-done.9
  61.9 0.7 copy.15.offsets
  62.6 0.0 copy-start.1
  62.6 21.1 %unpack.1 = (bf16[2624,768]{1,0:T(8,128)(2,1)}, bf16[656,2624]{1,0:T(8,128)(2,1)}, bf16[656,1408]{1,0:T(8,128)(2,1)}, bf16[1296,656]{1,0:T(8,128)(2,1)}, bf16[12...) custom-call(bf16[32,816,128]{2,1,0:T(8,128)(2,1)} %bitcast.52), custom_call_target="tpu_custom_call" | custom-call | tf_op jit(solution)/shard_map/unpack/pallas_call | solution.py:133
  83.7 0.0 copy-done.1
  83.7 0.5 copy.21
  84.2 0.0 copy-start.8
  84.3 0.0 copy-start.4
  84.3 0.0 copy-start.3
  84.3 2.5 pad.18.clone
  87.4 0.0 copy-done.8
  87.4 0.1 multiply_convert_fusion
  87.5 0.6 reshape.76.mask
  88.1 0.0 copy-done.4
  88.1 1.1 slice_bitcast_fusion.3
  89.2 0.0 copy-done.3
  89.2 1.4 fusion.6
  90.7 15.2 %lift.2.refs_0_ = bf16[2,2,2624,768]{3,2,1,0:T(8,128)(2,1)} custom-call(s32[12,2]{1,0:T(8,128)} %copy.15.offsets, s32[12]{0:T(128)} %bases.5, f32[8,12]{1,0:T(8,128)} %psi.5, bf16[1,656,768]{2,1,0:T(8,128)(2,1)} %get-tuple-element.57.lo, bf16[1,656,768]{2,1,0:T(8,128)(2,1)} %get-tuple-element.56.hi, bf16[2,2,5,656,768]{4,3,2,1,0:T(8,128)(2,1)} %get-tuple-element.30.own, ...), custom_call_target="tpu_custom_call" | custom-call | flops 41943040 | bytes 41943040 | tf_op jit(solution)/shard_map/lift/pallas_call | solution.py:509
  105.9 0.0 collective-permute-done.lo
  105.9 0.0 collective-permute-done.1.hi
  105.9 15.2 %lift.3 = bf16[2,2,2624,768]{3,2,1,0:T(8,128)(2,1)} custom-call(s32[12,2]{1,0:T(8,128)} %copy.15.offsets, s32[12]{0:T(128)} %bases.5, f32[8,12]{1,0:T(8,128)} %psi.5, bf16[1,656,768]{2,1,0:T(8,128)(2,1)} %collective-permute-done.lo, bf16[1,656,768]{2,1,0:T(8,128)(2,1)} %collective-permute-done.1.hi, ...), custom_call_target="tpu_custom_call", output_to_operand_aliasing={{}: (8, {})} | custom-call | flops 41943040 | bytes 41943040 | tf_op jit(solution)/shard_map/lift/pallas_call | solution.py:509
  121.2 72.3 %block.1 = (bf16[4,656,768]{2,1,0:T(8,128)(2,1)}, bf16[4,656,768]{2,1,0:T(8,128)(2,1)}, f32[656,1408]{1,0:T(8,128)}, f32[1296,768]{1,0:T(8,128)}, f32[2,656,128]{2,1,0:T(8,128)}) custom-call(bf16[4,2624,768]{2,1,0:T(8,128)(2,1)} %bitcast.44, bf16[4,656,768]{2,1,0:T(8,128)(2,1)} %bitcast.46, bf16[4,656,768]{2,1,0:T(8,128)(2,1)} %bitcast.50, ...), custom_call_target="tpu_custom_call" | custom-call | tf_op jit(solution)/shard_map/block/pallas_call | solution.py:790
  193.5 0.0 copy-start.2
  193.5 32.1 %lower.1 = (f32[2,2,656,768]{3,2,1,0:T(8,128)}, bf16[1,656,768]{2,1,0:T(8,128)(2,1)}, bf16[1,656,768]{2,1,0:T(8,128)(2,1)}, bf16[1,656,768]{2,1,0:T(8,128)(2,1)}, bf16[1,656,768]{2,1,0:T(8,128)(2,1)}) custom-call(s32[12,2]{1,0:T(8,128)} %copy.15.offsets, s32[12]{0:T(128)} %bases.5, f32[8,12]{1,0:T(8,128)} %psi.5, bf16[2,2,656,768]{3,2,1,0:T(8,128)(2,1)} %bitcast.47, ...), custom_call_target="tpu_custom_call" | custom-call | tf_op jit(solution)/shard_map/lower/pallas_call | solution.py:952
  225.6 5.5 %collective-permute-start.2 = (bf16[1,656,768]{2,1,0:T(8,128)(2,1)}, bf16[1,656,768]{2,1,0:T(8,128)(2,1)}, u32[]{:S(2)}, u32[]{:S(2)}) collective-permute-start(bf16[1,656,768]{2,1,0:T(8,128)(2,1)} %get-tuple-element.44), channel_id=1, source_target_pairs={{0,1},{1,2},{2,3},{4,5},{5,6},{6,7},{8,9},{9,10},{10,11},{12,13},{... | collective-permute-start | bytes 3022856 | tf_op jit(solution)/shard_map/ppermute | solution.py:1590
  231.1 1.3 collective-permute-start.3
  232.4 0.0 copy-done.2
  232.4 0.3 slice.45
  232.7 5.0 %copy.25 = bf16[2,2,641,720]{3,1,2,0:T(2,128)(2,1)} copy(bf16[2,2,641,720]{3,2,1,0:T(8,128)(2,1)S(1)} %slice.45) | data formatting | bytes 7384320
  237.7 33.0 %grads.1 = bf16[32,816,128]{2,1,0:T(8,128)(2,1)} custom-call(bf16[4,2624,768]{2,1,0:T(8,128)(2,1)} %bitcast.45, bf16[4,656,768]{2,1,0:T(8,128)(2,1)} %get-tuple-element.39.gconv, f32[656,1408]{1,0:T(8,128)} %get-tuple-element.40.gup, f32[1296,768]{1,0:T(8,128)} %get-tuple-element.41.gdn), custom_call_target="tpu_custom_call" | custom-call | tf_op jit(solution)/shard_map/grads/pallas_call | solution.py:324
  270.7 0.0 collective-permute-done.2.lo
  270.7 0.0 collective-permute-done.3.hi
  270.7 53.5 %scatter_grads.1 = (f32[809,128]{1,0:T(8,128)}, bf16[2,2,656,768]{3,2,1,0:T(8,128)(2,1)}) custom-call(bf16[8,4,816,128]{3,2,1,0:T(8,128)(2,1)} %bitcast.49, bf16[2,2,656,768]{3,2,1,0:T(8,128)(2,1)} %copy-done, bf16[2,2,656,768]{3,2,1,0:T(8,128)(2,1)} %bitcast.48, f32[2,2,656,768]{3,2,1,0:T(8,128)} %get-tuple-element.43.own, ...), custom_call_target="tpu_custom_call" | custom-call | tf_op jit(solution)/shard_map/scatter_grads/pallas_call | solution.py:1516
  324.2 2.4 slice_bitcast_fusion
  326.6 0.0 copy-start.5
  326.6 5.0 %copy.19 = bf16[1,2,2,720,641]{3,2,4,1,0:T(2,128)(2,1)} copy(bf16[1,2,2,720,641]{3,4,2,1,0:T(8,128)(2,1)S(1)} %slice_bitcast_fusion) | data formatting | bytes 7384320
  331.6 0.0 copy-done.5
  331.6 0.8 copy.29
  (2 shorter events, 0.0 us)
Async XLA Ops:
  0.6 2.7 copy-start.7
  4.2 2.6 copy-start
  4.2 1.5 copy-start.6
  4.2 57.7 %copy-start.9 = (s32[12,2]{0,1:T(2,128)S(1)}, s32[12,2]{0,1:T(2,128)}, u32[]{:S(2)}) copy-start(s32[12,2]{0,1:T(2,128)} %param.16) | copy-start | bytes 292
  53.6 52.3 %collective-permute-start = (bf16[1,656,768]{2,1,0:T(8,128)(2,1)}, bf16[1,656,768]{2,1,0:T(8,128)(2,1)}, u32[]{:S(2)}, u32[]{:S(2)}) collective-permute-start(bf16[1,656,768]{2,1,0:T(8,128)(2,1)} %get-tuple-element.28), channel_id=1, source_target_pairs={{0,1},{1,2},{2,3},{4,5},{5,6},{6,7},{8,9},{9,10},{10,11},{12,13},{... | collective-permute-start | bytes 3022856 | tf_op jit(solution)/shard_map/ppermute | solution.py:1576
  60.4 45.5 %collective-permute-start.1 = (bf16[1,656,768]{2,1,0:T(8,128)(2,1)}, bf16[1,656,768]{2,1,0:T(8,128)(2,1)}, u32[]{:S(2)}, u32[]{:S(2)}) collective-permute-start(bf16[1,656,768]{2,1,0:T(8,128)(2,1)} %get-tuple-element.29), channel_id=1, source_target_pairs={{1,0},{2,1},{3,2},{5,4},{6,5},{7,6},{9,8},{10,9},{11,10},{13,12},{... | collective-permute-start | bytes 3022856 | tf_op jit(solution)/shard_map/ppermute | solution.py:1576
  62.6 21.1 %copy-start.1 = (bf16[1,2,2,720,641]{3,2,4,1,0:T(2,128)(2,1)S(1)}, bf16[1,2,2,720,641]{3,2,4,1,0:T(2,128)(2,1)}, u32[]{:S(2)}) copy-start(bf16[1,2,2,720,641]{3,2,4,1,0:T(2,128)(2,1)} %param.11) | copy-start | bytes 11076484
  84.2 3.2 copy-start.8
  84.3 3.9 %copy-start.4 = (f32[4,656,128]{2,1,0:T(8,128)S(1)}, f32[4,656,128]{2,1,0:T(8,128)}, u32[]{:S(2)}) copy-start(f32[4,656,128]{2,1,0:T(8,128)} %get-tuple-element.31) | copy-start | bytes 4030468
  84.3 5.0 %copy-start.3 = (bf16[2,656,768]{2,1,0:T(8,128)(2,1)S(1)}, bf16[2,656,768]{2,1,0:T(8,128)(2,1)}, u32[]{:S(2)}) copy-start(bf16[2,656,768]{2,1,0:T(8,128)(2,1)} %get-tuple-element.27) | copy-start | bytes 6045700
  193.5 38.9 %copy-start.2 = (bf16[4,656,768]{2,1,0:T(8,128)(2,1)S(1)}, bf16[4,656,768]{2,1,0:T(8,128)(2,1)}, u32[]{:S(2)}) copy-start(bf16[4,656,768]{2,1,0:T(8,128)(2,1)} %get-tuple-element.38) | copy-start | bytes 12091396
  225.6 45.0 %collective-permute-start.2 = (bf16[1,656,768]{2,1,0:T(8,128)(2,1)}, bf16[1,656,768]{2,1,0:T(8,128)(2,1)}, u32[]{:S(2)}, u32[]{:S(2)}) collective-permute-start(bf16[1,656,768]{2,1,0:T(8,128)(2,1)} %get-tuple-element.44), channel_id=1, source_target_pairs={{0,1},{1,2},{2,3},{4,5},{5,6},{6,7},{8,9},{9,10},{10,11},{12,13},{... | collective-permute-start | bytes 3022856 | tf_op jit(solution)/shard_map/ppermute | solution.py:1590
  231.1 39.5 %collective-permute-start.3 = (bf16[1,656,768]{2,1,0:T(8,128)(2,1)}, bf16[1,656,768]{2,1,0:T(8,128)(2,1)}, u32[]{:S(2)}, u32[]{:S(2)}) collective-permute-start(bf16[1,656,768]{2,1,0:T(8,128)(2,1)} %get-tuple-element.45), channel_id=1, source_target_pairs={{1,0},{2,1},{3,2},{5,4},{6,5},{7,6},{9,8},{10,9},{11,10},{13,12},{... | collective-permute-start | bytes 3022856 | tf_op jit(solution)/shard_map/ppermute | solution.py:1591
  326.6 5.0 %copy-start.5 = (f32[809,128]{1,0:T(8,128)S(1)}, f32[809,128]{1,0:T(8,128)}, u32[]{:S(2)}) copy-start(f32[809,128]{1,0:T(8,128)} %get-tuple-element.50) | copy-start | bytes 1242628

commit v8 on v7

--- a/solution.py
+++ b/solution.py
@@ -470,7 +470,7 @@
             to = pl.ds(pl.multiple_of(k * CP + c * STEP, STEP), STEP)
             out[to, :] = cut(total, width).astype(BF16)
 
-        each_chunk(combine, 4)
+        each_chunk(combine, 8)
     last = slice(BASIS * CP - STEP, BASIS * CP)
     bias_row = CIN - (CP - STEP)
     sub = lax.broadcasted_iota(jnp.int32, (STEP, WIDE), 0)
@@ -479,49 +479,61 @@
     out[last, :] = jnp.where(sub == bias_row, ones, out[last, :].astype(F32)).astype(BF16)
 
 
-def lift_kernel(rows, slab, lat, width, offsets, bases, psi, lo, hi, own, gain, shift, *refs):
-    out, moved, built, sems, out_sems = refs[-5:]
+def lift_kernel(rows, lat, width, offsets, bases, psi, own, small, *refs):
+    out, moved, built, ends, sems, out_sems, end_sems = refs[-7:]
+    halos = refs[:-7]
+    slabs = out.shape[0]
     first_row = lax.axis_index("lat") * rows
-    copies = [
-        pltpu.make_async_copy(own.at[slab, r], moved.at[r + 1], sems.at[r]) for r in range(rows)
-    ]
-    for copy in copies:
+    ways = [halos[0].at[0], halos[0].at[1]] + [halo.at[0] for halo in halos[1:]]
+    sources = [pltpu.make_async_copy(way, ends.at[n], end_sems.at[n]) for n, way in enumerate(ways)]
+    for copy in sources:
         copy.start()
+
+    def inner(s):
+        return [pltpu.make_async_copy(own.at[s, r], moved.at[r + 1], sems.at[r]) for r in range(rows)]
+
     picks = points_of(bases)
-    for source, m in ((lo, 0), (hi, rows + 1)):
-        for _ in spread(source.at[0], gain, shift, width, moved.at[m]):
-            pass
-    for copy in copies:
-        copy.wait()
-    saves = []
+    saves = {}
+    for s in range(slabs):
+        for copy in inner(s):
+            copy.start()
+        for way, m in ((0, 0), (1, rows + 1)):
+            sources[2 * s + way].wait()
+            for _ in spread(ends.at[2 * s + way], small.at[0], small.at[1], width, moved.at[m]):
+                pass
+        for copy in inner(s):
+            copy.wait()
+        for r in range(rows):
+            if s:
+                saves[s - 1, r].wait()
+            combine_row(r, first_row, lat, width, offsets, picks, psi, moved, built.at[r])
+            saves[s, r] = pltpu.make_async_copy(built.at[r], out.at[s, r], out_sems.at[r])
+            saves[s, r].start()
     for r in range(rows):
-        combine_row(r, first_row, lat, width, offsets, picks, psi, moved, built.at[r])
-        saves.append(pltpu.make_async_copy(built.at[r], out.at[slab, r], out_sems.at[r]))
-        saves[r].start()
-    for save in saves:
-        save.wait()
-
-
-def lift(offsets, bases, psi, lo, hi, own, gain, shift, before, slab, lat, width):
+        saves[slabs - 1, r].wait()
+
+
+def lift(offsets, bases, psi, halos, own, small, lat, width):
     slabs, rows = own.shape[:2]
     smem = pl.BlockSpec(memory_space=pltpu.SMEM)
     anywhere, held = pl.BlockSpec(memory_space=pl.ANY), pl.BlockSpec(memory_space=pltpu.VMEM)
     return pl.pallas_call(
-        functools.partial(lift_kernel, rows, slab, lat, width),
-        in_specs=[smem, smem, smem, held, held, anywhere, held, held] + [anywhere] * len(before),
+        functools.partial(lift_kernel, rows, lat, width),
+        in_specs=[smem, smem, smem, anywhere, held] + [anywhere] * len(halos),
         out_specs=anywhere,
         out_shape=jax.ShapeDtypeStruct((slabs, rows, BASIS * CP, WIDE), BF16),
         scratch_shapes=[
             pltpu.VMEM((rows + 2, 2 * REACH + 1, CP, WIDE), BF16),
             pltpu.VMEM((rows, BASIS * CP, WIDE), BF16),
+            pltpu.VMEM((2 * slabs, CP, WIDE), BF16),
             pltpu.SemaphoreType.DMA((rows,)),
             pltpu.SemaphoreType.DMA((rows,)),
+            pltpu.SemaphoreType.DMA((2 * slabs,)),
         ],
-        input_output_aliases={8: 0} if before else {},
         compiler_params=pltpu.CompilerParams(vmem_limit_bytes=VMEM),
         cost_estimate=pl.CostEstimate(flops=40 << 20, bytes_accessed=40 << 20, transcendentals=0),
         name="lift",
-    )(offsets, bases, psi, lo, hi, own, gain, shift, *before)
+    )(offsets, bases, psi, own, small, *halos)
 
 
 GELU_A = math.sqrt(2.0 / math.pi)
@@ -703,8 +715,9 @@
 
 
 def block_kernel(
-    basis, x, cot, mask, wt, upt, up, dnt, dn, gain, shift, out, gconv, gup, gdn, sums, *scratch
+    basis, x, cot, mask, wt, upt, up, dnt, dn, small, out, gconv, gup, gdn, sums, *scratch
 ):
+    gain, shift = small.at[2], small.at[3]
     count = basis.shape[0]
     tiles = WIDE // TILE
     in_sems, out_sems = scratch[-2:]
@@ -779,7 +792,7 @@
             copy.wait()
 
 
-def block(basis, x, cot, mask, wt, upt, up, dnt, dn, gain, shift):
+def block(basis, x, cot, mask, wt, upt, up, dnt, dn, small):
     count = x.shape[0]
     anywhere = pl.BlockSpec(memory_space=pl.ANY)
     held = pl.BlockSpec(memory_space=pltpu.VMEM)
@@ -789,7 +802,7 @@
     per_job += [high, low, hidden_high, hidden_low, high, hidden_high, low, hidden_low]
     return pl.pallas_call(
         block_kernel,
-        in_specs=[anywhere] * 3 + [held] * 8,
+        in_specs=[anywhere] * 3 + [held] * 7,
         out_specs=[anywhere] * 2 + [held] * 3,
         out_shape=(
             jax.ShapeDtypeStruct((count, CP, WIDE), BF16),
@@ -801,7 +814,7 @@
         scratch_shapes=per_job * 2 + [pltpu.SemaphoreType.DMA((2, 3)), pltpu.SemaphoreType.DMA((2, 2))],
         compiler_params=pltpu.CompilerParams(vmem_limit_bytes=VMEM),
         name="block",
-    )(basis, x, cot, mask, wt, upt, up, dnt, dn, gain, shift)
+    )(basis, x, cot, mask, wt, upt, up, dnt, dn, small)
 
 
 def along_lanes(ref, at, values):
@@ -1129,7 +1142,7 @@
 
 def gather_kernel(
     dates, lats, lines, width, src, x, out, moved, small, halo, local_sem, z_send, z_recv, send, recv,
-    buffers, buffer_sems, landed, norm_sem, norm_send, norm_recv, halo_send, halo_recv,
+    buffers, buffer_sems, landed, norm_sem, norm_send, norm_recv, halo_send, halo_recv, near, near_sem,
 ):
     d, l = lax.axis_index("date"), lax.axis_index("lat")
     steps = dates.bit_length() - 1
@@ -1138,6 +1151,8 @@
     mine = jnp.logical_and(d == owner[0], l == owner[1])
     others = [(a, b) for a in range(dates) for b in range(lats) if (a, b) != owner]
     window = src.at[pl.ds(row, count)]
+    nearby = pltpu.make_async_copy(x, near, near_sem)
+    nearby.start()
 
     greet(dates, lats, d, l, owner)
 
@@ -1203,10 +1218,11 @@
             norms_to(0).wait_recv()
 
         read_norms(landed, first, small)
+        nearby.wait()
         for n, (s, r) in enumerate(rows):
             if n >= 2:
                 saves[n - 2].wait()
-            yield from spread(x.at[s, r], small.at[0], small.at[1], width, buffers.at[n % 2])
+            yield from spread(near.at[s, r], small.at[0], small.at[1], width, buffers.at[n % 2])
             save = pltpu.make_async_copy(buffers.at[n % 2], moved.at[s, r], buffer_sems.at[n % 2])
             save.start()
             saves.append(save)
@@ -1287,7 +1303,7 @@
     anywhere = pl.BlockSpec(memory_space=pl.ANY)
     return pl.pallas_call(
         functools.partial(gather_kernel, dates, lats, lines, width),
-        in_specs=[anywhere, pl.BlockSpec(memory_space=pltpu.VMEM)],
+        in_specs=[anywhere, anywhere],
         out_specs=[anywhere, anywhere, pl.BlockSpec(memory_space=pltpu.VMEM), anywhere],
         out_shape=(
             jax.ShapeDtypeStruct((dates, lats) + shard.shape, shard.dtype),
@@ -1309,6 +1325,8 @@
             pltpu.SemaphoreType.DMA(()),
             pltpu.SemaphoreType.DMA((2,)),
             pltpu.SemaphoreType.DMA((2,)),
+            pltpu.VMEM(x.shape, BF16),
+            pltpu.SemaphoreType.DMA(()),
         ],
         compiler_params=pltpu.CompilerParams(
             collective_id=2, has_side_effects=True, vmem_limit_bytes=VMEM
@@ -1347,9 +1365,9 @@
 
 
 def scatter_kernel(
-    dates, lats, lines, width, src, x, gconv, own, lo, hi, to_below, to_above, gain, second_sums, out, grad,
+    dates, lats, lines, width, src, x, gconv, own, lo, hi, to_below, to_above, small, second_sums, out, grad,
     sums, others, z_send, z_recv, send, recv, first_sums, tiny, landed, tiny_send, tiny_recv,
-    in_sems, out_sems, halo, halo_send, halo_recv, *row_buffers
+    in_sems, out_sems, halo, halo_send, halo_recv, near, near_sem, *row_buffers
 ):
     d, l = lax.axis_index("date"), lax.axis_index("lat")
     steps = dates.bit_length() - 1
@@ -1359,6 +1377,8 @@
     mine = jnp.logical_and(d == owner[0], l == owner[1])
     senders = [(a, b) for a in range(dates) for b in range(lats) if (a, b) != owner]
 
+    nearby = pltpu.make_async_copy(src, near, near_sem)
+    nearby.start()
     greet(dates, lats, d, l, owner)
     sent, flights, z = [], {}, {}
     half = len(row_buffers) // 2
@@ -1386,7 +1406,7 @@
         return halo.at[slab // 2, way]
 
     aside = input_rows(
-        width, x, gconv, own, lo, hi, gain, grad, first_sums,
+        width, x, gconv, own, lo, hi, small.at[0], grad, first_sums,
         [row_buffers[:half], row_buffers[half:]], in_sems, out_sems, arrived,
     )
 
@@ -1398,14 +1418,17 @@
 
     def held(o, p, i, mask):
         if i == 0:
-            return src.at[flipped(d, mask), lax.rem(l + o, lats), parts[p]]
+            return near.at[flipped(d, mask), lax.rem(l + o, lats), parts[p]]
         return sums.at[o, slot_of(i - 1, left(p, i - 1).index(mask)), parts[p]]
+
+    def first_block(o, p, mask):
+        return src.at[flipped(d, mask), lax.rem(l + o, lats), parts[p]]
 
     def cross(o, p, i, n):
         bit = paths[p][i]
         slot = slot_of(i, n)
         copy = pltpu.make_async_remote_copy(
-            src_ref=held(o, p, i, left(p, i)[n] | 1 << bit),
+            src_ref=held(o, p, i, left(p, i)[n] | 1 << bit) if i else first_block(o, p, left(p, i)[n] | 1 << bit),
             dst_ref=sums.at[o, slot, parts[p]],
             send_sem=send.at[o, p, slot],
             recv_sem=recv.at[o, p, slot],
@@ -1449,6 +1472,7 @@
             def _():
                 halo_copy(slab, way).start()
 
+    nearby.wait()
     for wave in range(lats + steps - 1):
         for i in range(steps):
             if 0 <= wave - i < lats:
@@ -1506,7 +1530,7 @@
                 halo_copy(slab, way).wait_send()
 
 
-def scatter(packed, lines, x, gconv, own, lo, hi, to_below, to_above, gain, second_sums, width):
+def scatter(packed, lines, x, gconv, own, lo, hi, to_below, to_above, small, second_sums, width):
     dates, lats, rows, lanes = packed.shape
     slots = dates - 1
     tiny = (vector_home(lines, lats)[3], LANES)
@@ -1515,7 +1539,7 @@
     row_buffers = [low, low, pltpu.VMEM((CP, WIDE), F32), low, low, low]
     return pl.pallas_call(
         functools.partial(scatter_kernel, dates, lats, lines, width),
-        in_specs=[held] + [anywhere] * 7 + [held] * 2,
+        in_specs=[anywhere] * 8 + [held] * 2,
         out_specs=[held, anywhere],
         out_shape=(jax.ShapeDtypeStruct((lines, lanes), F32), jax.ShapeDtypeStruct(x.shape, BF16)),
         scratch_shapes=[
@@ -1535,13 +1559,15 @@
             pltpu.VMEM((x.shape[0] // 2, 2, CP, WIDE), BF16),
             pltpu.SemaphoreType.DMA((x.shape[0] // 2, 2)),
             pltpu.SemaphoreType.DMA((x.shape[0] // 2, 2)),
+            pltpu.VMEM(packed.shape, BF16),
+            pltpu.SemaphoreType.DMA(()),
         ]
         + row_buffers * 2,
         compiler_params=pltpu.CompilerParams(
             collective_id=1, has_side_effects=True, vmem_limit_bytes=VMEM
         ),
         name="scatter_grads",
-    )(packed, x, gconv, own, lo, hi, to_below, to_above, gain, second_sums)
+    )(packed, x, gconv, own, lo, hi, to_below, to_above, small, second_sums)
 
 
 def local(inputs, noise, cotangent, params, psi, step_counts, pixel_mask, offsets, bases):
@@ -1570,20 +1596,17 @@
     mask = active.reshape(slabs, 1, 1) * pixel_mask[None]
     mask = jnp.pad(mask.astype(F32), ((0, 0), (0, 0), (0, WIDE - width)))
     matrices = unpack(gathered, lines)
-    halos, done = [(halo[:1], halo[1:])], halo
+    halos, done = [halo], halo
     for s in range(1, slabs):
         top, bottom, done = lax.optimization_barrier((*edges[s], done))
-        halos.append((lax.ppermute(top, "lat", upward), lax.ppermute(bottom, "lat", downward)))
-        done = halos[-1]
-    basis = ()
-    for s in range(slabs):
-        basis = (lift(offsets, bases, psi, *halos[s], moved, small[0], small[1], basis, s, lat, width),)
-    basis = basis[0]
+        done = lax.ppermute(top, "lat", upward), lax.ppermute(bottom, "lat", downward)
+        halos += done
+    basis = lift(offsets, bases, psi, halos, moved, small, lat, width)
     w, wt, up, upt, dn, dnt = matrices
     basis = basis.reshape(slabs * rows, BASIS * CP, WIDE)
     output, gconv, gup, gdn, second_sums = block(
         basis, x.reshape(slabs * rows, CP, WIDE), cot, mask.reshape(slabs * rows, 1, WIDE),
-        wt, upt, up, dnt, dn, small[2], small[3],
+        wt, upt, up, dnt, dn, small,
     )
     gconv_rows = gconv.reshape(slabs, rows, CP, WIDE)
     own, below_even, above_even, to_below, to_above = lower(offsets, bases, psi, gconv_rows, w, width)
@@ -1592,7 +1615,7 @@
     packed = grads(basis, gconv, gup, gdn, dates * lats, lines, held)
     summed, grad = scatter(
         packed.reshape(dates, lats, held, LANES), lines,
-        x, gconv_rows, own, from_below, from_above, to_below, to_above, small[0], second_sums, width,
+        x, gconv_rows, own, from_below, from_above, to_below, to_above, small, second_sums, width,
     )
 
     def by_pixel(values):

time: 337 us -> 330 us (0.979)
  Pallas kernels: 289 us -> 282 us
    pallas_call x3 -> x2, Pallas kernels: 103 us -> 99.3 us  [the longest x1 72.7 us: block(): pl.pallas_call(block_kernel, in_specs=[anywhere] * 3 + [held] * 7, out_sp...]
    unnamed x26 -> x24, local copies, waits for them, and re-layouts: 14.6 us -> 17.9 us
  transfers between devices with their start and end apart: 4 -> 4, of which waited for: 0 -> 0; matrix products, arithmetic and copies ran while one was open for 4% -> 4% of each run, Pallas kernels for 21% -> 17%
where the time goes in v8:
time: 330 us; the launch traced here: 325 us
  Pallas kernels  282 us (85%)
  local copies, waits for them, and re-layouts  26.2 us (8%)
  starting transfers between devices  14.7 us (4%)
    pallas_call x1, Pallas kernels, block(): pl.pallas_call(block_kernel, in_specs=[anywhere] * 3 + [held] * 7, out_sp...  72.7 us
    pallas_call x1, Pallas kernels, scatter(): pl.pallas_call(functools.partial(scatter_kernel, dates, lats, lines, widt...  51.4 us
    pallas_call x1, Pallas kernels, gather(): pl.pallas_call(functools.partial(gather_kernel, dates, lats, lines, width...  44.7 us
    pallas_call x1, Pallas kernels, grads(): pl.pallas_call(functools.partial(grads_kernel, nrow), in_specs=[anywhere]...  33 us
    pallas_call x1, Pallas kernels, lower(): pl.pallas_call(functools.partial(lower_kernel, rows, width), in_specs=[sm...  32.3 us
    pallas_call x1, Pallas kernels, lift(): pl.pallas_call(functools.partial(lift_kernel, rows, lat, width), in_specs...  26.6 us
    pallas_call x1, Pallas kernels, unpack(): pl.pallas_call(functools.partial(unpack_kernel, nrow, gathered.shape[1]),...  21 us
    unnamed x24, local copies, waits for them, and re-layouts  17.9 us
  transfers between devices with their start and end apart: 4, of which 0 were waited for; matrix products, arithmetic and copies ran while one was open for 4% of the time, Pallas kernels for 17%

profile of v8, /device:TPU:4, one launch (start us, length us, event | category | flops | bytes accessed | tf_op | source)
XLA Modules:
  0.0 325.5 jit_solution(13045515444474030049)
XLA Ops:
  0.6 0.0 copy-start.6
  0.6 2.6 copy.22
  3.3 0.0 copy-done.6
  3.3 0.9 fusion.5.x
  4.2 0.0 copy-start
  4.2 0.0 copy-start.5
  4.2 0.0 copy-start.8
  4.3 0.0 copy-start.7
  4.3 1.4 slice_bitcast_fusion.1
  5.7 0.0 copy-done.5
  5.7 1.2 pad.16.src
  6.9 0.0 copy-done
  6.9 44.7 %gather_params.1 = (bf16[8,4,816,128]{3,2,1,0:T(8,128)(2,1)}, bf16[2,2,5,656,768]{4,3,2,1,0:T(8,128)(2,1)}, f32[4,656,128]{2,1,0:T(8,128)}, bf16[2,656,768]{2,1,0:T(8,128)(2,1)}) custom-call(bf16[816,128]{1,0:T(8,128)(2,1)} %pad.16.src, bf16[2,2,656,768]{3,2,1,0:T(8,128)(2,1)} %copy-done), custom_call_target="tpu_custom_call" | custom-call | tf_op jit(solution)/shard_map/gather_params/pallas_call | solution.py:1304
  51.6 5.9 %collective-permute-start = (bf16[1,656,768]{2,1,0:T(8,128)(2,1)}, bf16[1,656,768]{2,1,0:T(8,128)(2,1)S(1)}, u32[]{:S(2)}, u32[]{:S(2)}) collective-permute-start(bf16[1,656,768]{2,1,0:T(8,128)(2,1)} %get-tuple-element.30), channel_id=1, source_target_pairs={{0,1},{1,2},{2,3},{4,5},{5,6},{6,7},{8,9},{9,10},{10,11},{12,13},{... | collective-permute-start | bytes 3022856 | tf_op jit(solution)/shard_map/ppermute | solution.py:1602
  57.5 1.5 collective-permute-start.1
  59.7 0.0 copy-done.8
  59.7 0.7 copy.13.offsets
  60.4 0.0 copy-done.7
  60.4 0.1 multiply_convert_fusion
  60.5 0.6 reshape.76.mask
  61.1 2.6 copy.19
  63.7 2.4 pad.18.clone
  66.1 21.0 %unpack.1 = (bf16[2624,768]{1,0:T(8,128)(2,1)}, bf16[656,2624]{1,0:T(8,128)(2,1)}, bf16[656,1408]{1,0:T(8,128)(2,1)}, bf16[1296,656]{1,0:T(8,128)(2,1)}, bf16[12...) custom-call(bf16[32,816,128]{2,1,0:T(8,128)(2,1)} %bitcast.44), custom_call_target="tpu_custom_call" | custom-call | tf_op jit(solution)/shard_map/unpack/pallas_call | solution.py:133
  87.1 0.0 collective-permute-done.refs_1_
  87.1 0.0 copy-start.2
  87.2 0.0 collective-permute-done.1.refs_2_
  87.2 0.0 copy-start.3
  87.2 0.9 copy-done.2
  88.1 0.3 copy-done.3
  88.4 26.6 %lift.1 = bf16[2,2,2624,768]{3,2,1,0:T(8,128)(2,1)} custom-call(s32[12,2]{1,0:T(8,128)} %copy.13.offsets, s32[12]{0:T(128)} %bases.3, f32[8,12]{1,0:T(8,128)} %psi.3, bf16[2,2,5,656,768]{4,3,2,1,0:T(8,128)(2,1)} %get-tuple-element.27.own, f32[4,656,128]{2,1,0:T(8,128)} %get-tuple-element.28.small, bf16[2,656,768]{2,1,0:T(8,128)(2,1)} %get-tuple-element.29.refs_0_, ...), custom_call_target="tpu_custom_call" | custom-call | flops 41943040 | bytes 41943040 | tf_op jit(solution)/shard_map/lift/pallas_call | solution.py:520
  115.0 72.7 %block.1 = (bf16[4,656,768]{2,1,0:T(8,128)(2,1)}, bf16[4,656,768]{2,1,0:T(8,128)(2,1)}, f32[656,1408]{1,0:T(8,128)}, f32[1296,768]{1,0:T(8,128)}, f32[2,656,128]{2,1,0:T(8,128)}) custom-call(bf16[4,2624,768]{2,1,0:T(8,128)(2,1)} %bitcast.36, bf16[4,656,768]{2,1,0:T(8,128)(2,1)} %bitcast.38, bf16[4,656,768]{2,1,0:T(8,128)(2,1)} %bitcast.42, ...), custom_call_target="tpu_custom_call" | custom-call | tf_op jit(solution)/shard_map/block/pallas_call | solution.py:803
  187.7 0.0 copy-start.1
  187.7 32.3 %lower.1 = (f32[2,2,656,768]{3,2,1,0:T(8,128)}, bf16[1,656,768]{2,1,0:T(8,128)(2,1)}, bf16[1,656,768]{2,1,0:T(8,128)(2,1)}, bf16[1,656,768]{2,1,0:T(8,128)(2,1)}, bf16[1,656,768]{2,1,0:T(8,128)(2,1)}) custom-call(s32[12,2]{1,0:T(8,128)} %copy.13.offsets, s32[12]{0:T(128)} %bases.3, f32[8,12]{1,0:T(8,128)} %psi.3, bf16[2,2,656,768]{3,2,1,0:T(8,128)(2,1)} %bitcast.39, ...), custom_call_target="tpu_custom_call" | custom-call | tf_op jit(solution)/shard_map/lower/pallas_call | solution.py:965
  220.0 5.9 %collective-permute-start.2 = (bf16[1,656,768]{2,1,0:T(8,128)(2,1)}, bf16[1,656,768]{2,1,0:T(8,128)(2,1)}, u32[]{:S(2)}, u32[]{:S(2)}) collective-permute-start(bf16[1,656,768]{2,1,0:T(8,128)(2,1)} %get-tuple-element.44), channel_id=1, source_target_pairs={{0,1},{1,2},{2,3},{4,5},{5,6},{6,7},{8,9},{9,10},{10,11},{12,13},{... | collective-permute-start | bytes 3022856 | tf_op jit(solution)/shard_map/ppermute | solution.py:1613
  225.9 1.3 collective-permute-start.3
  227.2 0.0 copy-done.1
  227.2 0.3 slice.18
  227.5 5.0 %copy.23 = bf16[2,2,641,720]{3,1,2,0:T(2,128)(2,1)} copy(bf16[2,2,641,720]{3,2,1,0:T(8,128)(2,1)S(1)} %slice.18) | data formatting | bytes 7384320
  232.5 33.0 %grads.1 = bf16[32,816,128]{2,1,0:T(8,128)(2,1)} custom-call(bf16[4,2624,768]{2,1,0:T(8,128)(2,1)} %bitcast.37, bf16[4,656,768]{2,1,0:T(8,128)(2,1)} %get-tuple-element.39.gconv, f32[656,1408]{1,0:T(8,128)} %get-tuple-element.40.gup, f32[1296,768]{1,0:T(8,128)} %get-tuple-element.41.gdn), custom_call_target="tpu_custom_call" | custom-call | tf_op jit(solution)/shard_map/grads/pallas_call | solution.py:324
  265.5 0.0 collective-permute-done.2.lo
  265.5 0.0 collective-permute-done.3.hi
  265.5 51.4 %scatter_grads.1 = (f32[809,128]{1,0:T(8,128)}, bf16[2,2,656,768]{3,2,1,0:T(8,128)(2,1)}) custom-call(bf16[8,4,816,128]{3,2,1,0:T(8,128)(2,1)} %bitcast.41, bf16[2,2,656,768]{3,2,1,0:T(8,128)(2,1)} %copy-done, bf16[2,2,656,768]{3,2,1,0:T(8,128)(2,1)} %bitcast.40, f32[2,2,656,768]{3,2,1,0:T(8,128)} %get-tuple-element.43.own, ...), custom_call_target="tpu_custom_call" | custom-call | tf_op jit(solution)/shard_map/scatter_grads/pallas_call | solution.py:1540
  316.9 2.4 slice_bitcast_fusion
  319.3 0.0 copy-start.4
  319.3 5.0 %copy.17 = bf16[1,2,2,720,641]{3,2,4,1,0:T(2,128)(2,1)} copy(bf16[1,2,2,720,641]{3,4,2,1,0:T(8,128)(2,1)S(1)} %slice_bitcast_fusion) | data formatting | bytes 7384320
  324.3 0.0 copy-done.4
  324.3 0.8 copy.26
  (2 shorter events, 0.0 us)
Async XLA Ops:
  0.6 2.7 copy-start.6
  4.2 2.6 copy-start
  4.2 1.5 copy-start.5
  4.2 55.4 %copy-start.8 = (s32[12,2]{0,1:T(2,128)S(1)}, s32[12,2]{0,1:T(2,128)}, u32[]{:S(2)}) copy-start(s32[12,2]{0,1:T(2,128)} %param.16) | copy-start | bytes 292
  4.3 56.1 %copy-start.7 = (s32[2,720]{1,0:T(2,128)S(1)}, s32[2,720]{1,0:T(2,128)}, u32[]{:S(2)}) copy-start(s32[2,720]{1,0:T(2,128)} %param.15) | copy-start | bytes 17284
  51.6 35.6 %collective-permute-start = (bf16[1,656,768]{2,1,0:T(8,128)(2,1)}, bf16[1,656,768]{2,1,0:T(8,128)(2,1)S(1)}, u32[]{:S(2)}, u32[]{:S(2)}) collective-permute-start(bf16[1,656,768]{2,1,0:T(8,128)(2,1)} %get-tuple-element.30), channel_id=1, source_target_pairs={{0,1},{1,2},{2,3},{4,5},{5,6},{6,7},{8,9},{9,10},{10,11},{12,13},{... | collective-permute-start | bytes 3022856 | tf_op jit(solution)/shard_map/ppermute | solution.py:1602
  57.5 29.7 %collective-permute-start.1 = (bf16[1,656,768]{2,1,0:T(8,128)(2,1)}, bf16[1,656,768]{2,1,0:T(8,128)(2,1)S(1)}, u32[]{:S(2)}, u32[]{:S(2)}) collective-permute-start(bf16[1,656,768]{2,1,0:T(8,128)(2,1)} %get-tuple-element.31), channel_id=1, source_target_pairs={{1,0},{2,1},{3,2},{5,4},{6,5},{7,6},{9,8},{10,9},{11,10},{13,12},{... | collective-permute-start | bytes 3022856 | tf_op jit(solution)/shard_map/ppermute | solution.py:1602
  87.1 1.0 copy-start.2
  87.2 1.3 copy-start.3
  187.7 39.5 %copy-start.1 = (bf16[4,656,768]{2,1,0:T(8,128)(2,1)S(1)}, bf16[4,656,768]{2,1,0:T(8,128)(2,1)}, u32[]{:S(2)}) copy-start(bf16[4,656,768]{2,1,0:T(8,128)(2,1)} %get-tuple-element.38) | copy-start | bytes 12091396
  220.0 45.5 %collective-permute-start.2 = (bf16[1,656,768]{2,1,0:T(8,128)(2,1)}, bf16[1,656,768]{2,1,0:T(8,128)(2,1)}, u32[]{:S(2)}, u32[]{:S(2)}) collective-permute-start(bf16[1,656,768]{2,1,0:T(8,128)(2,1)} %get-tuple-element.44), channel_id=1, source_target_pairs={{0,1},{1,2},{2,3},{4,5},{5,6},{6,7},{8,9},{9,10},{10,11},{12,13},{... | collective-permute-start | bytes 3022856 | tf_op jit(solution)/shard_map/ppermute | solution.py:1613
  225.9 39.6 %collective-permute-start.3 = (bf16[1,656,768]{2,1,0:T(8,128)(2,1)}, bf16[1,656,768]{2,1,0:T(8,128)(2,1)}, u32[]{:S(2)}, u32[]{:S(2)}) collective-permute-start(bf16[1,656,768]{2,1,0:T(8,128)(2,1)} %get-tuple-element.45), channel_id=1, source_target_pairs={{1,0},{2,1},{3,2},{5,4},{6,5},{7,6},{9,8},{10,9},{11,10},{13,12},{... | collective-permute-start | bytes 3022856 | tf_op jit(solution)/shard_map/ppermute | solution.py:1614
  319.3 5.0 %copy-start.4 = (f32[809,128]{1,0:T(8,128)S(1)}, f32[809,128]{1,0:T(8,128)}, u32[]{:S(2)}) copy-start(f32[809,128]{1,0:T(8,128)} %get-tuple-element.50) | copy-start | bytes 1242628

commit v9 on v8

--- a/solution.py
+++ b/solution.py
@@ -87,7 +87,7 @@
                     if j==J-1: val=jnp.where(lane<last,val,0.0)
                     chunks[pl.ds(j*height+8*g*pitch+b,8,stride=pitch),:]=val
             return 0
-        lax.fori_loop(0,period,body,0,unroll=8)
+        lax.fori_loop(0,period,body,0,unroll=16)
         def border(a,_):
             for j in range(J): chunks[pl.ds(j*height+a*pitch-8,8),:]=chunks[pl.ds(j*height+a*pitch,8),:]
             return 0
@@ -293,11 +293,11 @@
             copy(m)
             return 0
 
-        lax.fori_loop(0, rows // 8, body, 0, unroll=4)
+        lax.fori_loop(0, rows // 8, body, 0, unroll=8)
         copy(rows // 8)
     chunk_clear(chunks, 6, height, 2600, 128)
     step, first, _ = line_merge(flat, 0, chunks, 0, C, 128, 3)
-    lax.fori_loop(0, 128, step, first(), unroll=8)
+    lax.fori_loop(0, 128, step, first(), unroll=16)
     seam = OFF_UP // LANES
     for shard in range(shards):
         if nrow * shard < seam < nrow * shard + pad:
@@ -335,10 +335,10 @@
             pltpu.VMEM((6 * (136 * 24 + 8), LANES), F32),
             pltpu.VMEM(gup.shape, F32),
             pltpu.VMEM(gdn.shape, F32),
-            pltpu.VMEM((4, pad, LANES), BF16),
+            pltpu.VMEM((8, pad, LANES), BF16),
             pltpu.SemaphoreType.DMA((2, 2)),
             pltpu.SemaphoreType.DMA((2,)),
-            pltpu.SemaphoreType.DMA((4,)),
+            pltpu.SemaphoreType.DMA((8,)),
         ],
         compiler_params=pltpu.CompilerParams(vmem_limit_bytes=VMEM),
         name="grads",
@@ -824,8 +824,7 @@
     ref[at, :] = ref[at, :] + total
 
 
-GROUP = 11 * STEP
-GROUP_STEP = 10 * STEP
+GROUP = 7 * STEP
 
 
 def lower_kernel(rows, width, offsets, bases, psi, gconv, w, own, lo0, hi0, lo1, hi1, *scratch):
@@ -834,7 +833,7 @@
     sets = [scratch[:per_slab], scratch[per_slab : 2 * per_slab]]
     first_row = lax.axis_index("lat") * rows
     span = 2 * REACH + 1
-    groups = 1 + (CP - GROUP) // GROUP_STEP
+    groups = -(-CP // GROUP)
     for n in range(3 * span):
         place[n] = 0
         for r in range(rows):
@@ -846,7 +845,7 @@
             coef[r, n] = psi[first_row + r, p]
 
     def channels(g):
-        return pl.ds(pl.multiple_of(g * GROUP_STEP, STEP), GROUP)
+        return pl.ds(pl.multiple_of(jnp.minimum(g * GROUP, CP - GROUP), STEP), GROUP)
 
     def weights(j, g):
         return pltpu.make_async_copy(w.at[:, channels(g), :], sets[j][1], w_sems.at[j])

time: 330 us -> 326 us (0.988)
  Pallas kernels: 282 us -> 277 us
  transfers between devices with their start and end apart: 4 -> 4, of which waited for: 0 -> 0; matrix products, arithmetic and copies ran while one was open for 4% -> 4% of each run, Pallas kernels for 17% -> 16%
where the time goes in v9:
time: 326 us; the launch traced here: 321 us
  Pallas kernels  277 us (85%)
  local copies, waits for them, and re-layouts  26.2 us (8%)
  starting transfers between devices  14.6 us (4%)
    pallas_call x1, Pallas kernels, block(): pl.pallas_call(block_kernel, in_specs=[anywhere] * 3 + [held] * 7, out_sp...  72.7 us
    pallas_call x1, Pallas kernels, scatter(): pl.pallas_call(functools.partial(scatter_kernel, dates, lats, lines, widt...  51.4 us
    pallas_call x1, Pallas kernels, gather(): pl.pallas_call(functools.partial(gather_kernel, dates, lats, lines, width...  44.7 us
    pallas_call x1, Pallas kernels, lower(): pl.pallas_call(functools.partial(lower_kernel, rows, width), in_specs=[sm...  31.9 us
    pallas_call x1, Pallas kernels, grads(): pl.pallas_call(functools.partial(grads_kernel, nrow), in_specs=[anywhere]...  30.4 us
    pallas_call x1, Pallas kernels, lift(): pl.pallas_call(functools.partial(lift_kernel, rows, lat, width), in_specs...  26.6 us
    pallas_call x1, Pallas kernels, unpack(): pl.pallas_call(functools.partial(unpack_kernel, nrow, gathered.shape[1]),...  19.8 us
    unnamed x24, local copies, waits for them, and re-layouts  17.9 us
  transfers between devices with their start and end apart: 4, of which 0 were waited for; matrix products, arithmetic and copies ran while one was open for 4% of the time, Pallas kernels for 16%

profile of v9, /device:TPU:4, one launch (start us, length us, event | category | flops | bytes accessed | tf_op | source)
XLA Modules:
  0.0 321.0 jit_solution(4978439254389981058)
XLA Ops:
  0.6 0.0 copy-start.6
  0.6 2.6 copy.22
  3.3 0.0 copy-done.6
  3.3 0.9 fusion.5.x
  4.2 0.0 copy-start
  4.2 0.0 copy-start.5
  4.2 0.0 copy-start.8
  4.3 0.0 copy-start.7
  4.3 1.4 slice_bitcast_fusion.1
  5.7 0.0 copy-done.5
  5.7 1.2 pad.16.src
  6.9 0.0 copy-done
  6.9 44.7 %gather_params.1 = (bf16[8,4,816,128]{3,2,1,0:T(8,128)(2,1)}, bf16[2,2,5,656,768]{4,3,2,1,0:T(8,128)(2,1)}, f32[4,656,128]{2,1,0:T(8,128)}, bf16[2,656,768]{2,1,0:T(8,128)(2,1)}) custom-call(bf16[816,128]{1,0:T(8,128)(2,1)} %pad.16.src, bf16[2,2,656,768]{3,2,1,0:T(8,128)(2,1)} %copy-done), custom_call_target="tpu_custom_call" | custom-call | tf_op jit(solution)/shard_map/gather_params/pallas_call | solution.py:1303
  51.6 5.9 %collective-permute-start = (bf16[1,656,768]{2,1,0:T(8,128)(2,1)}, bf16[1,656,768]{2,1,0:T(8,128)(2,1)S(1)}, u32[]{:S(2)}, u32[]{:S(2)}) collective-permute-start(bf16[1,656,768]{2,1,0:T(8,128)(2,1)} %get-tuple-element.30), channel_id=1, source_target_pairs={{0,1},{1,2},{2,3},{4,5},{5,6},{6,7},{8,9},{9,10},{10,11},{12,13},{... | collective-permute-start | bytes 3022856 | tf_op jit(solution)/shard_map/ppermute | solution.py:1601
  57.5 1.5 collective-permute-start.1
  59.6 0.0 copy-done.8
  59.6 0.7 copy.13.offsets
  60.3 0.0 copy-done.7
  60.3 0.1 multiply_convert_fusion
  60.4 0.6 reshape.76.mask
  61.0 2.6 copy.19
  63.7 2.4 pad.18.clone
  66.1 19.8 %unpack.1 = (bf16[2624,768]{1,0:T(8,128)(2,1)}, bf16[656,2624]{1,0:T(8,128)(2,1)}, bf16[656,1408]{1,0:T(8,128)(2,1)}, bf16[1296,656]{1,0:T(8,128)(2,1)}, bf16[12...) custom-call(bf16[32,816,128]{2,1,0:T(8,128)(2,1)} %bitcast.44), custom_call_target="tpu_custom_call" | custom-call | tf_op jit(solution)/shard_map/unpack/pallas_call | solution.py:133
  85.9 0.0 collective-permute-done.refs_1_
  85.9 0.0 copy-start.2
  85.9 0.0 collective-permute-done.1.refs_2_
  85.9 0.0 copy-start.3
  85.9 0.9 copy-done.2
  86.9 0.3 copy-done.3
  87.2 26.6 %lift.1 = bf16[2,2,2624,768]{3,2,1,0:T(8,128)(2,1)} custom-call(s32[12,2]{1,0:T(8,128)} %copy.13.offsets, s32[12]{0:T(128)} %bases.3, f32[8,12]{1,0:T(8,128)} %psi.3, bf16[2,2,5,656,768]{4,3,2,1,0:T(8,128)(2,1)} %get-tuple-element.27.own, f32[4,656,128]{2,1,0:T(8,128)} %get-tuple-element.28.small, bf16[2,656,768]{2,1,0:T(8,128)(2,1)} %get-tuple-element.29.refs_0_, ...), custom_call_target="tpu_custom_call" | custom-call | flops 41943040 | bytes 41943040 | tf_op jit(solution)/shard_map/lift/pallas_call | solution.py:520
  113.8 72.7 %block.1 = (bf16[4,656,768]{2,1,0:T(8,128)(2,1)}, bf16[4,656,768]{2,1,0:T(8,128)(2,1)}, f32[656,1408]{1,0:T(8,128)}, f32[1296,768]{1,0:T(8,128)}, f32[2,656,128]{2,1,0:T(8,128)}) custom-call(bf16[4,2624,768]{2,1,0:T(8,128)(2,1)} %bitcast.36, bf16[4,656,768]{2,1,0:T(8,128)(2,1)} %bitcast.38, bf16[4,656,768]{2,1,0:T(8,128)(2,1)} %bitcast.42, ...), custom_call_target="tpu_custom_call" | custom-call | tf_op jit(solution)/shard_map/block/pallas_call | solution.py:803
  186.4 0.0 copy-start.1
  186.5 31.9 %lower.1 = (f32[2,2,656,768]{3,2,1,0:T(8,128)}, bf16[1,656,768]{2,1,0:T(8,128)(2,1)}, bf16[1,656,768]{2,1,0:T(8,128)(2,1)}, bf16[1,656,768]{2,1,0:T(8,128)(2,1)}, bf16[1,656,768]{2,1,0:T(8,128)(2,1)}) custom-call(s32[12,2]{1,0:T(8,128)} %copy.13.offsets, s32[12]{0:T(128)} %bases.3, f32[8,12]{1,0:T(8,128)} %psi.3, bf16[2,2,656,768]{3,2,1,0:T(8,128)(2,1)} %bitcast.39, ...), custom_call_target="tpu_custom_call" | custom-call | tf_op jit(solution)/shard_map/lower/pallas_call | solution.py:964
  218.4 5.9 %collective-permute-start.2 = (bf16[1,656,768]{2,1,0:T(8,128)(2,1)}, bf16[1,656,768]{2,1,0:T(8,128)(2,1)}, u32[]{:S(2)}, u32[]{:S(2)}) collective-permute-start(bf16[1,656,768]{2,1,0:T(8,128)(2,1)} %get-tuple-element.44), channel_id=1, source_target_pairs={{0,1},{1,2},{2,3},{4,5},{5,6},{6,7},{8,9},{9,10},{10,11},{12,13},{... | collective-permute-start | bytes 3022856 | tf_op jit(solution)/shard_map/ppermute | solution.py:1612
  224.3 1.3 collective-permute-start.3
  225.6 0.0 copy-done.1
  225.6 0.3 slice.18
  225.9 5.0 %copy.23 = bf16[2,2,641,720]{3,1,2,0:T(2,128)(2,1)} copy(bf16[2,2,641,720]{3,2,1,0:T(8,128)(2,1)S(1)} %slice.18) | data formatting | bytes 7384320
  230.8 30.4 %grads.1 = bf16[32,816,128]{2,1,0:T(8,128)(2,1)} custom-call(bf16[4,2624,768]{2,1,0:T(8,128)(2,1)} %bitcast.37, bf16[4,656,768]{2,1,0:T(8,128)(2,1)} %get-tuple-element.39.gconv, f32[656,1408]{1,0:T(8,128)} %get-tuple-element.40.gup, f32[1296,768]{1,0:T(8,128)} %get-tuple-element.41.gdn), custom_call_target="tpu_custom_call" | custom-call | tf_op jit(solution)/shard_map/grads/pallas_call | solution.py:324
  261.3 0.0 collective-permute-done.2.lo
  261.3 0.0 collective-permute-done.3.hi
  261.3 51.4 %scatter_grads.1 = (f32[809,128]{1,0:T(8,128)}, bf16[2,2,656,768]{3,2,1,0:T(8,128)(2,1)}) custom-call(bf16[8,4,816,128]{3,2,1,0:T(8,128)(2,1)} %bitcast.41, bf16[2,2,656,768]{3,2,1,0:T(8,128)(2,1)} %copy-done, bf16[2,2,656,768]{3,2,1,0:T(8,128)(2,1)} %bitcast.40, f32[2,2,656,768]{3,2,1,0:T(8,128)} %get-tuple-element.43.own, ...), custom_call_target="tpu_custom_call" | custom-call | tf_op jit(solution)/shard_map/scatter_grads/pallas_call | solution.py:1539
  312.7 2.4 slice_bitcast_fusion
  315.1 0.0 copy-start.4
  315.1 5.0 %copy.17 = bf16[1,2,2,720,641]{3,2,4,1,0:T(2,128)(2,1)} copy(bf16[1,2,2,720,641]{3,4,2,1,0:T(8,128)(2,1)S(1)} %slice_bitcast_fusion) | data formatting | bytes 7384320
  320.0 0.0 copy-done.4
  320.0 0.8 copy.26
  (2 shorter events, 0.0 us)
Async XLA Ops:
  0.6 2.7 copy-start.6
  4.2 2.6 copy-start
  4.2 1.5 copy-start.5
  4.2 55.4 %copy-start.8 = (s32[12,2]{0,1:T(2,128)S(1)}, s32[12,2]{0,1:T(2,128)}, u32[]{:S(2)}) copy-start(s32[12,2]{0,1:T(2,128)} %param.16) | copy-start | bytes 292
  4.3 56.1 %copy-start.7 = (s32[2,720]{1,0:T(2,128)S(1)}, s32[2,720]{1,0:T(2,128)}, u32[]{:S(2)}) copy-start(s32[2,720]{1,0:T(2,128)} %param.15) | copy-start | bytes 17284
  51.6 34.3 %collective-permute-start = (bf16[1,656,768]{2,1,0:T(8,128)(2,1)}, bf16[1,656,768]{2,1,0:T(8,128)(2,1)S(1)}, u32[]{:S(2)}, u32[]{:S(2)}) collective-permute-start(bf16[1,656,768]{2,1,0:T(8,128)(2,1)} %get-tuple-element.30), channel_id=1, source_target_pairs={{0,1},{1,2},{2,3},{4,5},{5,6},{6,7},{8,9},{9,10},{10,11},{12,13},{... | collective-permute-start | bytes 3022856 | tf_op jit(solution)/shard_map/ppermute | solution.py:1601
  57.5 28.4 %collective-permute-start.1 = (bf16[1,656,768]{2,1,0:T(8,128)(2,1)}, bf16[1,656,768]{2,1,0:T(8,128)(2,1)S(1)}, u32[]{:S(2)}, u32[]{:S(2)}) collective-permute-start(bf16[1,656,768]{2,1,0:T(8,128)(2,1)} %get-tuple-element.31), channel_id=1, source_target_pairs={{1,0},{2,1},{3,2},{5,4},{6,5},{7,6},{9,8},{10,9},{11,10},{13,12},{... | collective-permute-start | bytes 3022856 | tf_op jit(solution)/shard_map/ppermute | solution.py:1601
  85.9 1.0 copy-start.2
  85.9 1.3 copy-start.3
  186.4 39.1 %copy-start.1 = (bf16[4,656,768]{2,1,0:T(8,128)(2,1)S(1)}, bf16[4,656,768]{2,1,0:T(8,128)(2,1)}, u32[]{:S(2)}) copy-start(bf16[4,656,768]{2,1,0:T(8,128)(2,1)} %get-tuple-element.38) | copy-start | bytes 12091396
  218.4 42.9 %collective-permute-start.2 = (bf16[1,656,768]{2,1,0:T(8,128)(2,1)}, bf16[1,656,768]{2,1,0:T(8,128)(2,1)}, u32[]{:S(2)}, u32[]{:S(2)}) collective-permute-start(bf16[1,656,768]{2,1,0:T(8,128)(2,1)} %get-tuple-element.44), channel_id=1, source_target_pairs={{0,1},{1,2},{2,3},{4,5},{5,6},{6,7},{8,9},{9,10},{10,11},{12,13},{... | collective-permute-start | bytes 3022856 | tf_op jit(solution)/shard_map/ppermute | solution.py:1612
  224.3 37.0 %collective-permute-start.3 = (bf16[1,656,768]{2,1,0:T(8,128)(2,1)}, bf16[1,656,768]{2,1,0:T(8,128)(2,1)}, u32[]{:S(2)}, u32[]{:S(2)}) collective-permute-start(bf16[1,656,768]{2,1,0:T(8,128)(2,1)} %get-tuple-element.45), channel_id=1, source_target_pairs={{1,0},{2,1},{3,2},{5,4},{6,5},{7,6},{9,8},{10,9},{11,10},{13,12},{... | collective-permute-start | bytes 3022856 | tf_op jit(solution)/shard_map/ppermute | solution.py:1613
  315.1 5.0 %copy-start.4 = (f32[809,128]{1,0:T(8,128)S(1)}, f32[809,128]{1,0:T(8,128)}, u32[]{:S(2)}) copy-start(f32[809,128]{1,0:T(8,128)} %get-tuple-element.50) | copy-start | bytes 1242628
